TPU v7x, 32 devices: a whole 2x2x4 slice. The times are simulated.
32 devices in a mesh: rows: 8 (over y, x, core), units: 4 (over z).
Axes of the slice: x: 2, y: 2, z: 4, core: 2. Of those that a mesh axis runs over, the one named last changes fastest.
Arguments:
- token_ids: int32 [512, 32], P('rows'), may hold values from 0 to 274
- targets: int32 [512, 32], P('rows'), may hold values from 0 to 274
- lengths: int32 [512], P('rows'), may hold values from 1 to 32, as said below
- init_hidden: float32 [512, 2048], P('rows', 'units'), may hold values from -0.9 to 0.9
- init_cell: float32 [512, 2048], P('rows', 'units'), may hold values from -4 to 4
- embedding: bfloat16 [275, 100], replicated, may hold values from -5 to 5
- input_weight: bfloat16 [100, 4, 2048], P(None, None, 'units'), may hold values from -0.625 to 0.625
- recurrent_weight: bfloat16 [2048, 4, 2048], P('rows', None, 'units'), may hold values from -0.17675781 to 0.17675781
- gate_bias: float32 [4, 2048], P(None, 'units'), may hold values from -1 to 1
- decoder_weight: bfloat16 [2048, 275], P('units'), may hold values from -0.8984375 to 0.8984375
- decoder_bias: float32 [275], replicated, may hold values from -4 to 4
Outputs:
- total_loss: float32 [], replicated
- hidden_out: float32 [512, 32, 2048], P('rows', None, 'units')
- final_hidden: float32 [512, 2048], P('rows', 'units')
- final_cell: float32 [512, 2048], P('rows', 'units')
- grad_embedding: float32 [275, 100], replicated
- grad_input_weight: float32 [100, 4, 2048], P(None, None, 'units')
- grad_recurrent_weight: float32 [2048, 4, 2048], P('rows', None, 'units')
- grad_gate_bias: float32 [4, 2048], P(None, 'units')
- grad_decoder_weight: float32 [2048, 275], P('units')
- grad_decoder_bias: float32 [275], replicated
- grad_init_hidden: float32 [512, 2048], P('rows', 'units')
- grad_init_cell: float32 [512, 2048], P('rows', 'units')
Inputs may be any that keep to these rules, and one draw needn't show every extreme that they name: Each sequence's valid positions are its first lengths ones; each aligned block of 64 sequences holds one of length 32.
All inputs are finite; a program needn't handle non-finite values.
Results may differ from a plain program's by a relative error of at most 0.012.
Values may be sent and summed in bfloat16 or wider, within the bound.
No kernel may reach another device: no remote copies, remote signals or barrier semaphores. Data moves between devices by JAX's collectives and lax.ppermute only.
A program may use at most 128 MiB of HBM per device.

v0:
```python
import jax
import jax.numpy as jnp
from jax import lax
from jax.sharding import PartitionSpec as P


def contract(left, right, left_dim, right_dim):
    return lax.dot_general(
        left, right, (((left_dim,), (right_dim,)), ((), ())), preferred_element_type=jnp.float32
    )


def gate_values(preact, sequences, unit_width):
    shaped = preact.reshape(sequences, 4, unit_width)
    gate_in = jax.nn.sigmoid(shaped[:, 0])
    gate_forget = jax.nn.sigmoid(shaped[:, 1])
    gate_cell = jnp.tanh(shaped[:, 2])
    gate_out = jax.nn.sigmoid(shaped[:, 3])
    return (gate_in, gate_forget, gate_cell, gate_out)


def cross_entropy(logits, target_ids, alive, vocab_index, loss_scale):
    maximum = jnp.max(logits, axis=1, keepdims=True)
    log_total = jnp.log(jnp.sum(jnp.exp(logits - maximum), axis=1, keepdims=True)) + maximum
    probable = jnp.exp(logits - log_total)
    target_hot = (target_ids[:, None] == vocab_index[None, :]).astype(jnp.float32)
    picked = jnp.sum(logits * target_hot, axis=1)
    loss_part = jnp.sum((log_total[:, 0] - picked) * alive) * loss_scale
    dlogits = ((probable - target_hot) * (alive * loss_scale)[:, None]).astype(jnp.bfloat16)
    return (loss_part, dlogits)


def on_device(
    token_ids,
    targets,
    lengths,
    init_hidden,
    init_cell,
    embedding,
    input_weight,
    recurrent_weight,
    gate_bias,
    decoder_weight,
    decoder_bias,
):
    sequences, window = token_ids.shape
    unit_width = recurrent_weight.shape[2]
    rows_dev = recurrent_weight.shape[0]
    hidden_width = rows_dev * lax.axis_size("rows")
    vocab_size, embed_width = embedding.shape
    unit_count = lax.axis_size("units")
    unit_id = lax.axis_index("units")
    positions = sequences * window
    loss_scale = 1.0 / window
    weight_full = lax.all_gather(recurrent_weight, "rows", axis=0, tiled=True).reshape(
        hidden_width, 4 * unit_width
    )
    input_flat = input_weight.reshape(embed_width, 4 * unit_width)
    bias_flat = gate_bias.reshape(4 * unit_width)
    vocab_index = jnp.arange(vocab_size)
    ids_time = token_ids.T.reshape(positions)
    onehot = (ids_time[:, None] == vocab_index[None, :]).astype(jnp.bfloat16)
    embedded = jnp.dot(onehot, embedding, preferred_element_type=jnp.float32).astype(jnp.bfloat16)
    drive = jnp.dot(embedded, input_flat, preferred_element_type=jnp.float32).reshape(
        window, sequences, 4 * unit_width
    )
    active = (jnp.arange(window)[:, None] < lengths[None, :]).astype(jnp.float32)

    def advance(state_pair, inputs):
        hidden_prev, cell_prev = state_pair
        drive_now, alive = inputs
        gathered = lax.all_gather(hidden_prev.astype(jnp.bfloat16), "units", axis=1, tiled=True)
        preact = (
            drive_now
            + jnp.dot(gathered, weight_full, preferred_element_type=jnp.float32)
            + bias_flat
        )
        gate_in, gate_forget, gate_cell, gate_out = gate_values(preact, sequences, unit_width)
        cell_new = gate_forget * cell_prev + gate_in * gate_cell
        hidden_new = gate_out * jnp.tanh(cell_new)
        alive = alive[:, None]
        hidden_next = alive * hidden_new + (1.0 - alive) * hidden_prev
        cell_next = alive * cell_new + (1.0 - alive) * cell_prev
        return ((hidden_next, cell_next), (hidden_next, preact, gathered, cell_prev))

    (hidden_last, cell_last), (hidden_seq, preacts, gathered_seq, cells_prev) = lax.scan(
        advance, (init_hidden, init_cell), (drive, active)
    )
    hidden_low = hidden_seq.astype(jnp.bfloat16).reshape(positions, unit_width)
    target_time = targets.T.reshape(positions)
    active_flat = active.reshape(positions)
    quarter = positions // unit_count
    decoder_full = lax.all_gather(decoder_weight, "units", axis=0, tiled=True)
    quarter_rows = lax.all_to_all(hidden_low, "units", split_axis=0, concat_axis=1, tiled=True)
    logits = jnp.dot(quarter_rows, decoder_full, preferred_element_type=jnp.float32) + decoder_bias
    target_part = lax.dynamic_slice_in_dim(target_time, unit_id * quarter, quarter, 0)
    active_part = lax.dynamic_slice_in_dim(active_flat, unit_id * quarter, quarter, 0)
    loss_part, dlogits = cross_entropy(logits, target_part, active_part, vocab_index, loss_scale)
    back_grad = contract(dlogits, decoder_full, 1, 1).astype(jnp.bfloat16)
    decoder_grad = lax.all_to_all(back_grad, "units", split_axis=1, concat_axis=0, tiled=True)
    columns = quarter_rows
    decoder_part = lax.psum_scatter(
        contract(columns, dlogits, 0, 0), "units", scatter_dimension=0, tiled=True
    )
    bias_part = jnp.sum(dlogits.astype(jnp.float32), axis=0)
    decoder_steps = decoder_grad.astype(jnp.float32).reshape(window, sequences, unit_width)

    def retreat(grad_pair, inputs):
        grad_hidden, grad_cell = grad_pair
        preact, cell_prev, alive, decoder_now = inputs
        gate_in, gate_forget, gate_cell, gate_out = gate_values(preact, sequences, unit_width)
        cell_new = gate_forget * cell_prev + gate_in * gate_cell
        cell_tanh = jnp.tanh(cell_new)
        alive = alive[:, None]
        total = grad_hidden + decoder_now
        dhidden = alive * total
        dcell = alive * grad_cell + dhidden * gate_out * (1.0 - cell_tanh * cell_tanh)
        dpre = jnp.stack(
            [
                dcell * gate_cell * gate_in * (1.0 - gate_in),
                dcell * cell_prev * gate_forget * (1.0 - gate_forget),
                dcell * gate_in * (1.0 - gate_cell * gate_cell),
                dhidden * cell_tanh * gate_out * (1.0 - gate_out),
            ],
            axis=1,
        )
        dpre = dpre.reshape(sequences, 4 * unit_width).astype(jnp.bfloat16)
        recurrent_part = lax.psum_scatter(
            contract(weight_full, dpre, 1, 1), "units", scatter_dimension=0, tiled=True
        ).T
        hidden_prev_grad = (1.0 - alive) * total + recurrent_part
        cell_prev_grad = (1.0 - alive) * grad_cell + dcell * gate_forget
        return ((hidden_prev_grad, cell_prev_grad), dpre)

    (grad_hidden0, grad_cell0), dpres = lax.scan(
        retreat,
        (jnp.zeros_like(init_hidden), jnp.zeros_like(init_cell)),
        (preacts, cells_prev, active, decoder_steps),
        reverse=True,
    )
    dpre_flat = dpres.reshape(positions, 4 * unit_width)
    gathered_flat = gathered_seq.reshape(positions, hidden_width)
    columns = gathered_flat
    recurrent_grad = lax.psum_scatter(
        contract(columns, dpre_flat, 0, 0), "rows", scatter_dimension=0, tiled=True
    ).reshape(rows_dev, 4, unit_width)
    input_part = contract(embedded, dpre_flat, 0, 0)
    gate_part = jnp.sum(dpre_flat.astype(jnp.float32), axis=0)
    dembedded = contract(dpre_flat, input_flat, 1, 1)
    embed_part = lax.dot_general(
        onehot.astype(jnp.float32),
        dembedded,
        (((0,), (0,)), ((), ())),
        precision=lax.Precision.HIGHEST,
        preferred_element_type=jnp.float32,
    )
    input_grad, gate_grad, decoder_out = lax.psum((input_part, gate_part, decoder_part), "rows")
    embed_grad, decoder_bias_grad, total_loss = lax.psum(
        (embed_part, bias_part, loss_part), ("rows", "units")
    )
    return (
        total_loss,
        jnp.transpose(hidden_seq, (1, 0, 2)),
        hidden_last,
        cell_last,
        embed_grad,
        input_grad.reshape(embed_width, 4, unit_width),
        recurrent_grad,
        gate_grad.reshape(4, unit_width),
        decoder_out,
        decoder_bias_grad,
        grad_hidden0,
        grad_cell0,
    )


def solution(mesh):
    return jax.shard_map(
        on_device,
        mesh=mesh,
        in_specs=(
            P("rows", None),
            P("rows", None),
            P("rows"),
            P("rows", "units"),
            P("rows", "units"),
            P(),
            P(None, None, "units"),
            P("rows", None, "units"),
            P(None, "units"),
            P("units", None),
            P(),
        ),
        out_specs=(
            P(),
            P("rows", None, "units"),
            P("rows", "units"),
            P("rows", "units"),
            P(),
            P(None, None, "units"),
            P("rows", None, "units"),
            P(None, "units"),
            P("units", None),
            P(),
            P("rows", "units"),
            P("rows", "units"),
        ),
        check_vma=False,
    )
```

profile of v0, /device:TPU:0, one launch (start us, length us, event | category | flops | bytes accessed | tf_op | source)
XLA Modules:
  0.0 2216.9 jit_solution(5479906725853170630)
XLA Ops:
  20.3 47.6 %all-gather.3.cloned.1.call-done = bf16[2048,4,512]{2,1,0:T(4,128)(2,1)} async-done(((bf16[256,4,512]{2,1,0:T(4,128)(2,1)}), bf16[2048,4,512]{2,1,0:T(4,128)(2,1)}) %all-gather.3.cloned.1.call-update) | async-done | bytes 8388624 | tf_op jit(solution)/shard_map/all_gather | solution.py:55
  82.6 720.6 %while.39 = (s32[]{:T(128)}, f32[64,512]{1,0:T(8,128)S(1)}, f32[64,512]{1,0:T(8,128)S(1)}, f32[32,64,512]{2,1,0:T(8,128)}, f32[32,64,2048]{2,1,0:T(8,128)}, /*in...) while((s32[]{:T(128)}, f32[64,512]{1,0:T(8,128)S(1)}, ...), condition=%wide.region_1.2_spmd, body=%wide.region_0.1_spmd.sunk | while | flops 537788480 | bytes 15101305 | solution.py:86
  812.5 44.8 %all-to-all-done = bf16[4,512,512]{2,1,0:T(8,128)(2,1)} async-done(((bf16[4,512,512]{2,1,0:T(8,128)(2,1)}), bf16[4,512,512]{2,1,0:T(8,128)(2,1)}, u32[]{:S(2)}, u32[]{:S(2)}) %all-to-all-start) | async-done | bytes 2097184 | tf_op jit(solution)/shard_map/all_to_all | solution.py:94
  872.9 43.8 %all-to-all-done.1 = bf16[512,4,512]{2,0,1:T(8,128)(2,1)} async-done(((bf16[512,4,512]{2,0,1:T(8,128)(2,1)}), bf16[512,4,512]{2,0,1:T(8,128)(2,1)}, u32[]{:S(2)}, u32[]{:S(2)}) %all-to-all-start.1) | async-done | bytes 2097184 | tf_op jit(solution)/shard_map/all_to_all | solution.py:100
  925.1 1031.5 %while.40 = (s32[]{:T(128)}, f32[64,512]{1,0:T(8,128)S(1)}, f32[64,512]{1,0:T(8,128)S(1)}, bf16[32,64,2048]{2,1,0:T(8,128)(2,1)}, f32[32,64]{1,0:T(8,128)S(1)}, ...) while((s32[]{:T(128)}, f32[64,512]{1,0:T(8,128)S(1)}, ...), condition=%wide.region_9.10_spmd.clone, body=%wide.region_7.9_spmd.clone.sunk | while | flops 539525184 | bytes 20711368 | solution.py:135
  937.3 19.6 reduce-scatter.8.cloned.1.call-done
  1034.5 19.0 reduce-scatter.8.cloned.1.call-done
  1066.8 19.0 reduce-scatter.8.cloned.1.call-done
  1163.4 19.0 reduce-scatter.8.cloned.1.call-done
  1324.5 19.0 reduce-scatter.8.cloned.1.call-done
  1356.7 19.0 reduce-scatter.8.cloned.1.call-done
  1389.0 19.0 reduce-scatter.8.cloned.1.call-done
  1421.2 19.0 reduce-scatter.8.cloned.1.call-done
  1485.6 19.0 reduce-scatter.8.cloned.1.call-done
  1517.8 19.0 reduce-scatter.8.cloned.1.call-done
  1582.2 19.0 reduce-scatter.8.cloned.1.call-done
  1743.3 19.0 reduce-scatter.8.cloned.1.call-done
  1775.6 19.0 reduce-scatter.8.cloned.1.call-done
  1807.8 19.0 reduce-scatter.8.cloned.1.call-done
  1840.0 19.0 reduce-scatter.8.cloned.1.call-done
  1957.3 24.4 %convolution_bitcast_fusion.1 = f32[2048,2048]{1,0:T(8,128)} fusion(bf16[32,64,2048]{2,1,0:T(8,128)(2,1)} %get-tuple-element.261, bf16[32,64,2048]{2,1,0:T(8,128)(2,1)} %get-tuple-element.260), kind=kOutput, calls=%fused_computation.71 | convolution fusion | flops 17179869184 | bytes 33554432 | tf_op jit(solution)/shard_map/dot_general | solution.py:8
  2011.7 39.9 %all-reduce = (f32[]{:T(128)}, f32[275]{0:T(512)}) all-reduce(f32[]{:T(128)S(6)} %mul.299, f32[275]{0:T(512)S(1)} %get-tuple-element.351), channel_id=1, replica_groups=mesh['rows'=8,'units'=4] {'rows','units'}, use_global_device_ids=true, to_apply=%region_6.7 | all-reduce | flops 276 | bytes 2208 | tf_op jit(solution)/shard_map/psum | solution.py:158
  2071.4 53.1 %reduce-scatter.4.cloned.1.call-done = f32[256,2048]{1,0:T(8,128)} async-done(((f32[2048,2048]{1,0:T(8,128)}), f32[256,2048]{1,0:T(8,128)}) %reduce-scatter.4.cloned.1.call-update) | async-done | bytes 2097168 | tf_op jit(solution)/shard_map/reduce_scatter | solution.py:144
  2138.9 65.1 %all-reduce.7.cloned.1.call-done = (f32[100,4,512]{2,1,0:T(4,128)}, f32[512,275]{0,1:T(8,128)}) async-done(((f32[100,4,512]{2,1,0:T(4,128)}, f32[512,275]{0,1:T(8,128)}), (f32[100,4,512]{2,1,0:T(4,128)}, f32[512,275]{0,1:T(8,128)})) %all-reduce.7.cloned.1.call-update) | async-done | bytes 1382416 | tf_op jit(solution)/shard_map/psum | solution.py:157
  (935 shorter events, 1592.3 us)
Async XLA Ops:
  8.0 59.8 %all-gather.3.cloned.1.call-start = ((), (), s32[]{:S(2)}) async-start(), calls=%async_computation.5 | async-start | bytes 9437184 | tf_op jit(solution)/shard_map/all_gather | solution.py:55
  807.1 50.2 %all-to-all-start = ((bf16[4,512,512]{2,1,0:T(8,128)(2,1)}), bf16[4,512,512]{2,1,0:T(8,128)(2,1)}, u32[]{:S(2)}, u32[]{:S(2)}) async-start(bf16[4,512,512]{2,1,0:T(8,128)(2,1)} %bitcast.187), calls=%async_computation.1 | async-start | bytes 4194304 | tf_op jit(solution)/shard_map/all_to_all | solution.py:94
  811.7 48.5 %all-gather.5.cloned.1.call-start = ((), (), s32[]{:S(2)}) async-start(), calls=%async_computation.6 | async-start | bytes 1433600 | tf_op jit(solution)/shard_map/all_gather | solution.py:93
  866.2 50.5 %all-to-all-start.1 = ((bf16[512,4,512]{2,0,1:T(8,128)(2,1)}), bf16[512,4,512]{2,0,1:T(8,128)(2,1)}, u32[]{:S(2)}, u32[]{:S(2)}) async-start(bf16[512,4,512]{2,0,1:T(8,128)(2,1)} %bitcast.189), calls=%async_computation.2 | async-start | bytes 4194304 | tf_op jit(solution)/shard_map/all_to_all | solution.py:100
  925.1 31.8 %reduce-scatter.8.cloned.1.call-start = ((), (), s32[]{:S(2)}) async-start(), calls=%async_computation.11 | async-start | bytes 655360 | tf_op jit(solution)/shard_map/while/body/eval_jaxpr/reduce_scatter | solution.py:128
  990.1 31.2 %reduce-scatter.8.cloned.1.call-start = ((), (), s32[]{:S(2)}) async-start(), calls=%async_computation.11 | async-start | bytes 655360 | tf_op jit(solution)/shard_map/while/body/eval_jaxpr/reduce_scatter | solution.py:128
  1054.5 31.2 %reduce-scatter.8.cloned.1.call-start = ((), (), s32[]{:S(2)}) async-start(), calls=%async_computation.11 | async-start | bytes 655360 | tf_op jit(solution)/shard_map/while/body/eval_jaxpr/reduce_scatter | solution.py:128
  1086.7 31.2 %reduce-scatter.8.cloned.1.call-start = ((), (), s32[]{:S(2)}) async-start(), calls=%async_computation.11 | async-start | bytes 655360 | tf_op jit(solution)/shard_map/while/body/eval_jaxpr/reduce_scatter | solution.py:128
  1151.2 31.2 %reduce-scatter.8.cloned.1.call-start = ((), (), s32[]{:S(2)}) async-start(), calls=%async_computation.11 | async-start | bytes 655360 | tf_op jit(solution)/shard_map/while/body/eval_jaxpr/reduce_scatter | solution.py:128
  1183.4 31.2 %reduce-scatter.8.cloned.1.call-start = ((), (), s32[]{:S(2)}) async-start(), calls=%async_computation.11 | async-start | bytes 655360 | tf_op jit(solution)/shard_map/while/body/eval_jaxpr/reduce_scatter | solution.py:128
  1215.6 31.2 %reduce-scatter.8.cloned.1.call-start = ((), (), s32[]{:S(2)}) async-start(), calls=%async_computation.11 | async-start | bytes 655360 | tf_op jit(solution)/shard_map/while/body/eval_jaxpr/reduce_scatter | solution.py:128
  1247.8 31.2 %reduce-scatter.8.cloned.1.call-start = ((), (), s32[]{:S(2)}) async-start(), calls=%async_computation.11 | async-start | bytes 655360 | tf_op jit(solution)/shard_map/while/body/eval_jaxpr/reduce_scatter | solution.py:128
  1280.0 31.2 %reduce-scatter.8.cloned.1.call-start = ((), (), s32[]{:S(2)}) async-start(), calls=%async_computation.11 | async-start | bytes 655360 | tf_op jit(solution)/shard_map/while/body/eval_jaxpr/reduce_scatter | solution.py:128
  1312.3 31.2 %reduce-scatter.8.cloned.1.call-start = ((), (), s32[]{:S(2)}) async-start(), calls=%async_computation.11 | async-start | bytes 655360 | tf_op jit(solution)/shard_map/while/body/eval_jaxpr/reduce_scatter | solution.py:128
  1344.5 31.2 %reduce-scatter.8.cloned.1.call-start = ((), (), s32[]{:S(2)}) async-start(), calls=%async_computation.11 | async-start | bytes 655360 | tf_op jit(solution)/shard_map/while/body/eval_jaxpr/reduce_scatter | solution.py:128
  1408.9 31.2 %reduce-scatter.8.cloned.1.call-start = ((), (), s32[]{:S(2)}) async-start(), calls=%async_computation.11 | async-start | bytes 655360 | tf_op jit(solution)/shard_map/while/body/eval_jaxpr/reduce_scatter | solution.py:128
  1441.1 31.2 %reduce-scatter.8.cloned.1.call-start = ((), (), s32[]{:S(2)}) async-start(), calls=%async_computation.11 | async-start | bytes 655360 | tf_op jit(solution)/shard_map/while/body/eval_jaxpr/reduce_scatter | solution.py:128
  1505.6 31.2 %reduce-scatter.8.cloned.1.call-start = ((), (), s32[]{:S(2)}) async-start(), calls=%async_computation.11 | async-start | bytes 655360 | tf_op jit(solution)/shard_map/while/body/eval_jaxpr/reduce_scatter | solution.py:128
  1537.8 31.2 %reduce-scatter.8.cloned.1.call-start = ((), (), s32[]{:S(2)}) async-start(), calls=%async_computation.11 | async-start | bytes 655360 | tf_op jit(solution)/shard_map/while/body/eval_jaxpr/reduce_scatter | solution.py:128
  1570.0 31.2 %reduce-scatter.8.cloned.1.call-start = ((), (), s32[]{:S(2)}) async-start(), calls=%async_computation.11 | async-start | bytes 655360 | tf_op jit(solution)/shard_map/while/body/eval_jaxpr/reduce_scatter | solution.py:128
  1956.7 47.7 %reduce-scatter.6.cloned.1.call-start = ((), (), s32[]{:S(2)}) async-start(), calls=%async_computation.9 | async-start | bytes 2867200 | tf_op jit(solution)/shard_map/reduce_scatter | solution.py:102
  1957.2 167.2 %reduce-scatter.4.cloned.1.call-start = ((), (), s32[]{:S(2)}) async-start(), calls=%async_computation.8 | async-start | bytes 18874368 | tf_op jit(solution)/shard_map/reduce_scatter | solution.py:144
  1981.7 157.2 %all-reduce.5.cloned.1.call-start = ((), (), s32[]{:S(2)}) async-start(), calls=%async_computation.7 | async-start | bytes 286720 | tf_op jit(solution)/shard_map/psum | solution.py:158
  1991.8 212.2 %all-reduce.7.cloned.1.call-start = ((), (), s32[]{:S(2)}) async-start(), calls=%async_computation.10 | async-start | bytes 2785280 | tf_op jit(solution)/shard_map/psum | solution.py:157
  (30 other events, 800.4 us)
Sparse Core Ops, SparseCore 0:
  10.8 57.0 all-gather.2
  936.2 20.6 reduce-scatter.7
  1001.3 19.9 reduce-scatter.7
  1033.5 19.9 reduce-scatter.7
  1065.7 19.9 reduce-scatter.7
  1097.9 19.9 reduce-scatter.7
  1130.2 19.9 reduce-scatter.7
  1162.4 19.9 reduce-scatter.7
  1194.6 19.9 reduce-scatter.7
  1226.8 19.9 reduce-scatter.7
  1259.0 19.9 reduce-scatter.7
  1291.3 19.9 reduce-scatter.7
  1323.5 19.9 reduce-scatter.7
  1355.7 19.9 reduce-scatter.7
  1387.9 19.9 reduce-scatter.7
  1420.1 19.9 reduce-scatter.7
  1452.3 19.9 reduce-scatter.7
  1484.6 19.9 reduce-scatter.7
  1516.8 19.9 reduce-scatter.7
  1549.0 19.9 reduce-scatter.7
  1581.2 19.9 reduce-scatter.7
  1613.4 19.9 reduce-scatter.7
  1991.9 146.9 all-reduce.4
  2143.2 60.7 all-reduce.6
  (11 shorter events, 218.9 us)
Sparse Core Ops, SparseCore 1:
  813.7 43.7 all-gather.4
  1959.5 44.9 reduce-scatter.5
  2007.8 116.6 reduce-scatter.3
where the time goes:
time: 2220 us
  waiting for transfers between devices  881 us (40%)
  blocking collectives  510 us (23%)
  matrix products  458 us (21%)
  local copies, waits for them, and re-layouts  185 us (8%)
  other arithmetic  150 us (7%)
    reduce_scatter x32, waiting for transfers between devices, retreat(): lax.psum_scatter(contract(weight_full, dpre, 1, 1), 'units', scatter_dime...  607 us
    all_gather x32, blocking collectives, advance(): lax.all_gather(hidden_prev.astype(jnp.bfloat16), 'units', axis=1, tiled=T...  456 us
    dot_general x37, matrix products, contract(): lax.dot_general(left, right, (((left_dim,), (right_dim,)), ((), ())), pre...  258 us
    dot_general x32, matrix products, advance(): jnp.dot(gathered, weight_full, preferred_element_type=jnp.float32)  187 us
    psum x1, waiting for transfers between devices, on_device(): lax.psum((input_part, gate_part, decoder_part), 'rows')  65.1 us
    reduce_scatter x1, waiting for transfers between devices, on_device(): lax.psum_scatter(contract(columns, dpre_flat, 0, 0), 'rows', scatter_dime...  53.1 us
    all_gather x1, waiting for transfers between devices, on_device(): lax.all_gather(recurrent_weight, 'rows', axis=0, tiled=True)  47.6 us
    dynamic_update_slice x64, local copies, waits for them, and re-layouts, on_device(): lax.scan(advance, (init_hidden, init_cell), (drive, active))  46.7 us
  transfers between devices with their start and end apart: 40, of which 39 were waited for; matrix products, arithmetic and copies ran while one was open for 5% of the time, Pallas kernels for 0%

commit v1 on v0

v1 whole, which is shorter than its diff:
```python
import functools
import math

import jax
import jax.numpy as jnp
from jax import lax
from jax.experimental import pallas as pl
from jax.experimental.pallas import tpu as pltpu
from jax.sharding import PartitionSpec as P

BF16 = jnp.bfloat16
F32 = jnp.float32
LANES = 128
ID_BASE = 16
MIB = 2**20
STEP_VMEM = 26 * MIB
BACK_VMEM = 26 * MIB
LOAD_VMEM = 4 * MIB
ASSEMBLE_VMEM = 16 * MIB
FORWARD_CHUNKS = (8, 8, 8, 8)
BACKWARD_CHUNKS = (8, 8, 8, 5, 3)
LAST_CHUNKS = 2
ANYWHERE = pl.BlockSpec(memory_space=pl.ANY)
IN_VMEM = pl.BlockSpec(memory_space=pltpu.VMEM)
IN_SMEM = pl.BlockSpec(memory_space=pltpu.SMEM)


def contract(left, right, left_dim, right_dim):
    return lax.dot_general(
        left, right, (((left_dim,), (right_dim,)), ((), ())), preferred_element_type=F32
    )


def keep_near(value):
    return pltpu.with_memory_space_constraint(value, pltpu.VMEM)


def row_shift(sizes, axis, step):
    size_y, size_x, size_c = sizes
    pairs = []
    for y in range(size_y):
        for x in range(size_x):
            for c in range(size_c):
                to = [y, x, c]
                to[axis] = (to[axis] + step) % sizes[axis]
                pairs.append(
                    ((y * size_x + x) * size_c + c, (to[0] * size_x + to[1]) * size_c + to[2])
                )
    return pairs


def send_rows(value, sizes, axis, step):
    return lax.ppermute(value, "rows", row_shift(sizes, axis, step))


def send_units(value, step):
    count = lax.axis_size("units")
    return lax.ppermute(value, "units", [(z, (z + step) % count) for z in range(count)])


def swap_units(value, bits):
    count = lax.axis_size("units")
    return lax.ppermute(value, "units", [(z, z ^ bits) for z in range(count)])


def in_hbm(shape, dtype):
    return pltpu.HBM(shape, dtype)


def keep_far(value):
    return pltpu.with_memory_space_constraint(value, pltpu.HBM)


LITTLE = pl.CostEstimate(flops=0, bytes_accessed=1024, transcendentals=0)


def hold_kernel(*refs):
    pass


def hold(values, ties):
    return pl.pallas_call(
        hold_kernel,
        in_specs=[ANYWHERE] * (len(values) + len(ties)),
        out_specs=[ANYWHERE] * len(values),
        out_shape=[in_hbm(v.shape, v.dtype) for v in values],
        input_output_aliases={i: i for i in range(len(values))},
        cost_estimate=LITTLE,
        name="hold",
    )(*[keep_far(v) for v in values], *ties)


def assemble_kernel(plan, count, ties, *refs):
    where = refs[0]
    sources = refs[1 : 1 + count]
    outs = refs[1 + count + ties :]
    below = where[1] < 2
    for out, blocks in zip(outs, plan):
        for index, block in enumerate(blocks):
            if len(block) == 1:
                ((source, at),) = block
                out[index] = sources[source][at]
            else:
                (low, low_at), (high, high_at) = block

                @pl.when(below)
                def _():
                    out[index] = sources[low][low_at]

                @pl.when(jnp.logical_not(below))
                def _():
                    out[index] = sources[high][high_at]


def assemble(where, outs, ties=()):
    sources, plan = [], []
    for blocks in outs:
        entry = []
        for block in blocks:
            choices = block if isinstance(block[0], tuple) else (block,)
            row = []
            for array, index in choices:
                known = [i for i, other in enumerate(sources) if other is array]
                if not known:
                    sources.append(array)
                    known = [len(sources) - 1]
                row.append((known[0], index))
            entry.append(tuple(row))
        plan.append(tuple(entry))
    shape, dtype = sources[0].shape[1:], sources[0].dtype
    return pl.pallas_call(
        functools.partial(assemble_kernel, tuple(plan), len(sources), len(ties)),
        in_specs=[IN_SMEM] + [IN_VMEM] * len(sources) + [ANYWHERE] * len(ties),
        out_specs=[IN_VMEM] * len(plan),
        out_shape=[jax.ShapeDtypeStruct((len(blocks),) + shape, dtype) for blocks in plan],
        compiler_params=pltpu.CompilerParams(vmem_limit_bytes=ASSEMBLE_VMEM),
        cost_estimate=LITTLE,
        name="assemble",
    )(where, *sources, *ties)


def piece_copies(where, sizes, units, rows_dev, places, arrays, target, sems):
    size_y, size_x, size_c = sizes
    me_r, me_z = where[0], where[1]
    me_c = lax.rem(me_r, size_c)
    me_x = lax.rem(lax.div(me_r, size_c), size_x)
    me_y = lax.div(me_r, size_c * size_x)

    def back(me, shift, size):
        return lax.rem(me - shift + size, size)

    copies = []
    for array, array_places in zip(arrays, places):
        rows = array.shape[1]
        for index, (offset, dz, dy, dx, dc) in enumerate(array_places):
            z = back(me_z, dz, units)
            r = (back(me_y, dy, size_y) * size_x + back(me_x, dx, size_x)) * size_c
            r = r + back(me_c, dc, size_c)
            first = pl.multiple_of(r * rows_dev + offset, rows)
            to = target.at[z, pl.ds(first, rows)]
            copies.append(
                (dz, pltpu.make_async_copy(array.at[index], to, sems.at[len(copies)]))
            )
    return copies


def load_kernel(count, config, *refs):
    places, sizes, units, rows_dev = config
    where, arrays = refs[0], refs[1 : 1 + count]
    target, sems = refs[-2:]
    copies = piece_copies(where, sizes, units, rows_dev, places, arrays, target, sems)
    for _, copy in copies:
        copy.start()
    for _, copy in copies:
        copy.wait()


def load_pieces(weight, shape, where, held, sizes, rows_dev, ties=()):
    arrays = [array for array, _ in held]
    places = tuple(tuple(array_places) for _, array_places in held)
    count = len(arrays)
    total = sum(len(p) for p in places)
    operands = [where] + arrays + list(ties)
    specs = [IN_SMEM] + [ANYWHERE] * (len(operands) - 1)
    aliases = {}
    if weight is not None:
        operands.append(keep_near(weight))
        specs.append(IN_VMEM)
        aliases = {len(operands) - 1: 0}
    return pl.pallas_call(
        functools.partial(load_kernel, count, (places, sizes, shape[0], rows_dev)),
        in_specs=specs,
        out_specs=IN_VMEM,
        out_shape=pltpu.VMEM(shape, BF16),
        input_output_aliases=aliases,
        scratch_shapes=[pltpu.SemaphoreType.DMA((total,))],
        compiler_params=pltpu.CompilerParams(vmem_limit_bytes=MIB),
        cost_estimate=LITTLE,
        name="load_pieces",
    )(*operands)


def gather_weight(own, where, sizes, shape, ready, pack, seqs):
    rows_dev, block = own.shape
    half = rows_dev // 2
    both = own.reshape(2, half, block)
    offsets = (0, half)

    def places(dz, parts=(0, 1)):
        return [(offsets[part], dz, 0, 0, 0) for part in parts]

    def far(array_places, axis):
        return [tuple(1 if i == axis + 2 else v for i, v in enumerate(p)) for p in array_places]

    def swap(axis, pair):
        array, array_places = pair
        return send_rows(array, sizes, axis, 1), far(array_places, axis)

    def blocks(*pairs):
        return [(array, i) for array, array_places in pairs for i in range(len(array_places))]

    def all_places(*pairs):
        return sum([array_places for _, array_places in pairs], [])

    own_top, own_low = assemble(where, [[(both, 0)], [(both, 1)]])
    x1 = swap(1, (own_top, places(0, (0,))))
    y1 = swap(0, (own_low, places(0, (1,))))
    z1 = (send_units(both, 1), places(1))
    arrived = [(both, places(0)), z1, x1, y1]
    both2, x_next, y_next, c_next = assemble(
        where,
        [
            [(both, 0), (both, 1)],
            [(both, 1), (y1[0], 0), (z1[0], 0)],
            [(both, 0), (x1[0], 0), (z1[0], 1)],
            blocks(*arrived),
        ],
    )
    x2 = swap(1, (x_next, places(0, (1,)) + y1[1] + places(1, (0,))))
    y2 = swap(0, (y_next, places(0, (0,)) + x1[1] + places(1, (1,))))
    z3 = (send_units(both2, 3), places(3))
    c2 = swap(2, (c_next, all_places(*arrived)))
    found = list(arrived)
    arrived = [z3, x2, y2]
    x_next, y_next, c_next = assemble(
        where,
        [
            [(z1[0], 1), (y2[0], 2), (z3[0], 0)],
            [(z1[0], 0), (x2[0], 2), (z3[0], 1)],
            blocks(*arrived),
        ],
    )
    x3 = swap(1, (x_next, places(1, (1,)) + y2[1][2:] + places(3, (0,))))
    y3 = swap(0, (y_next, places(1, (0,)) + x2[1][2:] + places(3, (1,))))
    up = lax.ppermute(z1[0], "units", [(1, 2), (2, 3)])
    down = lax.ppermute(z3[0], "units", [(2, 1), (1, 0)])
    c3 = swap(2, (c_next, all_places(*arrived)))
    found += arrived + [c2]
    z2_top, z2_low = ((down, 0), (up, 0)), ((down, 1), (up, 1))
    arrived = [x3, y3]
    x_next, y_next, c_next, z2_next = assemble(
        where,
        [
            [(z3[0], 1), (y3[0], 2), z2_top],
            [(z3[0], 0), (x3[0], 2), z2_low],
            blocks(*arrived) + [z2_top, z2_low],
            [z2_top, z2_low],
        ],
        ready,
    )
    z2 = (z2_next, places(2))
    arrived.append(z2)
    x4 = swap(1, (x_next, places(3, (1,)) + y3[1][2:] + places(2, (0,))))
    y4 = swap(0, (y_next, places(3, (0,)) + x3[1][2:] + places(2, (1,))))
    c4 = swap(2, (c_next, all_places(*arrived)))
    packs = [pack[0]]
    for bits in range(1, shape[0]):
        packs.append(swap_units(hold([pack[bits]], [z2_next])[0], bits))
    found += arrived + [c3]
    arrived = [x4, y4]
    x_next, y_next, c_next = assemble(
        where,
        [[(z2[0], 1), (y4[0], 2)], [(z2[0], 0), (x4[0], 2)], blocks(*arrived)],
    )
    x5 = swap(1, (x_next, places(2, (1,)) + y4[1][2:]))
    y5 = swap(0, (y_next, places(2, (0,)) + x4[1][2:]))
    c5 = swap(2, (c_next, all_places(*arrived)))
    found += arrived + [c4]
    arrived = [x5, y5]
    (c_next,) = assemble(where, [blocks(*arrived)], packs[1:])
    c6 = swap(2, (c_next, all_places(*arrived)))
    found += arrived + [c5]
    found.append(c6)
    win_rows = pack[0].shape[0] - 2 * seqs
    others = send_rows(jnp.stack([v[:win_rows] for v in packs]), sizes, 2, 1)
    win, hidden, cell = join_packs(where, packs, others, seqs)
    weight = load_pieces(None, shape, where, found, sizes, rows_dev, [win])
    return weight, win, hidden, cell


def load_whole_kernel(source, target, sems):
    copies = [
        pltpu.make_async_copy(source.at[z], target.at[z], sems.at[z])
        for z in range(source.shape[0])
    ]
    for copy in copies:
        copy.start()
    for copy in copies:
        copy.wait()


def load_whole(whole, shape):
    return pl.pallas_call(
        load_whole_kernel,
        in_specs=[ANYWHERE],
        out_specs=IN_VMEM,
        out_shape=pltpu.VMEM(shape, BF16),
        scratch_shapes=[pltpu.SemaphoreType.DMA((shape[0],))],
        compiler_params=pltpu.CompilerParams(vmem_limit_bytes=LOAD_VMEM),
        name="load_whole",
    )(whole.reshape(shape))


def turn_blocks(weight):
    tile = 256
    tiles = weight.shape[1] // tile

    def block(z, carry):
        for i in range(tiles):
            at_i = slice(i * tile, (i + 1) * tile)
            weight[z, at_i, at_i] = weight[z, at_i, at_i].T
            for j in range(i + 1, tiles):
                at_j = slice(j * tile, (j + 1) * tile)
                upper = weight[z, at_i, at_j].T
                weight[z, at_i, at_j] = weight[z, at_j, at_i].T
                weight[z, at_j, at_i] = upper
        return carry

    lax.fori_loop(0, weight.shape[0], block, 0)


def join_kernel(halves, *refs):
    where = refs[0]
    win, hidden, cell = refs[-4:-1]
    sems = refs[-1]
    packs, others = refs[1:-4], ()
    if halves == 2:
        packs, others = refs[1:-5], refs[-5]
    rows = win.shape[1] // halves
    width = win.shape[2] // 4
    copies = []
    for bits, pack in enumerate(packs):
        z = jnp.bitwise_xor(where[1], bits)
        first = 0 if halves == 1 else lax.rem(where[0], 2) * rows
        to = win.at[z, pl.ds(pl.multiple_of(first, rows), rows)]
        copies.append(pltpu.make_async_copy(pack.at[pl.ds(0, rows)], to, sems.at[len(copies)]))
        if halves == 2:
            to = win.at[z, pl.ds(pl.multiple_of(rows - first, rows), rows)]
            copies.append(pltpu.make_async_copy(others.at[bits], to, sems.at[len(copies)]))
    for copy in copies:
        copy.start()
    for bits, pack in enumerate(packs):
        z = jnp.bitwise_xor(where[1], bits)
        at = pl.ds(pl.multiple_of(z * width, width), width)
        seqs = hidden.shape[0]
        upper = pack[rows : rows + seqs, :].astype(F32)
        lower = pack[rows + seqs : rows + 2 * seqs, : 2 * width].astype(F32)
        sums = upper[:, : 2 * width] + upper[:, 2 * width :] + lower
        hidden[:, at] = sums[:, :width]
        cell[:, at] = sums[:, width:]
    for copy in copies:
        copy.wait()


def pack_state(win_rows, state):
    terms = []
    for _ in range(3):
        term = state.astype(BF16)
        terms += [term[0], term[1]]
        state = state - term.astype(F32)
    width = state.shape[2]
    upper = jnp.concatenate(terms[:4], axis=1)
    lower = jnp.concatenate(terms[4:] + [jnp.zeros_like(terms[0])] * 2, axis=1)
    return jnp.concatenate([win_rows, upper, lower], axis=0)


def join_packs(where, packs, others, seqs):
    units = len(packs)
    block = packs[0].shape[1]
    halves = 1 if others is None else 2
    padded = halves * (packs[0].shape[0] - 2 * seqs)
    shape = (seqs, units * block // 4)
    extra = [] if others is None else [others]
    return pl.pallas_call(
        functools.partial(join_kernel, halves),
        in_specs=[IN_SMEM] + [IN_VMEM] * (units + len(extra)),
        out_specs=[IN_VMEM] * 3,
        out_shape=[
            pltpu.VMEM((units, padded, block), BF16),
            jax.ShapeDtypeStruct(shape, F32),
            jax.ShapeDtypeStruct(shape, F32),
        ],
        scratch_shapes=[pltpu.SemaphoreType.DMA((units * halves,))],
        compiler_params=pltpu.CompilerParams(vmem_limit_bytes=8 * MIB),
        cost_estimate=LITTLE,
        name="join_packs",
    )(where, *packs, *extra)


def gates_of(acc, unit_width):
    return (
        jax.nn.sigmoid(acc[:, :unit_width]),
        jax.nn.sigmoid(acc[:, unit_width : 2 * unit_width]),
        jnp.tanh(acc[:, 2 * unit_width : 3 * unit_width]),
        jax.nn.sigmoid(acc[:, 3 * unit_width :]),
    )


def forward_kernel(start, ties, *refs):
    lengths, embedded, hidden0, cell0, win, weight = refs[:6]
    preact_o, cells_o, before_o, low_o, hidden, cell = refs[6 + ties :]
    step = pl.program_id(0)
    units, _, block = weight.shape
    unit_width = block // 4

    @pl.when(step == 0)
    def _():
        hidden[...] = hidden0[...]
        cell[...] = cell0[...]

    alive = (start + step < lengths[...]).astype(F32)
    before_o[0] = hidden[...].astype(BF16)
    low = before_o[0]
    now = embedded[0]
    for z in range(units):
        at = slice(z * unit_width, (z + 1) * unit_width)
        acc = jnp.dot(low, weight[z], preferred_element_type=F32)
        acc = acc + jnp.dot(now, win[z], preferred_element_type=F32)
        preact_o[0, z] = acc
        gate_in, gate_forget, gate_cell, gate_out = gates_of(acc, unit_width)
        cell_prev = cell[:, at]
        hidden_prev = hidden[:, at]
        cell_new = gate_forget * cell_prev + gate_in * gate_cell
        hidden_new = gate_out * jnp.tanh(cell_new)
        hidden_next = alive * hidden_new + (1.0 - alive) * hidden_prev
        cells_o[0, :, at] = cell_prev
        cell[:, at] = alive * cell_new + (1.0 - alive) * cell_prev
        hidden[:, at] = hidden_next
        low_o[0, :, at] = hidden_next.astype(BF16)


def step_cost(steps):
    return pl.CostEstimate(flops=0, bytes_accessed=steps * 16 * MIB, transcendentals=0)


def run_forward(lengths, embedded, hidden, cell, win, weight, start, steps, ties):
    seqs, hidden_width = hidden.shape
    units, _, block = win.shape
    stepped = lambda *shape: pl.BlockSpec((1,) + shape, lambda t: (t,) + (0,) * len(shape))
    later = lambda *shape: pl.BlockSpec((1,) + shape, lambda t: (t + start,) + (0,) * len(shape))
    return pl.pallas_call(
        functools.partial(forward_kernel, start, len(ties)),
        grid=(steps,),
        in_specs=[IN_VMEM, later(seqs, embedded.shape[2])] + [IN_VMEM] * 4 + [ANYWHERE] * len(ties),
        out_specs=[
            stepped(units, seqs, block),
            stepped(seqs, hidden_width),
            stepped(seqs, hidden_width),
            stepped(seqs, hidden_width),
            IN_VMEM,
            IN_VMEM,
        ],
        out_shape=[
            in_hbm((steps, units, seqs, block), F32),
            in_hbm((steps, seqs, hidden_width), F32),
            in_hbm((steps, seqs, hidden_width), BF16),
            in_hbm((steps, seqs, hidden_width), BF16),
            jax.ShapeDtypeStruct((seqs, hidden_width), F32),
            jax.ShapeDtypeStruct((seqs, hidden_width), F32),
        ],
        compiler_params=pltpu.CompilerParams(
            vmem_limit_bytes=STEP_VMEM, dimension_semantics=("arbitrary",)
        ),
        cost_estimate=step_cost(steps),
        name="forward_steps",
    )(
        lengths, keep_far(embedded), hidden, cell, keep_near(win), keep_near(weight),
        *ties,
    )


def backward_kernel(first_step, steps, ties, last, *refs):
    where, lengths, preact, cells, decoder, turned = refs[:6]
    refs = refs[6 + ties :]
    if not last:
        grad_h0, grad_c0 = refs[:2]
        refs = refs[2:]
    dpre_o, (grad_h, grad_c) = refs[:-2], refs[-2:]
    index = pl.program_id(0)
    step = first_step + steps - 1 - index
    units, block, _ = turned.shape
    unit_width = block // 4
    me_z = where[1]

    @pl.when(index == 0)
    def _():
        grad_h[...] = jnp.zeros_like(grad_h) if last else grad_h0[...]
        grad_c[...] = jnp.zeros_like(grad_c) if last else grad_c0[...]

    alive = (step < lengths[...]).astype(F32)
    total_grad = grad_h[...] + decoder[0].astype(F32)
    grad_h[...] = total_grad
    acc = (1.0 - alive) * total_grad
    for bits in range(units):
        z = jnp.bitwise_xor(me_z, bits)
        at = pl.ds(pl.multiple_of(z * unit_width, unit_width), unit_width)
        gate_in, gate_forget, gate_cell, gate_out = gates_of(preact[0, z], unit_width)
        cell_prev = cells[0, :, at]
        cell_new = gate_forget * cell_prev + gate_in * gate_cell
        cell_tanh = jnp.tanh(cell_new)
        dhidden = alive * grad_h[:, at]
        grad_cell = grad_c[:, at]
        dcell = alive * grad_cell + dhidden * gate_out * (1.0 - cell_tanh * cell_tanh)
        dpre = jnp.concatenate(
            [
                (dcell * gate_cell * gate_in * (1.0 - gate_in)).astype(BF16),
                (dcell * cell_prev * gate_forget * (1.0 - gate_forget)).astype(BF16),
                (dcell * gate_in * (1.0 - gate_cell * gate_cell)).astype(BF16),
                (dhidden * cell_tanh * gate_out * (1.0 - gate_out)).astype(BF16),
            ],
            axis=1,
        )
        grad_c[:, at] = (1.0 - alive) * grad_cell + dcell * gate_forget
        dpre_o[bits][0] = dpre
        acc = acc + jnp.dot(dpre, turned[z], preferred_element_type=F32)
    grad_h[...] = acc


def run_backward(
    where, lengths, preact, cells, offset, decoder, grads, turned, first_step, steps, ties
):
    _, units, seqs, block = preact.shape
    hidden_width = cells.shape[2]

    def backwards(last, *shape):
        return pl.BlockSpec((1,) + shape, lambda t: (last - t,) + (0,) * len(shape))

    last = first_step - offset + steps - 1
    return pl.pallas_call(
        functools.partial(backward_kernel, first_step, steps, len(ties), grads is None),
        grid=(steps,),
        in_specs=[
            IN_SMEM,
            IN_VMEM,
            backwards(last, units, seqs, block),
            backwards(last, seqs, hidden_width),
            backwards(first_step + steps - 1, seqs, hidden_width),
            IN_VMEM,
        ]
        + [ANYWHERE] * len(ties)
        + [IN_VMEM] * (0 if grads is None else 2),
        out_specs=[backwards(steps - 1, seqs, block)] * units + [IN_VMEM] * 2,
        out_shape=[in_hbm((steps, seqs, block), BF16)] * units
        + [jax.ShapeDtypeStruct((seqs, hidden_width), F32)] * 2,
        compiler_params=pltpu.CompilerParams(
            vmem_limit_bytes=BACK_VMEM, dimension_semantics=("arbitrary",)
        ),
        cost_estimate=step_cost(steps),
        name="backward_steps",
    )(
        where, lengths, keep_far(preact), keep_far(cells), keep_far(decoder), keep_near(turned), *ties,
        *([] if grads is None else grads),
    )


def decoder_kernel(chunks, units, scale, vocab, *refs):
    where, bias, targets, alive = refs[:4]
    lows = refs[4 : 4 + chunks]
    refs = refs[4 + chunks :]
    arrived, refs = refs[:units], refs[units:]
    turned, back, loss, bias_grad = refs[1:5]
    parts, (low, decoder, sems) = refs[5:-3], refs[-3:]
    unit_width = parts[0].shape[0]
    me_z = where[1]
    copies = []
    first = 0
    for number, chunk in enumerate(lows):
        count = chunk.shape[0]
        copies.append(
            pltpu.make_async_copy(chunk, low.at[pl.ds(first, count)], sems.at[number])
        )
        first += count
    for bits in range(units):
        first = jnp.bitwise_xor(me_z, bits) * unit_width
        to = decoder.at[pl.ds(pl.multiple_of(first, unit_width), unit_width)]
        copies.append(pltpu.make_async_copy(arrived[bits], to, sems.at[chunks + bits]))
    for copy in copies:
        copy.start()
    turn_blocks(turned)
    for copy in copies:
        copy.wait()
    weights = decoder[...]
    logits = jnp.dot(low[...], weights, preferred_element_type=F32) + bias[...]
    column = lax.broadcasted_iota(jnp.int32, logits.shape, 1)
    real = column < vocab
    maximum = jnp.max(jnp.where(real, logits, -jnp.inf), axis=1, keepdims=True)
    powers = jnp.where(real, jnp.exp(logits - maximum), 0.0)
    log_total = jnp.log(jnp.sum(powers, axis=1, keepdims=True)) + maximum
    probable = jnp.where(real, jnp.exp(logits - log_total), 0.0)
    hit = column == targets[...]
    picked = jnp.sum(jnp.where(hit, logits, 0.0), axis=1, keepdims=True)
    loss[...] = jnp.sum((log_total - picked) * alive[...], axis=0, keepdims=True) * scale
    dlogits = (probable - hit.astype(F32)) * (alive[...] * scale)
    dlogits = dlogits.astype(BF16)
    bias_grad[...] = jnp.sum(dlogits.astype(F32), axis=0, keepdims=True)
    back[...] = contract(dlogits, weights, 1, 1).astype(BF16)
    for bits in range(units):
        z = jnp.bitwise_xor(me_z, bits)
        at = pl.ds(pl.multiple_of(z * unit_width, unit_width), unit_width)
        parts[bits][...] = contract(low[:, at], dlogits, 0, 0).astype(parts[bits].dtype)


def run_decoder(where, pieces, bias, targets, alive, lows, scale, vocab, weight):
    units = len(pieces)
    hidden_width = lows[0].shape[1]
    padded = bias.shape[1]
    local = targets.shape[0]
    unit_width = hidden_width // units
    chunks = len(lows)
    return pl.pallas_call(
        functools.partial(decoder_kernel, chunks, units, scale, vocab),
        in_specs=[IN_SMEM] + [IN_VMEM] * 3 + [ANYWHERE] * (chunks + units) + [IN_VMEM],
        out_specs=[IN_VMEM] * (4 + units),
        out_shape=[
            pltpu.VMEM(weight.shape, BF16),
            in_hbm((local, hidden_width), BF16),
            in_hbm((1, 1), F32),
            in_hbm((1, padded), F32),
            in_hbm((unit_width, padded), F32),
        ]
        + [in_hbm((unit_width, padded), BF16)] * (units - 1),
        scratch_shapes=[
            pltpu.VMEM((local, hidden_width), BF16),
            pltpu.VMEM((hidden_width, padded), BF16),
            pltpu.SemaphoreType.DMA((chunks + len(pieces),)),
        ],
        compiler_params=pltpu.CompilerParams(vmem_limit_bytes=STEP_VMEM),
        input_output_aliases={4 + chunks + units: 0},
        name="decoder",
    )(
        where, bias, targets, alive, *[keep_far(v) for v in lows],
        *[keep_far(array) for array in pieces], keep_near(weight),
    )


def grow_kernel(spec, mode, sizes, *refs):
    refs = list(refs)
    where = refs.pop(0)
    arrays = [[refs.pop(0) for _ in range(count)] for count, _, _, _, _ in spec]
    dpres = [refs.pop(0) for _ in spec]
    column_sems, dpre_sems, column, dpre = refs[-4:]
    refs = refs[:-4]
    outer = jnp.logical_or(where[1] == 0, where[1] == 3)
    copies, pairs = [], []
    first = 0
    for number, (count, row, rows, _, parts) in enumerate(spec):
        at = pl.ds(first, rows)
        options = []
        for array, part in zip(arrays[number], parts):
            source = array if part is None else array.at[part]
            options.append(
                pltpu.make_async_copy(
                    source.at[pl.ds(row, rows)], column.at[at], column_sems.at[number]
                )
            )
        if count == 1:
            copies.append(options[0])
        else:
            pairs.append(options)
        copies.append(pltpu.make_async_copy(dpres[number], dpre.at[at], dpre_sems.at[number]))
        first += rows
    for copy in copies:
        copy.start()
    for inner_copy, outer_copy in pairs:
        pl.when(outer)(outer_copy.start)
        pl.when(jnp.logical_not(outer))(inner_copy.start)
    for copy in copies:
        copy.wait()
    for inner_copy, outer_copy in pairs:
        pl.when(outer)(outer_copy.wait)
        pl.when(jnp.logical_not(outer))(inner_copy.wait)
    d = dpre[...]

    if mode in ("first", "sum"):
        if mode == "sum":
            total_in, refs = refs[0], refs[1:]
        total, refs = refs[-1], refs[:-1]
        tile = 256

        def block(index, carry):
            at = pl.ds(pl.multiple_of(index * tile, tile), tile)
            part = contract(column[:, at], d, 0, 0)
            total[at, :] = part if mode == "first" else total_in[at, :] + part
            return carry

        lax.fori_loop(0, column.shape[1] // tile, block, 0)
    else:
        total_in, refs = refs[0], refs[1:]
        out, refs = refs[-1], refs[:-1]
        size_y, size_x, size_c = sizes
        dc = 1 if mode == "other" else 0
        me_r = where[0]
        me_c = lax.rem(me_r, size_c)
        me_x = lax.rem(lax.div(me_r, size_c), size_x)
        me_y = lax.div(me_r, size_c * size_x)
        tile = out.shape[1]

        def block(index, carry):
            dy = lax.div(index, size_x)
            dx = lax.rem(index, size_x)
            to = lax.rem(me_y + dy, size_y) * size_x + lax.rem(me_x + dx, size_x)
            to = to * size_c + lax.rem(me_c + dc, size_c)
            at = pl.ds(pl.multiple_of(to * tile, tile), tile)
            part = contract(column[:, at], d, 0, 0) + total_in[at, :]
            out[index] = part.astype(out.dtype)
            return carry

        lax.fori_loop(0, size_y * size_x, block, 0)
    if mode == "other":
        return

    if mode == "first":
        embedded, win, small, hot_sum = refs
    else:
        embedded, win, small_in, hot_in, small, hot_sum = refs
    words = jnp.concatenate([embedded[e : e + n, :] for _, _, n, e, _ in spec], axis=0)
    part = contract(words, d, 0, 0)
    small[...] = part if mode == "first" else part + small_in[...]
    back = contract(d, win[...], 1, 1)
    high = words[:, -2:-1].astype(F32)
    low = words[:, -1:].astype(F32)
    ids = (high * ID_BASE + low).astype(jnp.int32)
    vocab = lax.broadcasted_iota(jnp.int32, (ids.shape[0], hot_sum.shape[0]), 1)
    hot = (vocab == ids).astype(F32).astype(BF16)
    part = None
    for _ in range(3):
        term = back.astype(BF16)
        back = back - term.astype(F32)
        more = contract(hot, term, 0, 0)
        part = more if part is None else part + more
    hot_sum[...] = part if mode == "first" else part + hot_in[...]


def run_grow(where, runs, embedded, win, totals, mode, sizes, rows_dev, vocab):
    spec, arrays, dpres = [], [], []
    for choices, row, dpre, word in runs:
        rows = dpre.shape[0]
        spec.append((len(choices), row, rows, word, tuple(part for _, part in choices)))
        arrays += [keep_far(array) for array, _ in choices]
        dpres.append(keep_far(dpre))
    positions = sum(n for _, _, n, _, _ in spec)
    block, hidden_width = dpres[0].shape[1], runs[0][0][0][0].shape[-1]
    padded = embedded.shape[1]
    near = sizes[0] * sizes[1]
    operands = [where] + arrays + dpres
    specs = [IN_SMEM] + [ANYWHERE] * (len(operands) - 1)
    out_shape = []
    if mode != "first":
        operands.append(keep_near(totals[0]))
        specs.append(IN_VMEM)
    if mode != "other":
        operands += [embedded, win]
        specs += [IN_VMEM] * 2
        if mode != "first":
            operands += list(totals[1:])
            specs += [IN_VMEM] * 2
        out_shape = [
            jax.ShapeDtypeStruct((padded, block), F32),
            jax.ShapeDtypeStruct((vocab, padded), F32),
        ]
    if mode == "first":
        out_shape.append(pltpu.VMEM((hidden_width, block), F32))
    elif mode == "sum":
        out_shape.append(jax.ShapeDtypeStruct((hidden_width, block), F32))
    elif mode == "other":
        out_shape.append(jax.ShapeDtypeStruct((near, rows_dev, block), BF16))
    else:
        out_shape.append(jax.ShapeDtypeStruct((near, rows_dev, block), F32))
    return pl.pallas_call(
        functools.partial(grow_kernel, tuple(spec), mode, sizes),
        in_specs=specs,
        out_specs=[IN_VMEM] * len(out_shape),
        out_shape=out_shape,
        scratch_shapes=[
            pltpu.SemaphoreType.DMA((len(spec),)),
            pltpu.SemaphoreType.DMA((len(spec),)),
            pltpu.VMEM((positions, hidden_width), BF16),
            pltpu.VMEM((positions, block), BF16),
        ],
        compiler_params=pltpu.CompilerParams(vmem_limit_bytes=36 * MIB),
        name="weight_gradient",
    )(*operands)


def first_sum_kernel(kept, moved, send_a, keep_a, send_b, keep_b):
    width = send_a.shape[2]
    for dy in range(2):
        for dx in range(2):
            total = kept[dy * 2 + dx] + moved[dy * 2 + dx].astype(F32)
            for dx_first, out, keep, part in (
                (True, send_a, keep_a, total[:, :width]),
                (False, send_b, keep_b, total[:, width:]),
            ):
                near, index = (dx, dy) if dx_first else (dy, dx)
                if near == 0:
                    keep[index] = part
                else:
                    out[index] = part.astype(BF16)


def second_sum_kernel(keep_a, moved_a, keep_b, moved_b, send_a, last_a, send_b, last_b):
    for keep, moved, send, last in (
        (keep_a, moved_a, send_a, last_a),
        (keep_b, moved_b, send_b, last_b),
    ):
        last[...] = keep[0] + moved[0].astype(F32)
        send[...] = (keep[1] + moved[1].astype(F32)).astype(BF16)


def last_sum_kernel(last_a, moved_a, last_b, moved_b, out):
    width = out.shape[2]
    for index, (last, moved) in enumerate(((last_a, moved_a), (last_b, moved_b))):
        for part in range(2):
            at = slice(part * width, (part + 1) * width)
            out[:, 2 * index + part, :] = last[:, at] + moved[:, at].astype(F32)


def run_sum(kernel, out_shape, *operands):
    return pl.pallas_call(
        kernel,
        in_specs=[IN_VMEM] * len(operands),
        out_specs=[IN_VMEM] * len(out_shape),
        out_shape=out_shape,
        compiler_params=pltpu.CompilerParams(vmem_limit_bytes=40 * MIB),
        name="sum_rows",
    )(*operands)


def reduce_rows(kept, sent, sizes):
    _, rows_dev, block = kept.shape
    half = block // 2
    pair = jax.ShapeDtypeStruct((2, rows_dev, half), BF16)
    pair_sum = jax.ShapeDtypeStruct((2, rows_dev, half), F32)
    one = jax.ShapeDtypeStruct((rows_dev, half), BF16)
    one_sum = jax.ShapeDtypeStruct((rows_dev, half), F32)
    moved = send_rows(sent, sizes, 2, 1)
    send_a, keep_a, send_b, keep_b = run_sum(
        first_sum_kernel, [pair, pair_sum, pair, pair_sum], kept, moved
    )
    moved_a = send_rows(send_a, sizes, 1, 1)
    moved_b = send_rows(send_b, sizes, 0, 1)
    send_a, last_a, send_b, last_b = run_sum(
        second_sum_kernel, [one, one_sum, one, one_sum], keep_a, moved_a, keep_b, moved_b
    )
    moved_a = send_rows(send_a, sizes, 0, 1)
    moved_b = send_rows(send_b, sizes, 1, 1)
    (out,) = run_sum(
        last_sum_kernel,
        [jax.ShapeDtypeStruct((rows_dev, 4, block // 4), F32)],
        last_a, moved_a, last_b, moved_b,
    )
    return out


def show_kernel(chunks, *refs):
    where, last = refs[:2]
    befores, out, held, sems = refs[2:-3], refs[-3], refs[-2], refs[-1]
    units, window, seqs, width = held.shape
    me_z = where[1]
    outer = jnp.logical_or(me_z == 0, me_z == 3)
    lanes = pl.ds(pl.multiple_of(me_z * width, width), width)
    always, pairs = [], []
    start = 0
    for chunk, steps in enumerate(chunks):
        own, near, inner, far = befores[4 * chunk : 4 * chunk + 4]
        at = pl.ds(start, steps)

        def copy(source, bits):
            return pltpu.make_async_copy(
                source.at[:, :, lanes], held.at[bits, at], sems.at[chunk, bits]
            )

        always += [copy(own, 0), copy(near, 1)]
        for bits in (2, 3):
            pairs.append((copy(inner.at[3 - bits], bits), copy(far.at[bits - 2], bits)))
        start += steps
    for one in always:
        one.start()
    for inner_copy, outer_copy in pairs:
        pl.when(outer)(outer_copy.start)
        pl.when(jnp.logical_not(outer))(inner_copy.start)
    for one in always:
        one.wait()
    for inner_copy, outer_copy in pairs:
        pl.when(outer)(outer_copy.wait)
        pl.when(jnp.logical_not(outer))(inner_copy.wait)
    for bits in range(units):
        first = pl.multiple_of(jnp.bitwise_xor(me_z, bits) * seqs, seqs)
        rows = pl.ds(first, seqs)
        shown = jnp.swapaxes(held[bits].astype(F32), 0, 1)
        out[rows, : window - 1, :] = shown[:, 1:, :]
        out[rows, window - 1, :] = last[rows, :]


def show_hidden(where, last, befores, chunks, seqs):
    sequences, width = last.shape
    units = sequences // seqs
    window = sum(chunks)
    flat = [keep_far(v) for before in befores for v in before]
    return pl.pallas_call(
        functools.partial(show_kernel, chunks),
        in_specs=[IN_SMEM, IN_VMEM] + [ANYWHERE] * len(flat),
        out_specs=IN_VMEM,
        out_shape=jax.ShapeDtypeStruct((sequences, window, width), F32),
        scratch_shapes=[
            pltpu.VMEM((units, window, seqs, width), BF16),
            pltpu.SemaphoreType.DMA((len(chunks), units)),
        ],
        compiler_params=pltpu.CompilerParams(vmem_limit_bytes=40 * MIB),
        name="show_hidden",
    )(where, last, *flat)


def by_place(mine, other, here):
    return jnp.where(here == 0, jnp.stack([mine, other]), jnp.stack([other, mine]))


def sum_rows(value, me_r, sizes):
    if sizes != (2, 2, 2):
        return lax.psum(value, "rows")
    me = (me_r // 4, (me_r // 2) % 2, me_r % 2)
    count, width = value.shape
    held = value.reshape(2, 2, 2, count // 8, width)
    for axis in (2, 1, 0):
        keep = lax.dynamic_index_in_dim(held, me[axis], axis, keepdims=False)
        send = lax.dynamic_index_in_dim(held, 1 - me[axis], axis, keepdims=False)
        held = keep + send_rows(send.astype(BF16), sizes, axis, 1).astype(F32)
    held = held.astype(BF16)
    for axis in (0, 1, 2):
        held = by_place(held, send_rows(held, sizes, axis, 1), me[axis])
    return held.transpose(2, 1, 0, 3, 4).reshape(count, width).astype(F32)


def sum_all(value, sizes):
    units = lax.axis_size("units")
    if sizes != (2, 2, 2) or units != 4:
        return lax.psum(value, ("rows", "units"))
    for bits in (1, 2):
        value = value + swap_units(value, bits)
    for axis in (2, 1, 0):
        value = value + send_rows(value, sizes, axis, 1)
    return value


def on_device(
    sizes,
    token_ids,
    targets,
    lengths,
    init_hidden,
    init_cell,
    embedding,
    input_weight,
    recurrent_weight,
    gate_bias,
    decoder_weight,
    decoder_bias,
):
    sequences, window = token_ids.shape
    rows_dev, _, unit_width = recurrent_weight.shape
    units = lax.axis_size("units")
    block = 4 * unit_width
    hidden_width = units * unit_width
    vocab_size, embed_width = embedding.shape
    me_z = lax.axis_index("units")
    me_r = lax.axis_index("rows")
    where = jnp.stack([me_r, me_z]).astype(jnp.int32)
    seqs = sequences // units
    local = window * seqs
    loss_scale = 1.0 / window
    vocab_index = jnp.arange(vocab_size)
    others = range(1, units)

    padded = -(-(embed_width + 3) // LANES) * LANES
    terms = []
    left = gate_bias.reshape(1, block)
    for _ in range(3):
        term = left.astype(BF16)
        terms.append(term)
        left = left - term.astype(F32)
    win_own = jnp.concatenate(
        [input_weight.reshape(embed_width, block)]
        + terms
        + [jnp.zeros((padded - embed_width - 3, block), BF16)],
        axis=0,
    )
    tokens = jnp.arange(vocab_size)
    table = jnp.concatenate(
        [
            embedding,
            jnp.ones((vocab_size, 3), BF16),
            jnp.zeros((vocab_size, padded - embed_width - 5), BF16),
            jnp.stack([tokens // ID_BASE, tokens % ID_BASE], axis=1).astype(BF16),
        ],
        axis=1,
    )
    vocab_padded = -(-vocab_size // LANES) * LANES
    decoder_own = jnp.pad(decoder_weight, ((0, 0), (0, vocab_padded - vocab_size)))

    def share(value, bits, axis=0):
        origin = jnp.bitwise_xor(me_z, bits)
        return lax.dynamic_slice_in_dim(value, origin * seqs, seqs, axis)

    states = jnp.stack([init_hidden, init_cell])

    ids_time = jnp.stack([share(token_ids, bits).T for bits in range(units)])
    onehot = (ids_time[..., None] == tokens).astype(BF16).reshape(units * local, vocab_size)
    embedded = jnp.dot(onehot, table, preferred_element_type=F32).astype(BF16)
    embedded_own = embedded[:local].reshape(window, seqs, padded)
    lengths_own = share(lengths, 0).reshape(seqs, 1)
    target_own = share(targets, 0).T.reshape(local, 1)
    active = jnp.arange(window)[:, None] < lengths_own[:, 0][None, :]
    active = active.astype(F32).reshape(local, 1)
    bias_row = jnp.pad(decoder_bias, (0, vocab_padded - vocab_size)).reshape(1, vocab_padded)
    ready = [
        embedded, embedded_own, lengths_own, target_own, active, bias_row, win_own, decoder_own
    ]
    own_weight = recurrent_weight.reshape(rows_dev, block)
    shape = (units, hidden_width, block)
    square = sizes == (2, 2, 2) and units == 4
    win_rows = win_own
    if square:
        win_rows = lax.dynamic_slice_in_dim(
            win_own, lax.rem(me_r, 2) * (padded // 2), padded // 2, 0
        )
    pack = [pack_state(win_rows, share(states, bits, 1)) for bits in range(units)]
    if square:
        weight, win, hidden, cell = gather_weight(
            own_weight, where, sizes, shape, ready + pack, pack, seqs
        )
    else:
        weight = load_whole(lax.all_gather(own_weight, ("units", "rows"), axis=0), shape)
        packs = [pack[0]] + [swap_units(pack[bits], bits) for bits in others]
        win, hidden, cell = join_packs(where, packs, None, seqs)

    start = 0
    chunks = []
    befores = []
    lows = []
    decoders = [decoder_own]
    started = []

    def due():
        return [keep_far(v) for v in started[-2]] if len(started) > 1 else []

    def pass_on():
        launched = []
        for before in befores:
            if len(before) == 1:
                before.append(swap_units(before[0], 1))
            elif len(before) == 2:
                (joined,) = assemble(where, [[(before[0][None], 0), (before[1][None], 0)]])
                before.append(lax.ppermute(joined, "units", [(1, 2), (2, 1)]))
            elif len(before) == 3:
                before.append(lax.ppermute(before[2], "units", [(1, 0), (2, 3)]))
            else:
                continue
            launched.append(before[-1])
        return launched

    for steps in FORWARD_CHUNKS:
        preact, cells, before, low, hidden, cell = run_forward(
            lengths_own, embedded_own, hidden, cell, win, weight, start, steps, due()
        )
        befores.append([before])
        launched = pass_on()
        if start == 0:
            decoders += [swap_units(decoder_own, bits) for bits in others]
            launched += decoders[1:]
        started.append(launched)
        chunks.append((start, steps, preact, cells))
        lows.append(low.reshape(steps * seqs, hidden_width))
        start += steps
    final_hidden, final_cell = hidden, cell

    out = run_decoder(
        where, decoders, bias_row, target_own, active, lows, loss_scale, vocab_size, weight
    )
    turned, back_grad, loss_part, bias_part, decoder_mine = out[:5]
    decoder_parts = out[5:]
    back_grad = back_grad.reshape(window, seqs, hidden_width)

    grads = None
    end = window
    dpres = []
    pairs = []
    for number, steps in enumerate(BACKWARD_CHUNKS):
        first = end - steps
        for which, (offset, size, preact, cells) in enumerate(chunks):
            if offset <= first and end <= offset + size:
                break
        out = run_backward(
            where, lengths_own, preact, cells, offset, back_grad, grads, turned, first, steps, due()
        )
        grads = out[units:]
        dpres.append([out[0]] + [swap_units(out[bits], bits) for bits in others])
        started.append(dpres[-1][1:] + pass_on())
        pairs.append((first, end, first - offset, which))
        end = first

    flat = sum(befores, []) + list(decoder_parts)
    flat += [where, embedded, decoder_mine, bias_part, loss_part, final_hidden, final_cell, win_own]
    flat = hold(flat, [grads[0]])
    befores = [flat[i * 4 : (i + 1) * 4] for i in range(len(befores))]
    flat = flat[len(befores) * 4 :]
    decoder_parts, flat = flat[: units - 1], flat[units - 1 :]
    where, embedded, decoder_mine, bias_part, loss_part = flat[:5]
    final_hidden, final_cell, win_own = flat[5:]
    me_r, me_z = where[0], where[1]

    def grow(numbers, totals, mode):
        runs = []
        for number in numbers:
            first, end, offset, which = pairs[number]
            own, near, inner, far = [
                v.reshape(v.shape[:-3] + (-1, hidden_width)) for v in befores[which]
            ]
            for bits in range(units):
                choices = [
                    [(own, None)],
                    [(near, None)],
                    [(inner, 1), (far, 0)],
                    [(inner, 0), (far, 1)],
                ][bits]
                dpre = dpres[number][bits].reshape(-1, block)
                runs.append((choices, offset * seqs, dpre, bits * local + first * seqs))
        return run_grow(
            where, runs, embedded, win_own, totals, mode, sizes, rows_dev, vocab_padded
        )

    numbers = range(len(BACKWARD_CHUNKS))
    early, late = numbers[:-LAST_CHUNKS], numbers[-LAST_CHUNKS:]
    small, hot_sum, total = grow(early, None, "first")
    if square:
        (sent,) = grow(late, (total,), "other")
        small, hot_sum, kept = grow(late, (total, small, hot_sum), "own")
        recurrent_grad = reduce_rows(kept, sent, sizes)
    else:
        small, hot_sum, total = grow(late, (total, small, hot_sum), "sum")
        recurrent_grad = lax.psum_scatter(
            total.astype(BF16), "rows", scatter_dimension=0, tiled=True
        )
        recurrent_grad = recurrent_grad.astype(F32).reshape(rows_dev, 4, unit_width)
    decoder_sum = decoder_mine
    for bits in others:
        decoder_sum = decoder_sum + swap_units(decoder_parts[bits - 1], bits).astype(F32)

    small = jnp.concatenate([small, decoder_sum.reshape(-1, block)], axis=0)
    small = sum_rows(small, me_r, sizes)
    decoder_out = small[padded:].reshape(unit_width, vocab_padded)[:, :vocab_size]
    column = lax.broadcasted_iota(jnp.int32, hot_sum.shape, 1)
    pack = jnp.where(column < embed_width, hot_sum, bias_part.T)
    pack = jnp.where(column == embed_width + 1, loss_part, pack)
    pack = sum_all(pack, sizes)

    ends = jnp.stack([final_hidden, final_cell] + list(grads))
    shares = []
    for bits in range(units):
        to = jnp.bitwise_xor(me_z, bits)
        piece = lax.dynamic_slice_in_dim(ends, to * unit_width, unit_width, 2)
        shares.append(piece if bits == 0 else swap_units(piece, bits))
    shares = jnp.stack(shares)

    def ordered(value):
        return [
            lax.dynamic_index_in_dim(value, jnp.bitwise_xor(me_z, z), 0, keepdims=False)
            for z in range(units)
        ]

    ends = jnp.concatenate(ordered(shares), axis=1)

    hidden_out = show_hidden(where, ends[0], befores, FORWARD_CHUNKS, seqs)

    return (
        pack[0, embed_width + 1],
        hidden_out,
        ends[0],
        ends[1],
        pack[:vocab_size, :embed_width],
        small[:embed_width].reshape(embed_width, 4, unit_width),
        recurrent_grad,
        small[embed_width].reshape(4, unit_width),
        decoder_out,
        pack[:vocab_size, embed_width],
        ends[2],
        ends[3],
    )


def plane_sizes(rows):
    chips = rows // 2
    size_x = math.isqrt(chips)
    while chips % size_x:
        size_x -= 1
    return (chips // size_x, size_x, 2)


def solution(mesh):
    sizes = plane_sizes(mesh.shape["rows"])
    return jax.shard_map(
        functools.partial(on_device, sizes),
        mesh=mesh,
        in_specs=(
            P("rows", None),
            P("rows", None),
            P("rows"),
            P("rows", "units"),
            P("rows", "units"),
            P(),
            P(None, None, "units"),
            P("rows", None, "units"),
            P(None, "units"),
            P("units", None),
            P(),
        ),
        out_specs=(
            P(),
            P("rows", None, "units"),
            P("rows", "units"),
            P("rows", "units"),
            P(),
            P(None, None, "units"),
            P("rows", None, "units"),
            P(None, "units"),
            P("units", None),
            P(),
            P("rows", "units"),
            P("rows", "units"),
        ),
        check_vma=False,
    )
```

time: 2220 us -> 901 us (0.41)
  waiting for transfers between devices: 881 us -> 256 us
  blocking collectives: 510 us -> 0 us
  matrix products: 458 us -> 1.83 us
  Pallas kernels: 0 us -> 425 us
  other arithmetic: 150 us -> 15.8 us
  local copies, waits for them, and re-layouts: 185 us -> 64.8 us
  starting transfers between devices: 11 us -> 119 us
    reduce_scatter x34 -> x0, waiting for transfers between devices: 667 us -> none  [the longest x32 607 us: retreat(): lax.psum_scatter(contract(weight_full, dpre, 1, 1), 'units', scatter_dime...]
    dot_general x73 -> x1, matrix products: 458 us -> 1.83 us  [on_device(): embedded = jnp.dot(onehot, table, preferred_element_type=F32).astype(BF16)]
    all_gather x32 -> x0, blocking collectives: 456 us -> none  [advance(): lax.all_gather(hidden_prev.astype(jnp.bfloat16), 'units', axis=1, tiled=T...]
    pallas_call x0 -> x33, Pallas kernels: none -> 425 us  [the longest x4 161 us: run_forward(): pl.pallas_call(functools.partial(forward_kernel, start, len(ties)), grid=...]
    ppermute x0 -> x75, waiting for transfers between devices: none -> 256 us  [the longest x33 126 us: swap_units(): return lax.ppermute(value, 'units', [(z, z ^ bits) for z in range(count)])]
    ppermute x0 -> x75, starting transfers between devices: none -> 119 us  [the longest x33 77.3 us: swap_units(): return lax.ppermute(value, 'units', [(z, z ^ bits) for z in range(count)])]
    all_to_all x2 -> x0, waiting for transfers between devices: 88.7 us -> none  [the longest x1 44.8 us: on_device(): lax.all_to_all(hidden_low, 'units', split_axis=0, concat_axis=1, tiled=True)]
    psum x2 -> x0, waiting for transfers between devices: 75.9 us -> none  [the longest x1 65.1 us: on_device(): lax.psum((input_part, gate_part, decoder_part), 'rows')]
  transfers between devices with their start and end apart: 40 -> 75, of which waited for: 39 -> 32; matrix products, arithmetic and copies ran while one was open for 5% -> 6% of each run, Pallas kernels for 0% -> 38%
where the time goes in v1:
time: 901 us; the launch traced here: 894 us
  Pallas kernels  425 us (47%)
  waiting for transfers between devices  256 us (28%)
  starting transfers between devices  119 us (13%)
  local copies, waits for them, and re-layouts  64.8 us (7%)
  other arithmetic  15.8 us (2%)
  between operations  9.9 us (1%)
    pallas_call x4, Pallas kernels, run_forward(): pl.pallas_call(functools.partial(forward_kernel, start, len(ties)), grid=...  161 us
    pallas_call x5, Pallas kernels, run_backward(): pl.pallas_call(functools.partial(backward_kernel, first_step, steps, len(...  157 us
    ppermute x33, waiting for transfers between devices, swap_units(): return lax.ppermute(value, 'units', [(z, z ^ bits) for z in range(count)])  126 us
    ppermute x30, waiting for transfers between devices, send_rows(): return lax.ppermute(value, 'rows', row_shift(sizes, axis, step))  83.1 us
    ppermute x33, starting transfers between devices, swap_units(): return lax.ppermute(value, 'units', [(z, z ^ bits) for z in range(count)])  77.3 us
    pallas_call x3, Pallas kernels, run_grow(): pl.pallas_call(functools.partial(grow_kernel, tuple(spec), mode, sizes),...  48.5 us
    unnamed x237, local copies, waits for them, and re-layouts  30 us
    ppermute x2, waiting for transfers between devices, send_units(): lax.ppermute(value, 'units', [(z, (z + step) % count) for z in range(coun...  27.9 us
  transfers between devices with their start and end apart: 75, of which 32 were waited for; matrix products, arithmetic and copies ran while one was open for 6% of the time, Pallas kernels for 38%

profile of v1, /device:TPU:0, one launch (start us, length us, event | category | flops | bytes accessed | tf_op | source)
XLA Modules:
  0.0 893.5 jit_solution(1758559817311075431)
XLA Ops:
  43.4 18.7 %collective-permute-done.3.refs_3_.refs_1_.refs_5_ = bf16[2,128,2048]{2,1,0:T(8,128)(2,1)S(1)} collective-permute-done((bf16[2,128,2048]{2,1,0:T(8,128)(2,1)S(1)}, bf16[2,128,2048]{2,1,0:T(8,128)(2,1)S(1)}, u32[]{:S(2)}, u32[]{:S(2)}) %collective-permute-start.3) | collective-permute-done | bytes 1048608 | tf_op jit(solution)/shard_map/ppermute | solution.py:58
  88.5 19.4 %collective-permute-done.7.refs_3_ = bf16[2,128,2048]{2,1,0:T(8,128)(2,1)} collective-permute-done((bf16[2,128,2048]{2,1,0:T(8,128)(2,1)S(1)}, bf16[2,128,2048]{2,1,0:T(8,128)(2,1)}, u32[]{:S(2)}, u32[]{:S(2)}) %collective-permute-start.7) | collective-permute-done | bytes 1048608 | tf_op jit(solution)/shard_map/ppermute | solution.py:256
  124.1 12.2 %collective-permute-done.12.refs_4_.refs_5_ = bf16[96,2048]{1,0:T(8,128)(2,1)S(1)} collective-permute-done((bf16[96,2048]{1,0:T(8,128)(2,1)}, bf16[96,2048]{1,0:T(8,128)(2,1)S(1)}, u32[]{:S(2)}, u32[]{:S(2)}) %collective-permute-start.12) | collective-permute-done | bytes 393248 | tf_op jit(solution)/shard_map/ppermute | solution.py:63
  136.4 12.7 %collective-permute-start.10 = (bf16[96,2048]{1,0:T(8,128)(2,1)}, bf16[96,2048]{1,0:T(8,128)(2,1)S(1)}, u32[]{:S(2)}, u32[]{:S(2)}) collective-permute-start(bf16[96,2048]{1,0:T(8,128)(2,1)} %hold.4), channel_id=1, source_target_pairs={{0,1},{1,0},{2,3},{3,2},{4,5},{5,4},{6,7},{7,6},{8,9},{9,8},{10,11... | collective-permute-start | bytes 1179656 | tf_op jit(solution)/shard_map/ppermute | solution.py:63
  160.4 21.0 %collective-permute-done.19.refs_1_.refs_16_ = bf16[2,128,2048]{2,1,0:T(8,128)(2,1)S(1)} collective-permute-done((bf16[2,128,2048]{2,1,0:T(8,128)(2,1)S(1)}, bf16[2,128,2048]{2,1,0:T(8,128)(2,1)S(1)}, u32[]{:S(2)}, u32[]{:S(2)}) %collective-permute-start.19) | collective-permute-done | bytes 1048608 | tf_op jit(solution)/shard_map/ppermute | solution.py:53
  202.0 40.1 %forward_steps.4 = (f32[8,4,16,2048]{3,2,1,0:T(8,128)}, f32[8,16,2048]{2,1,0:T(8,128)}, bf16[8,16,2048]{2,1,0:T(8,128)(2,1)}, bf16[8,16,2048]{2,1,0:T(8,128)(2,1...) custom-call(s32[16,1]{1,0:T(8,128)} %copy-done.42, bf16[32,16,128]{2,1,0:T(8,128)(2,1)} %bitcast.215, f32[16,2048]{1,0:T(8,128)} %copy-done.46, ...), custom_call_target="tpu_custom_call" | custom-call | bytes 134217728 | tf_op jit(solution)/shard_map/forward_steps/pallas_call | solution.py:461
  242.2 40.1 %forward_steps.5 = (f32[8,4,16,2048]{3,2,1,0:T(8,128)}, f32[8,16,2048]{2,1,0:T(8,128)}, bf16[8,16,2048]{2,1,0:T(8,128)(2,1)}, bf16[8,16,2048]{2,1,0:T(8,128)(2,1...) custom-call(s32[16,1]{1,0:T(8,128)} %copy-done.42, bf16[32,16,128]{2,1,0:T(8,128)(2,1)} %bitcast.216, ...), custom_call_target="tpu_custom_call" | custom-call | bytes 134217728 | tf_op jit(solution)/shard_map/forward_steps/pallas_call | solution.py:461
  291.1 14.3 %collective-permute-done.29.refs_7_.refs_9_ = bf16[512,384]{1,0:T(8,128)(2,1)S(1)} collective-permute-done((bf16[512,384]{1,0:T(8,128)(2,1)S(1)}, bf16[512,384]{1,0:T(8,128)(2,1)S(1)}, u32[]{:S(2)}, u32[]{:S(2)}) %collective-permute-start.29) | collective-permute-done | bytes 393248 | tf_op jit(solution)/shard_map/ppermute | solution.py:63
  305.3 32.3 %collective-permute-done.30.refs_8_.refs_10_ = bf16[512,384]{1,0:T(8,128)(2,1)S(1)} collective-permute-done((bf16[512,384]{1,0:T(8,128)(2,1)S(1)}, bf16[512,384]{1,0:T(8,128)(2,1)S(1)}, u32[]{:S(2)}, u32[]{:S(2)}) %collective-permute-start.30) | collective-permute-done | bytes 393248 | tf_op jit(solution)/shard_map/ppermute | solution.py:63
  338.6 40.5 %forward_steps.6 = (f32[8,4,16,2048]{3,2,1,0:T(8,128)}, f32[8,16,2048]{2,1,0:T(8,128)}, bf16[8,16,2048]{2,1,0:T(8,128)(2,1)}, bf16[8,16,2048]{2,1,0:T(8,128)(2,1...) custom-call(s32[16,1]{1,0:T(8,128)} %copy-done.42, bf16[32,16,128]{2,1,0:T(8,128)(2,1)} %bitcast.217, ...), custom_call_target="tpu_custom_call" | custom-call | bytes 134217728 | tf_op jit(solution)/shard_map/forward_steps/pallas_call | solution.py:461
  401.7 40.1 %forward_steps.7 = (f32[8,4,16,2048]{3,2,1,0:T(8,128)}, f32[8,16,2048]{2,1,0:T(8,128)}, bf16[8,16,2048]{2,1,0:T(8,128)(2,1)}, bf16[8,16,2048]{2,1,0:T(8,128)(2,1...) custom-call(s32[16,1]{1,0:T(8,128)} %copy-done.42, bf16[32,16,128]{2,1,0:T(8,128)(2,1)} %bitcast.218, ...), custom_call_target="tpu_custom_call" | custom-call | bytes 134217728 | tf_op jit(solution)/shard_map/forward_steps/pallas_call | solution.py:461
  445.9 11.8 %collective-permute-done.35.refs_8_.refs_13_ = bf16[8,16,2048]{2,1,0:T(8,128)(2,1)S(1)} collective-permute-done((bf16[8,16,2048]{2,1,0:T(8,128)(2,1)}, bf16[8,16,2048]{2,1,0:T(8,128)(2,1)S(1)}, u32[]{:S(2)}, u32[]{:S(2)}) %collective-permute-start.35) | collective-permute-done | bytes 524320 | tf_op jit(solution)/shard_map/ppermute | solution.py:63
  460.2 15.8 %decoder.1 = (bf16[4,2048,2048]{2,1,0:T(8,128)(2,1)S(1)}, bf16[512,2048]{1,0:T(8,128)(2,1)}, f32[1,1]{1,0:T(1,128)}, f32[1,384]{1,0:T(1,128)}, f32[512,384]{1,0:...) custom-call(s32[2]{0:T(128)} %copy-done.44, ...), custom_call_target="tpu_custom_call", output_to_operand_aliasing={{0}: (12, {})} | custom-call | tf_op jit(solution)/shard_map/decoder/pallas_call | solution.py:630
  478.4 38.6 %backward_steps.5 = (bf16[8,16,2048]{2,1,0:T(8,128)(2,1)}, bf16[8,16,2048]{2,1,0:T(8,128)(2,1)}, bf16[8,16,2048]{2,1,0:T(8,128)(2,1)}, bf16[8,16,2048]{2,1,0:T(8...) custom-call(s32[2]{0:T(128)} %copy-done.44, s32[16,1]{1,0:T(8,128)} %copy-done.42, ...), custom_call_target="tpu_custom_call" | custom-call | bytes 134217728 | tf_op jit(solution)/shard_map/backward_steps/pallas_call | solution.py:549
  522.2 38.7 %backward_steps.6 = (bf16[8,16,2048]{2,1,0:T(8,128)(2,1)}, bf16[8,16,2048]{2,1,0:T(8,128)(2,1)}, bf16[8,16,2048]{2,1,0:T(8,128)(2,1)}, bf16[8,16,2048]{2,1,0:T(8...) custom-call(s32[2]{0:T(128)} %copy-done.44, s32[16,1]{1,0:T(8,128)} %copy-done.42, ...), custom_call_target="tpu_custom_call" | custom-call | bytes 134217728 | tf_op jit(solution)/shard_map/backward_steps/pallas_call | solution.py:549
  568.5 38.9 %backward_steps.7 = (bf16[8,16,2048]{2,1,0:T(8,128)(2,1)}, bf16[8,16,2048]{2,1,0:T(8,128)(2,1)}, bf16[8,16,2048]{2,1,0:T(8,128)(2,1)}, bf16[8,16,2048]{2,1,0:T(8...) custom-call(s32[2]{0:T(128)} %copy-done.44, s32[16,1]{1,0:T(8,128)} %copy-done.42, ...), custom_call_target="tpu_custom_call" | custom-call | bytes 134217728 | tf_op jit(solution)/shard_map/backward_steps/pallas_call | solution.py:549
  608.5 13.2 %collective-permute-done.44.refs_6_ = bf16[8,16,2048]{2,1,0:T(8,128)(2,1)S(1)} collective-permute-done((bf16[8,16,2048]{2,1,0:T(8,128)(2,1)}, bf16[8,16,2048]{2,1,0:T(8,128)(2,1)S(1)}, u32[]{:S(2)}, u32[]{:S(2)}) %collective-permute-start.44) | collective-permute-done | bytes 524320 | tf_op jit(solution)/shard_map/ppermute | solution.py:63
  624.9 24.9 %backward_steps.8 = (bf16[5,16,2048]{2,1,0:T(8,128)(2,1)}, bf16[5,16,2048]{2,1,0:T(8,128)(2,1)}, bf16[5,16,2048]{2,1,0:T(8,128)(2,1)}, bf16[5,16,2048]{2,1,0:T(8...) custom-call(s32[2]{0:T(128)} %copy-done.44, s32[16,1]{1,0:T(8,128)} %copy-done.42, ...), custom_call_target="tpu_custom_call" | custom-call | bytes 83886080 | tf_op jit(solution)/shard_map/backward_steps/pallas_call | solution.py:549
  653.1 16.1 %backward_steps.9 = (bf16[3,16,2048]{2,1,0:T(8,128)(2,1)}, bf16[3,16,2048]{2,1,0:T(8,128)(2,1)}, bf16[3,16,2048]{2,1,0:T(8,128)(2,1)}, bf16[3,16,2048]{2,1,0:T(8...) custom-call(s32[2]{0:T(128)} %copy-done.44, s32[16,1]{1,0:T(8,128)} %copy-done.42, ...), custom_call_target="tpu_custom_call" | custom-call | bytes 50331648 | tf_op jit(solution)/shard_map/backward_steps/pallas_call | solution.py:549
  669.2 9.9 %collective-permute-start.50 = (bf16[3,16,2048]{2,1,0:T(8,128)(2,1)}, bf16[3,16,2048]{2,1,0:T(8,128)(2,1)S(1)}, u32[]{:S(2)}, u32[]{:S(2)}) collective-permute-start(bf16[3,16,2048]{2,1,0:T(8,128)(2,1)} %get-tuple-element.214), channel_id=1, source_target_pairs={{0,1},{1,0},{2,3},{3,2},{4,5},{5,4},{6,7},{7,6},{8,9},{9,8},{10,11... | collective-permute-start | bytes 589832 | tf_op jit(solution)/shard_map/ppermute | solution.py:63
  697.6 25.8 %weight_gradient.3 = (f32[128,2048]{1,0:T(8,128)}, f32[384,128]{1,0:T(8,128)S(1)}, f32[2048,2048]{1,0:T(8,128)S(1)}) custom-call(s32[2]{0:T(128)S(1)} %copy-done.45, bf16[128,2048]{1,0:T(8,128)(2,1)} %bitcast.213, bf16[128,2048]{1,0:T(8,128)(2,1)} %bitcast.207, bf16[2,128,2048]{2,1,0:T(8,128)(2,1)} %bitcast.234, bf16[2,128,2048]{2,1,0:T(8,128)(2,1)} %bitcast.238, ...), custom_call_target="tpu_custom_call" | custom-call | tf_op jit(solution)/shard_map/weight_gradient/pallas_call | solution.py:789
  725.3 12.3 %weight_gradient.5 = bf16[4,256,2048]{2,1,0:T(8,128)(2,1)} custom-call(s32[2]{0:T(128)S(1)} %copy-done.45, bf16[128,2048]{1,0:T(8,128)(2,1)} %bitcast.198, bf16[128,2048]{1,0:T(8,128)(2,1)} %bitcast.193, bf16[2,128,2048]{2,1,0:T(8,128)(2,1)} %bitcast.59.refs_3_.refs_5_.refs_9_.refs_11_, bf16[2,128,2048]{2,1,0:T(8,128)(2,1)} %bitcast.219, ...), custom_call_target="tpu_custom_call" | custom-call | tf_op jit(solution)/shard_map/weight_gradient/pallas_call | solution.py:789
  754.9 10.4 %weight_gradient.4 = (f32[128,2048]{1,0:T(8,128)}, f32[384,128]{1,0:T(8,128)S(1)}, f32[4,256,2048]{2,1,0:T(8,128)}) custom-call(s32[2]{0:T(128)S(1)} %copy-done.45, bf16[128,2048]{1,0:T(8,128)(2,1)} %bitcast.200, bf16[128,2048]{1,0:T(8,128)(2,1)} %bitcast.195, bf16[2,128,2048]{2,1,0:T(8,128)(2,1)} %bitcast.59.refs_3_.refs_5_.refs_9_.refs_11_, ...), custom_call_target="tpu_custom_call" | custom-call | tf_op jit(solution)/shard_map/weight_gradient/pallas_call | solution.py:789
  842.1 22.1 %collective-permute-done.67 = bf16[28,2048]{1,0:T(8,128)(2,1)S(1)} collective-permute-done((bf16[28,2048]{1,0:T(8,128)(2,1)S(1)}, bf16[28,2048]{1,0:T(8,128)(2,1)S(1)}, u32[]{:S(2)}, u32[]{:S(2)}) %collective-permute-start.67) | collective-permute-done | bytes 114720 | tf_op jit(solution)/shard_map/ppermute | solution.py:53
  (485 shorter events, 313.8 us)
Async XLA Ops:
  124.0 61.2 %collective-permute-start.15 = (bf16[8,128,2048]{2,1,0:T(8,128)(2,1)}, bf16[8,128,2048]{2,1,0:T(8,128)(2,1)}, u32[]{:S(2)}, u32[]{:S(2)}) collective-permute-start(bf16[8,128,2048]{2,1,0:T(8,128)(2,1)} %copy-done.49), channel_id=1, source_target_pairs={{0,4},{4,0},{8,12},{12,8},{16,20},{20,16},{24,28},{28,24},{1,5},{5... | collective-permute-start | bytes 12582920 | tf_op jit(solution)/shard_map/ppermute | solution.py:53
  242.1 42.3 %collective-permute-start.23 = (bf16[8,16,2048]{2,1,0:T(8,128)(2,1)}, bf16[8,16,2048]{2,1,0:T(8,128)(2,1)S(1)}, u32[]{:S(2)}, u32[]{:S(2)}) collective-permute-start(bf16[8,16,2048]{2,1,0:T(8,128)(2,1)} %get-tuple-element.153.refs_0_), channel_id=1, source_target_pairs={{0,1},{1,0},{2,3},{3,2},{4,5},{5,4},{6,7},{7,6},{8,9},{9,8},{10,11... | collective-permute-start | bytes 1572872 | tf_op jit(solution)/shard_map/ppermute | solution.py:63
  282.3 104.6 %collective-permute-start.26 = (bf16[8,16,2048]{2,1,0:T(8,128)(2,1)}, bf16[8,16,2048]{2,1,0:T(8,128)(2,1)S(1)}, u32[]{:S(2)}, u32[]{:S(2)}) collective-permute-start(bf16[8,16,2048]{2,1,0:T(8,128)(2,1)} %get-tuple-element.156.refs_4_), channel_id=1, source_target_pairs={{0,1},{1,0},{2,3},{3,2},{4,5},{5,4},{6,7},{7,6},{8,9},{9,8},{10,11... | collective-permute-start | bytes 1572872 | tf_op jit(solution)/shard_map/ppermute | solution.py:63
  285.0 115.4 %collective-permute-start.24 = (bf16[2,8,16,2048]{3,2,1,0:T(8,128)(2,1)S(1)}, bf16[2,8,16,2048]{3,2,1,0:T(8,128)(2,1)}, u32[]{:S(2)}, u32[]{:S(2)}) collective-permute-start(bf16[2,8,16,2048]{3,2,1,0:T(8,128)(2,1)S(1)} %assemble.16), channel_id=1, source_target_pairs={{1,2},{2,1},{5,6},{6,5},{9,10},{10,9},{13,14},{14,13},{17,18},{18,... | collective-permute-start | bytes 3145736 | tf_op jit(solution)/shard_map/ppermute | solution.py:1073
  287.5 50.2 %collective-permute-start.30 = (bf16[512,384]{1,0:T(8,128)(2,1)S(1)}, bf16[512,384]{1,0:T(8,128)(2,1)S(1)}, u32[]{:S(2)}, u32[]{:S(2)}) collective-permute-start(bf16[512,384]{1,0:T(8,128)(2,1)S(1)} %copy-done.30), channel_id=1, source_target_pairs={{0,2},{1,3},{2,0},{3,1},{4,6},{5,7},{6,4},{7,5},{8,10},{9,11},{10,... | collective-permute-start | bytes 1179656 | tf_op jit(solution)/shard_map/ppermute | solution.py:63
  288.6 49.1 %collective-permute-start.31 = (bf16[512,384]{1,0:T(8,128)(2,1)S(1)}, bf16[512,384]{1,0:T(8,128)(2,1)S(1)}, u32[]{:S(2)}, u32[]{:S(2)}) collective-permute-start(bf16[512,384]{1,0:T(8,128)(2,1)S(1)} %copy-done.30), channel_id=1, source_target_pairs={{0,3},{1,2},{2,1},{3,0},{4,7},{5,6},{6,5},{7,4},{8,11},{9,10},{10,... | collective-permute-start | bytes 1179656 | tf_op jit(solution)/shard_map/ppermute | solution.py:63
  388.5 56.1 %collective-permute-start.27 = (bf16[2,8,16,2048]{3,2,1,0:T(8,128)(2,1)}, bf16[2,8,16,2048]{3,2,1,0:T(8,128)(2,1)}, u32[]{:S(2)}, u32[]{:S(2)}) collective-permute-start(bf16[2,8,16,2048]{3,2,1,0:T(8,128)(2,1)} %assemble.17), channel_id=1, source_target_pairs={{1,2},{2,1},{5,6},{6,5},{9,10},{10,9},{13,14},{14,13},{17,18},{18,... | collective-permute-start | bytes 3145736 | tf_op jit(solution)/shard_map/ppermute | solution.py:1073
  398.8 77.3 %collective-permute-start.33 = (bf16[2,8,16,2048]{3,2,1,0:T(8,128)(2,1)S(1)}, bf16[2,8,16,2048]{3,2,1,0:T(8,128)(2,1)}, u32[]{:S(2)}, u32[]{:S(2)}) collective-permute-start(bf16[2,8,16,2048]{3,2,1,0:T(8,128)(2,1)S(1)} %assemble.18), channel_id=1, source_target_pairs={{1,2},{2,1},{5,6},{6,5},{9,10},{10,9},{13,14},{14,13},{17,18},{18,... | collective-permute-start | bytes 3145736 | tf_op jit(solution)/shard_map/ppermute | solution.py:1073
  400.4 76.9 %collective-permute-start.25 = (bf16[2,8,16,2048]{3,2,1,0:T(8,128)(2,1)}, bf16[2,8,16,2048]{3,2,1,0:T(8,128)(2,1)S(1)}, u32[]{:S(2)}, u32[]{:S(2)}) collective-permute-start(bf16[2,8,16,2048]{3,2,1,0:T(8,128)(2,1)} %collective-permute-done.24.refs_6_.refs_2_), channel_id=1, source_target_pairs={{1,0},{2,3},{5,4},{6,7},{9,8},{10,11},{13,12},{14,15},{17,16},{18,... | collective-permute-start | bytes 3145736 | tf_op jit(solution)/shard_map/ppermute | solution.py:1075
  444.6 76.1 %collective-permute-start.28 = (bf16[2,8,16,2048]{3,2,1,0:T(8,128)(2,1)}, bf16[2,8,16,2048]{3,2,1,0:T(8,128)(2,1)S(1)}, u32[]{:S(2)}, u32[]{:S(2)}) collective-permute-start(bf16[2,8,16,2048]{3,2,1,0:T(8,128)(2,1)} %collective-permute-done.27.refs_7_.refs_6_), channel_id=1, source_target_pairs={{1,0},{2,3},{5,4},{6,7},{9,8},{10,11},{13,12},{14,15},{17,16},{18,... | collective-permute-start | bytes 3145736 | tf_op jit(solution)/shard_map/ppermute | solution.py:1075
  459.5 101.5 %collective-permute-start.36 = (bf16[2,8,16,2048]{3,2,1,0:T(8,128)(2,1)S(1)}, bf16[2,8,16,2048]{3,2,1,0:T(8,128)(2,1)S(1)}, u32[]{:S(2)}, u32[]{:S(2)}) collective-permute-start(bf16[2,8,16,2048]{3,2,1,0:T(8,128)(2,1)S(1)} %assemble.19), channel_id=1, source_target_pairs={{1,2},{2,1},{5,6},{6,5},{9,10},{10,9},{13,14},{14,13},{17,18},{18,... | collective-permute-start | bytes 3145736 | tf_op jit(solution)/shard_map/ppermute | solution.py:1073
  476.1 91.4 %collective-permute-start.34 = (bf16[2,8,16,2048]{3,2,1,0:T(8,128)(2,1)}, bf16[2,8,16,2048]{3,2,1,0:T(8,128)(2,1)S(1)}, u32[]{:S(2)}, u32[]{:S(2)}) collective-permute-start(bf16[2,8,16,2048]{3,2,1,0:T(8,128)(2,1)} %collective-permute-done.33.refs_7_.refs_10_), channel_id=1, source_target_pairs={{1,0},{2,3},{5,4},{6,7},{9,8},{10,11},{13,12},{14,15},{17,16},{18,... | collective-permute-start | bytes 3145736 | tf_op jit(solution)/shard_map/ppermute | solution.py:1075
  517.0 45.3 %collective-permute-start.38 = (bf16[8,16,2048]{2,1,0:T(8,128)(2,1)}, bf16[8,16,2048]{2,1,0:T(8,128)(2,1)S(1)}, u32[]{:S(2)}, u32[]{:S(2)}) collective-permute-start(bf16[8,16,2048]{2,1,0:T(8,128)(2,1)} %get-tuple-element.183), channel_id=1, source_target_pairs={{0,1},{1,0},{2,3},{3,2},{4,5},{5,4},{6,7},{7,6},{8,9},{9,8},{10,11... | collective-permute-start | bytes 1572872 | tf_op jit(solution)/shard_map/ppermute | solution.py:63
  519.7 45.3 %collective-permute-start.39 = (bf16[8,16,2048]{2,1,0:T(8,128)(2,1)}, bf16[8,16,2048]{2,1,0:T(8,128)(2,1)}, u32[]{:S(2)}, u32[]{:S(2)}) collective-permute-start(bf16[8,16,2048]{2,1,0:T(8,128)(2,1)} %get-tuple-element.184), channel_id=1, source_target_pairs={{0,2},{1,3},{2,0},{3,1},{4,6},{5,7},{6,4},{7,5},{8,10},{9,11},{10,... | collective-permute-start | bytes 1572872 | tf_op jit(solution)/shard_map/ppermute | solution.py:63
  520.7 45.3 %collective-permute-start.40 = (bf16[8,16,2048]{2,1,0:T(8,128)(2,1)}, bf16[8,16,2048]{2,1,0:T(8,128)(2,1)}, u32[]{:S(2)}, u32[]{:S(2)}) collective-permute-start(bf16[8,16,2048]{2,1,0:T(8,128)(2,1)} %get-tuple-element.185), channel_id=1, source_target_pairs={{0,3},{1,2},{2,1},{3,0},{4,7},{5,6},{6,5},{7,4},{8,11},{9,10},{10,... | collective-permute-start | bytes 1572872 | tf_op jit(solution)/shard_map/ppermute | solution.py:63
  561.0 62.8 %collective-permute-start.37 = (bf16[2,8,16,2048]{3,2,1,0:T(8,128)(2,1)S(1)}, bf16[2,8,16,2048]{3,2,1,0:T(8,128)(2,1)S(1)}, u32[]{:S(2)}, u32[]{:S(2)}) collective-permute-start(bf16[2,8,16,2048]{3,2,1,0:T(8,128)(2,1)S(1)} %collective-permute-done.36.refs_10_.refs_14_), channel_id=1, source_target_pairs={{1,0},{2,3},{5,4},{6,7},{9,8},{10,11},{13,12},{14,15},{17,16},{18,... | collective-permute-start | bytes 3145736 | tf_op jit(solution)/shard_map/ppermute | solution.py:1075
  562.3 59.4 %collective-permute-start.44 = (bf16[8,16,2048]{2,1,0:T(8,128)(2,1)}, bf16[8,16,2048]{2,1,0:T(8,128)(2,1)S(1)}, u32[]{:S(2)}, u32[]{:S(2)}) collective-permute-start(bf16[8,16,2048]{2,1,0:T(8,128)(2,1)} %get-tuple-element.195), channel_id=1, source_target_pairs={{0,1},{1,0},{2,3},{3,2},{4,5},{5,4},{6,7},{7,6},{8,9},{9,8},{10,11... | collective-permute-start | bytes 1572872 | tf_op jit(solution)/shard_map/ppermute | solution.py:63
  565.1 56.7 %collective-permute-start.45 = (bf16[8,16,2048]{2,1,0:T(8,128)(2,1)}, bf16[8,16,2048]{2,1,0:T(8,128)(2,1)S(1)}, u32[]{:S(2)}, u32[]{:S(2)}) collective-permute-start(bf16[8,16,2048]{2,1,0:T(8,128)(2,1)} %get-tuple-element.196), channel_id=1, source_target_pairs={{0,2},{1,3},{2,0},{3,1},{4,6},{5,7},{6,4},{7,5},{8,10},{9,11},{10,... | collective-permute-start | bytes 1572872 | tf_op jit(solution)/shard_map/ppermute | solution.py:63
  566.0 57.7 %collective-permute-start.46 = (bf16[8,16,2048]{2,1,0:T(8,128)(2,1)}, bf16[8,16,2048]{2,1,0:T(8,128)(2,1)S(1)}, u32[]{:S(2)}, u32[]{:S(2)}) collective-permute-start(bf16[8,16,2048]{2,1,0:T(8,128)(2,1)} %get-tuple-element.197), channel_id=1, source_target_pairs={{0,3},{1,2},{2,1},{3,0},{4,7},{5,6},{6,5},{7,4},{8,11},{9,10},{10,... | collective-permute-start | bytes 1572872 | tf_op jit(solution)/shard_map/ppermute | solution.py:63
  607.4 42.4 %collective-permute-start.41 = (bf16[8,16,2048]{2,1,0:T(8,128)(2,1)}, bf16[8,16,2048]{2,1,0:T(8,128)(2,1)S(1)}, u32[]{:S(2)}, u32[]{:S(2)}) collective-permute-start(bf16[8,16,2048]{2,1,0:T(8,128)(2,1)} %get-tuple-element.192), channel_id=1, source_target_pairs={{0,1},{1,0},{2,3},{3,2},{4,5},{5,4},{6,7},{7,6},{8,9},{9,8},{10,11... | collective-permute-start | bytes 1572872 | tf_op jit(solution)/shard_map/ppermute | solution.py:63
  679.1 44.7 %collective-permute-start.47 = (bf16[5,16,2048]{2,1,0:T(8,128)(2,1)}, bf16[5,16,2048]{2,1,0:T(8,128)(2,1)S(1)}, u32[]{:S(2)}, u32[]{:S(2)}) collective-permute-start(bf16[5,16,2048]{2,1,0:T(8,128)(2,1)} %get-tuple-element.210), channel_id=1, source_target_pairs={{0,1},{1,0},{2,3},{3,2},{4,5},{5,4},{6,7},{7,6},{8,9},{9,8},{10,11... | collective-permute-start | bytes 983048 | tf_op jit(solution)/shard_map/ppermute | solution.py:63
  679.2 44.7 %collective-permute-start.48 = (bf16[5,16,2048]{2,1,0:T(8,128)(2,1)}, bf16[5,16,2048]{2,1,0:T(8,128)(2,1)S(1)}, u32[]{:S(2)}, u32[]{:S(2)}) collective-permute-start(bf16[5,16,2048]{2,1,0:T(8,128)(2,1)} %get-tuple-element.211), channel_id=1, source_target_pairs={{0,2},{1,3},{2,0},{3,1},{4,6},{5,7},{6,4},{7,5},{8,10},{9,11},{10,... | collective-permute-start | bytes 983048 | tf_op jit(solution)/shard_map/ppermute | solution.py:63
  681.6 42.3 %collective-permute-start.49 = (bf16[5,16,2048]{2,1,0:T(8,128)(2,1)S(1)}, bf16[5,16,2048]{2,1,0:T(8,128)(2,1)S(1)}, u32[]{:S(2)}, u32[]{:S(2)}) collective-permute-start(bf16[5,16,2048]{2,1,0:T(8,128)(2,1)S(1)} %copy-done.113), channel_id=1, source_target_pairs={{0,3},{1,2},{2,1},{3,0},{4,7},{5,6},{6,5},{7,4},{8,11},{9,10},{10,... | collective-permute-start | bytes 983048 | tf_op jit(solution)/shard_map/ppermute | solution.py:63
  737.7 93.9 %collective-permute-start.70 = (bf16[4,256,2048]{2,1,0:T(8,128)(2,1)}, bf16[4,256,2048]{2,1,0:T(8,128)(2,1)}, u32[]{:S(2)}, u32[]{:S(2)}) collective-permute-start(bf16[4,256,2048]{2,1,0:T(8,128)(2,1)} %weight_gradient.5), channel_id=1, source_target_pairs={{0,4},{4,0},{8,12},{12,8},{16,20},{20,16},{24,28},{28,24},{1,5},{5... | collective-permute-start | bytes 12582920 | tf_op jit(solution)/shard_map/ppermute | solution.py:53
  (167 other events, 3388.7 us)

commit v2 on v1

--- a/solution.py
+++ b/solution.py
@@ -12,14 +12,14 @@
 F32 = jnp.float32
 LANES = 128
 ID_BASE = 16
+EXTRA_ROWS = 8
 MIB = 2**20
 STEP_VMEM = 26 * MIB
 BACK_VMEM = 26 * MIB
 LOAD_VMEM = 4 * MIB
 ASSEMBLE_VMEM = 16 * MIB
-FORWARD_CHUNKS = (8, 8, 8, 8)
-BACKWARD_CHUNKS = (8, 8, 8, 5, 3)
-LAST_CHUNKS = 2
+FORWARD_CHUNKS = (9, 9, 7, 7)
+BACKWARD_CHUNKS = (7, 7, 9, 6, 3)
 ANYWHERE = pl.BlockSpec(memory_space=pl.ANY)
 IN_VMEM = pl.BlockSpec(memory_space=pltpu.VMEM)
 IN_SMEM = pl.BlockSpec(memory_space=pltpu.SMEM)
@@ -85,6 +85,7 @@
         out_specs=[ANYWHERE] * len(values),
         out_shape=[in_hbm(v.shape, v.dtype) for v in values],
         input_output_aliases={i: i for i in range(len(values))},
+        compiler_params=pltpu.CompilerParams(vmem_limit_bytes=MIB),
         cost_estimate=LITTLE,
         name="hold",
     )(*[keep_far(v) for v in values], *ties)
@@ -128,12 +129,14 @@
             entry.append(tuple(row))
         plan.append(tuple(entry))
     shape, dtype = sources[0].shape[1:], sources[0].dtype
+    total = len(sources) + sum(len(blocks) for blocks in outs)
+    vmem = min(ASSEMBLE_VMEM, MIB + total * math.prod(shape) * 4)
     return pl.pallas_call(
         functools.partial(assemble_kernel, tuple(plan), len(sources), len(ties)),
         in_specs=[IN_SMEM] + [IN_VMEM] * len(sources) + [ANYWHERE] * len(ties),
         out_specs=[IN_VMEM] * len(plan),
         out_shape=[jax.ShapeDtypeStruct((len(blocks),) + shape, dtype) for blocks in plan],
-        compiler_params=pltpu.CompilerParams(vmem_limit_bytes=ASSEMBLE_VMEM),
+        compiler_params=pltpu.CompilerParams(vmem_limit_bytes=vmem),
         cost_estimate=LITTLE,
         name="assemble",
     )(where, *sources, *ties)
@@ -573,16 +576,66 @@
     )
 
 
-def decoder_kernel(chunks, units, scale, vocab, *refs):
+def decoder_rows(vocab, units):
+    return -(-vocab // (units * 16)) * 16
+
+
+def pack_decoder(decoder, units):
+    unit_width, vocab = decoder.shape
+    rows = decoder_rows(vocab, units)
+    turned = jnp.pad(decoder.T, ((0, rows * units - vocab), (0, 0)))
+    turned = turned.reshape(units, rows, unit_width).transpose(1, 0, 2)
+    return turned.reshape(rows, units * unit_width)
+
+
+def join_rows_kernel(count, *refs):
+    out = refs[-1]
+    first = 0
+    for source in refs[:count]:
+        rows = source.shape[0]
+        out[first : first + rows, :] = source[...]
+        first += rows
+
+
+def join_rows(arrays, ties=()):
+    rows = sum(a.shape[0] for a in arrays)
+    return pl.pallas_call(
+        functools.partial(join_rows_kernel, len(arrays)),
+        in_specs=[IN_VMEM] * len(arrays) + [ANYWHERE] * len(ties),
+        out_specs=IN_VMEM,
+        out_shape=jax.ShapeDtypeStruct((rows, arrays[0].shape[1]), arrays[0].dtype),
+        compiler_params=pltpu.CompilerParams(vmem_limit_bytes=6 * MIB),
+        cost_estimate=LITTLE,
+        name="join_rows",
+    )(*arrays, *ties)
+
+
+SOURCES = ((0,), (1,), (3, 4), (2, 5))
+
+
+def is_outer(z):
+    return jnp.logical_or(z == 0, z == 3)
+
+
+def wait_or_start(method, copies, pairs, outer):
+    for copy in copies:
+        getattr(copy, method)()
+    for inner_copy, outer_copy in pairs:
+        pl.when(outer)(getattr(outer_copy, method))
+        pl.when(jnp.logical_not(outer))(getattr(inner_copy, method))
+
+
+def decoder_kernel(chunks, first_row, scale, vocab, square, *refs):
     where, bias, targets, alive = refs[:4]
     lows = refs[4 : 4 + chunks]
     refs = refs[4 + chunks :]
-    arrived, refs = refs[:units], refs[units:]
-    turned, back, loss, bias_grad = refs[1:5]
-    parts, (low, decoder, sems) = refs[5:-3], refs[-3:]
-    unit_width = parts[0].shape[0]
-    me_z = where[1]
-    copies = []
+    sources = refs[:6]
+    turned, back, extras, sent, kept, low, decoder, sems, decoder_sems = refs[7:]
+    units, hidden_width, _ = turned.shape
+    unit_width = hidden_width // units
+    me_r, me_z = where[0], where[1]
+    outer = is_outer(me_z)
+    copies, pairs = [], []
     first = 0
     for number, chunk in enumerate(lows):
         count = chunk.shape[0]
@@ -590,17 +643,31 @@
             pltpu.make_async_copy(chunk, low.at[pl.ds(first, count)], sems.at[number])
         )
         first += count
+    rows = decoder_rows(vocab, units)
     for bits in range(units):
-        first = jnp.bitwise_xor(me_z, bits) * unit_width
-        to = decoder.at[pl.ds(pl.multiple_of(first, unit_width), unit_width)]
-        copies.append(pltpu.make_async_copy(arrived[bits], to, sems.at[chunks + bits]))
-    for copy in copies:
-        copy.start()
+        z = jnp.bitwise_xor(me_z, bits)
+        to = pl.ds(pl.multiple_of(z * unit_width, unit_width), unit_width)
+        for part in range(units):
+
+            def copy(source):
+                source = source.at[
+                    pl.ds(first_row, rows), pl.ds(part * unit_width, unit_width)
+                ]
+                return pltpu.make_async_copy(
+                    source, decoder.at[pl.ds(part * rows, rows), to], decoder_sems.at[bits, part]
+                )
+
+            by_place = SOURCES[bits]
+            if len(by_place) == 1:
+                copies.append(copy(sources[by_place[0]]))
+            else:
+                pairs.append([copy(sources[place]) for place in by_place])
+    wait_or_start("start", copies, pairs, outer)
+    decoder[units * rows :, :] = jnp.zeros_like(decoder[units * rows :, :])
     turn_blocks(turned)
-    for copy in copies:
-        copy.wait()
+    wait_or_start("wait", copies, pairs, outer)
     weights = decoder[...]
-    logits = jnp.dot(low[...], weights, preferred_element_type=F32) + bias[...]
+    logits = contract(low[...], weights, 1, 1) + bias[...]
     column = lax.broadcasted_iota(jnp.int32, logits.shape, 1)
     real = column < vocab
     maximum = jnp.max(jnp.where(real, logits, -jnp.inf), axis=1, keepdims=True)
@@ -609,43 +676,60 @@
     probable = jnp.where(real, jnp.exp(logits - log_total), 0.0)
     hit = column == targets[...]
     picked = jnp.sum(jnp.where(hit, logits, 0.0), axis=1, keepdims=True)
-    loss[...] = jnp.sum((log_total - picked) * alive[...], axis=0, keepdims=True) * scale
+    loss = jnp.sum((log_total - picked) * alive[...], axis=0, keepdims=True) * scale
     dlogits = (probable - hit.astype(F32)) * (alive[...] * scale)
     dlogits = dlogits.astype(BF16)
-    bias_grad[...] = jnp.sum(dlogits.astype(F32), axis=0, keepdims=True)
-    back[...] = contract(dlogits, weights, 1, 1).astype(BF16)
-    for bits in range(units):
-        z = jnp.bitwise_xor(me_z, bits)
-        at = pl.ds(pl.multiple_of(z * unit_width, unit_width), unit_width)
-        parts[bits][...] = contract(low[:, at], dlogits, 0, 0).astype(parts[bits].dtype)
-
-
-def run_decoder(where, pieces, bias, targets, alive, lows, scale, vocab, weight):
-    units = len(pieces)
-    hidden_width = lows[0].shape[1]
+    bias_grad = jnp.sum(dlogits.astype(F32), axis=0, keepdims=True)
+    parts = bias_grad.shape[1] // LANES
+    for part in range(parts):
+        extras[part : part + 1, :] = bias_grad[:, part * LANES : (part + 1) * LANES]
+    extras[parts:, :] = jnp.broadcast_to(loss, (extras.shape[0] - parts, LANES))
+    back[...] = jnp.dot(dlogits, weights, preferred_element_type=F32).astype(BF16)
+    if not square:
+        kept[...] = contract(low[...], dlogits, 0, 0)
+        return
+    tile = kept.shape[2]
+    for dc, out in ((1, sent), (0, kept)):
+        for dy in range(2):
+            for dx in range(2):
+                to = jnp.bitwise_xor(me_r, dy * 4 + dx * 2 + dc)
+                at = pl.ds(pl.multiple_of(to * tile, tile), tile)
+                part = contract(dlogits, low[:, at], 0, 0)
+                out[dy * 2 + dx] = part[: kept.shape[1], :].astype(out.dtype)
+
+
+def run_decoder(
+    where, pieces, first_row, bias, targets, alive, lows, scale, vocab, weight, rows_dev, square
+):
+    units, hidden_width, _ = weight.shape
     padded = bias.shape[1]
     local = targets.shape[0]
-    unit_width = hidden_width // units
     chunks = len(lows)
+    turned_rows = -(-vocab // 16) * 16
+    parts = [
+        in_hbm((4, turned_rows, rows_dev), BF16),
+        in_hbm((4, turned_rows, rows_dev), F32),
+    ]
+    if not square:
+        parts = [in_hbm((8, LANES), F32), in_hbm((hidden_width, padded), F32)]
     return pl.pallas_call(
-        functools.partial(decoder_kernel, chunks, units, scale, vocab),
-        in_specs=[IN_SMEM] + [IN_VMEM] * 3 + [ANYWHERE] * (chunks + units) + [IN_VMEM],
-        out_specs=[IN_VMEM] * (4 + units),
+        functools.partial(decoder_kernel, chunks, first_row, scale, vocab, square),
+        in_specs=[IN_SMEM] + [IN_VMEM] * 3 + [ANYWHERE] * (chunks + 6) + [IN_VMEM],
+        out_specs=[IN_VMEM] * 5,
         out_shape=[
             pltpu.VMEM(weight.shape, BF16),
             in_hbm((local, hidden_width), BF16),
-            in_hbm((1, 1), F32),
-            in_hbm((1, padded), F32),
-            in_hbm((unit_width, padded), F32),
+            in_hbm((8, LANES), F32),
         ]
-        + [in_hbm((unit_width, padded), BF16)] * (units - 1),
+        + parts,
         scratch_shapes=[
             pltpu.VMEM((local, hidden_width), BF16),
-            pltpu.VMEM((hidden_width, padded), BF16),
-            pltpu.SemaphoreType.DMA((chunks + len(pieces),)),
+            pltpu.VMEM((padded, hidden_width), BF16),
+            pltpu.SemaphoreType.DMA((chunks,)),
+            pltpu.SemaphoreType.DMA((units, units)),
         ],
         compiler_params=pltpu.CompilerParams(vmem_limit_bytes=STEP_VMEM),
-        input_output_aliases={4 + chunks + units: 0},
+        input_output_aliases={10 + chunks: 0},
         name="decoder",
     )(
         where, bias, targets, alive, *[keep_far(v) for v in lows],
@@ -653,153 +737,272 @@
     )
 
 
-def grow_kernel(spec, mode, sizes, *refs):
-    refs = list(refs)
-    where = refs.pop(0)
-    arrays = [[refs.pop(0) for _ in range(count)] for count, _, _, _, _ in spec]
-    dpres = [refs.pop(0) for _ in spec]
-    column_sems, dpre_sems, column, dpre = refs[-4:]
-    refs = refs[:-4]
-    outer = jnp.logical_or(where[1] == 0, where[1] == 3)
-    copies, pairs = [], []
-    first = 0
-    for number, (count, row, rows, _, parts) in enumerate(spec):
-        at = pl.ds(first, rows)
-        options = []
-        for array, part in zip(arrays[number], parts):
-            source = array if part is None else array.at[part]
-            options.append(
-                pltpu.make_async_copy(
-                    source.at[pl.ds(row, rows)], column.at[at], column_sems.at[number]
-                )
-            )
-        if count == 1:
-            copies.append(options[0])
-        else:
-            pairs.append(options)
-        copies.append(pltpu.make_async_copy(dpres[number], dpre.at[at], dpre_sems.at[number]))
-        first += rows
-    for copy in copies:
-        copy.start()
-    for inner_copy, outer_copy in pairs:
-        pl.when(outer)(outer_copy.start)
-        pl.when(jnp.logical_not(outer))(inner_copy.start)
-    for copy in copies:
-        copy.wait()
-    for inner_copy, outer_copy in pairs:
-        pl.when(outer)(outer_copy.wait)
-        pl.when(jnp.logical_not(outer))(inner_copy.wait)
-    d = dpre[...]
-
-    if mode in ("first", "sum"):
-        if mode == "sum":
-            total_in, refs = refs[0], refs[1:]
-        total, refs = refs[-1], refs[:-1]
-        tile = 256
-
-        def block(index, carry):
-            at = pl.ds(pl.multiple_of(index * tile, tile), tile)
-            part = contract(column[:, at], d, 0, 0)
-            total[at, :] = part if mode == "first" else total_in[at, :] + part
-            return carry
-
-        lax.fori_loop(0, column.shape[1] // tile, block, 0)
+def add_kernel(halve, kept, moved, *refs):
+    outs = refs[-2:]
+    if halve:
+        send, keep = outs
+        count = kept.shape[0] // 2
+        for index in range(count):
+            send_at, keep_at = (2 * index + 1, 2 * index)
+            send[index] = (kept[send_at] + moved[send_at].astype(F32)).astype(BF16)
+            keep[index] = kept[keep_at] + moved[keep_at].astype(F32)
     else:
-        total_in, refs = refs[0], refs[1:]
-        out, refs = refs[-1], refs[:-1]
-        size_y, size_x, size_c = sizes
-        dc = 1 if mode == "other" else 0
-        me_r = where[0]
-        me_c = lax.rem(me_r, size_c)
-        me_x = lax.rem(lax.div(me_r, size_c), size_x)
-        me_y = lax.div(me_r, size_c * size_x)
-        tile = out.shape[1]
-
-        def block(index, carry):
-            dy = lax.div(index, size_x)
-            dx = lax.rem(index, size_x)
-            to = lax.rem(me_y + dy, size_y) * size_x + lax.rem(me_x + dx, size_x)
-            to = to * size_c + lax.rem(me_c + dc, size_c)
-            at = pl.ds(pl.multiple_of(to * tile, tile), tile)
-            part = contract(column[:, at], d, 0, 0) + total_in[at, :]
-            out[index] = part.astype(out.dtype)
-            return carry
-
-        lax.fori_loop(0, size_y * size_x, block, 0)
-    if mode == "other":
-        return
-
-    if mode == "first":
-        embedded, win, small, hot_sum = refs
+        total = kept[...] + moved[...].astype(F32)
+        outs[0][...] = total.astype(BF16)
+        outs[1][...] = total
+
+
+def add_parts(kept, moved, halve=False, ties=()):
+    shape = kept.shape
+    if halve:
+        shape = (shape[0] // 2,) + shape[1:]
+    return pl.pallas_call(
+        functools.partial(add_kernel, halve),
+        in_specs=[IN_VMEM] * 2 + [ANYWHERE] * len(ties),
+        out_specs=[IN_VMEM] * 2,
+        out_shape=[in_hbm(shape, BF16), in_hbm(shape, F32)],
+        compiler_params=pltpu.CompilerParams(vmem_limit_bytes=8 * MIB),
+        cost_estimate=LITTLE,
+        name="add_parts",
+    )(kept, moved, *ties)
+
+
+def sum_and_choose_kernel(axis, passed, where, mine, block, other, other_block, *refs):
+    total, out = refs[passed : passed + 2]
+    me_r, me_z = where[0], where[1]
+    if axis == 0:
+        stays = lax.div(me_r, 4) == lax.div(me_z, 2)
     else:
-        embedded, win, small_in, hot_in, small, hot_sum = refs
-    words = jnp.concatenate([embedded[e : e + n, :] for _, _, n, e, _ in spec], axis=0)
-    part = contract(words, d, 0, 0)
-    small[...] = part if mode == "first" else part + small_in[...]
-    back = contract(d, win[...], 1, 1)
+        stays = lax.rem(lax.div(me_r, 2), 2) == lax.rem(me_z, 2)
+
+    @pl.when(stays)
+    def _():
+        out[...] = block[...]
+
+    @pl.when(jnp.logical_not(stays))
+    def _():
+        out[...] = other_block[...]
+
+    total[...] = mine[...] + other[...]
+
+
+def sum_and_choose(where, axis, mine, block, other, other_block, passed):
+    count = len(passed)
+    out = pl.pallas_call(
+        functools.partial(sum_and_choose_kernel, axis, count),
+        in_specs=[IN_SMEM] + [IN_VMEM] * 4 + [ANYWHERE] * count,
+        out_specs=[IN_VMEM] * 2 + [ANYWHERE] * count,
+        out_shape=[
+            jax.ShapeDtypeStruct(mine.shape, F32),
+            jax.ShapeDtypeStruct(block.shape, BF16),
+        ]
+        + [jax.ShapeDtypeStruct(v.shape, v.dtype) for v in passed],
+        input_output_aliases={5 + i: 2 + i for i in range(count)},
+        compiler_params=pltpu.CompilerParams(vmem_limit_bytes=4 * MIB),
+        cost_estimate=LITTLE,
+        name="sum_and_choose",
+    )(where, mine, block, other, other_block, *passed)
+    return out[0], out[1], list(out[2:])
+
+
+def little_sums(words, d, win, rows):
+    small = contract(words, d, 0, 0)
+    back = contract(d, win, 1, 1)
     high = words[:, -2:-1].astype(F32)
     low = words[:, -1:].astype(F32)
     ids = (high * ID_BASE + low).astype(jnp.int32)
-    vocab = lax.broadcasted_iota(jnp.int32, (ids.shape[0], hot_sum.shape[0]), 1)
+    vocab = lax.broadcasted_iota(jnp.int32, (ids.shape[0], rows), 1)
     hot = (vocab == ids).astype(F32).astype(BF16)
-    part = None
+    total = None
     for _ in range(3):
         term = back.astype(BF16)
         back = back - term.astype(F32)
-        more = contract(hot, term, 0, 0)
-        part = more if part is None else part + more
-    hot_sum[...] = part if mode == "first" else part + hot_in[...]
-
-
-def run_grow(where, runs, embedded, win, totals, mode, sizes, rows_dev, vocab):
+        part = contract(hot, term, 0, 0)
+        total = part if total is None else total + part
+    return small, total
+
+
+def little_kernel(spec, ties, *refs):
+    dpres, refs = refs[: len(spec)], refs[len(spec) :]
+    embedded, win, extras = refs[:3]
+    small, hot_sum, dpre, sems = refs[3 + ties :]
+    copies = []
+    first = 0
+    for number, (rows, _) in enumerate(spec):
+        to = dpre.at[pl.ds(first, rows)]
+        copies.append(pltpu.make_async_copy(dpres[number], to, sems.at[number]))
+        first += rows
+    wait_or_start("start", copies, [], None)
+    wait_or_start("wait", copies, [], None)
+    words = jnp.concatenate([embedded[e : e + n, :] for n, e in spec], axis=0)
+    rows = hot_sum.shape[0] - EXTRA_ROWS
+    small[...], hot_sum[:rows, :] = little_sums(words, dpre[...], win[...], rows)
+    hot_sum[rows:, :] = extras[...]
+
+
+def run_little(runs, embedded, win, extras, vocab, ties):
+    spec = tuple((dpre.shape[0], word) for _, _, dpre, word in runs)
+    positions = sum(n for n, _ in spec)
+    block = win.shape[1]
+    padded = embedded.shape[1]
+    return pl.pallas_call(
+        functools.partial(little_kernel, spec, len(ties)),
+        in_specs=[ANYWHERE] * len(runs) + [IN_VMEM] * 3 + [ANYWHERE] * len(ties),
+        out_specs=[IN_VMEM] * 2,
+        out_shape=[in_hbm((padded, block), F32), in_hbm((vocab + EXTRA_ROWS, padded), F32)],
+        scratch_shapes=[
+            pltpu.VMEM((positions, block), BF16),
+            pltpu.SemaphoreType.DMA((len(runs),)),
+        ],
+        compiler_params=pltpu.CompilerParams(vmem_limit_bytes=24 * MIB),
+        cost_estimate=LITTLE,
+        name="little_gradients",
+    )(*[keep_far(run[2]) for run in runs], embedded, win, extras, *ties)
+
+
+def grow_kernel(spec, mode, sizes, blocks, early, *refs):
+    refs = list(refs)
+    where = refs.pop(0)
+    arrays = [[refs.pop(0) for _ in range(count)] for count, _, _, _ in spec]
+    dpres = [refs.pop(0) for _ in spec]
+    column, dpre, column_sems, dpre_sems = refs[-4:]
+    refs = refs[:-4]
+    out, refs = refs[-1], refs[:-1]
+    step = pl.program_id(0)
+    size_y, size_x, size_c = sizes
+    me_r = where[0]
+    me_c = lax.rem(me_r, size_c)
+    me_x = lax.rem(lax.div(me_r, size_c), size_x)
+    me_y = lax.div(me_r, size_c * size_x)
+    outer = is_outer(where[1])
+    tile = column.shape[2]
+
+    def place(index):
+        if mode == "sum":
+            return index
+        dy = lax.div(index, size_x)
+        dx = lax.rem(index, size_x)
+        dc = 1 if mode == "other" else 0
+        to = lax.rem(me_y + dy, size_y) * size_x + lax.rem(me_x + dx, size_x)
+        return to * size_c + lax.rem(me_c + dc, size_c)
+
+    def column_copies(method, index):
+        slot = lax.rem(index, 2)
+        lanes = pl.ds(pl.multiple_of(place(index) * tile, tile), tile)
+        copies, pairs = [], []
+        first = 0
+        for number, (count, row, rows, _) in enumerate(spec):
+            options = [
+                pltpu.make_async_copy(
+                    array.at[pl.ds(row, rows), lanes],
+                    column.at[slot, pl.ds(first, rows)],
+                    column_sems.at[slot, number],
+                )
+                for array in arrays[number]
+            ]
+            if count == 1:
+                copies.append(options[0])
+            else:
+                pairs.append(options)
+            first += rows
+        wait_or_start(method, copies, pairs, outer)
+
+    @pl.when(step == 0)
+    def _():
+        copies = []
+        first = 0
+        for number, (_, _, rows, _) in enumerate(spec):
+            at = pl.ds(first, rows)
+            copies.append(
+                pltpu.make_async_copy(dpres[number], dpre.at[at], dpre_sems.at[number])
+            )
+            first += rows
+        wait_or_start("start", copies, [], outer)
+        column_copies("start", step)
+        wait_or_start("wait", copies, [], outer)
+
+    @pl.when(step + 1 < blocks)
+    def _():
+        column_copies("start", step + 1)
+
+    if mode != "own":
+        embedded, win, small_in, hot_in = refs[:4]
+        small, hot_sum = refs[-2:]
+
+        @pl.when(step == 0)
+        def _():
+            words, first = [], 0
+            for _, _, rows, word in spec:
+                if first >= early:
+                    words.append(embedded[word : word + rows, :])
+                first += rows
+            words = jnp.concatenate(words, axis=0)
+            rows = hot_sum.shape[0] - EXTRA_ROWS
+            part, hot = little_sums(words, dpre[early:, :], win[...], rows)
+            small[...] = part + small_in[...]
+            hot_sum[:rows, :] = hot + hot_in[:rows, :]
+            hot_sum[rows:, :] = hot_in[rows:, :]
+    else:
+        small = refs[0]
+
+    column_copies("wait", step)
+    part = contract(column[lax.rem(step, 2)], dpre[...], 0, 0)
+    if mode == "sum":
+        out[...] = part
+    else:
+        small_tile = out.shape[1] - tile
+        small_at = pl.multiple_of(place(step) * small_tile, small_tile)
+        out[0, :tile, :] = part.astype(out.dtype)
+        out[0, tile:, :] = small[pl.ds(small_at, small_tile), :].astype(out.dtype)
+
+
+def run_grow(where, runs, early, embedded, win, little, mode, sizes, rows_dev):
     spec, arrays, dpres = [], [], []
     for choices, row, dpre, word in runs:
-        rows = dpre.shape[0]
-        spec.append((len(choices), row, rows, word, tuple(part for _, part in choices)))
-        arrays += [keep_far(array) for array, _ in choices]
+        spec.append((len(choices), row, dpre.shape[0], word))
+        arrays += [keep_far(array) for array in choices]
         dpres.append(keep_far(dpre))
-    positions = sum(n for _, _, n, _, _ in spec)
-    block, hidden_width = dpres[0].shape[1], runs[0][0][0][0].shape[-1]
+    positions = sum(n for _, _, n, _ in spec)
+    block, hidden_width = dpres[0].shape[1], runs[0][0][0].shape[-1]
     padded = embedded.shape[1]
     near = sizes[0] * sizes[1]
+    tile = 256 if mode == "sum" else rows_dev
+    blocks = hidden_width // tile if mode == "sum" else near
     operands = [where] + arrays + dpres
     specs = [IN_SMEM] + [ANYWHERE] * (len(operands) - 1)
-    out_shape = []
-    if mode != "first":
-        operands.append(keep_near(totals[0]))
-        specs.append(IN_VMEM)
-    if mode != "other":
-        operands += [embedded, win]
-        specs += [IN_VMEM] * 2
-        if mode != "first":
-            operands += list(totals[1:])
-            specs += [IN_VMEM] * 2
-        out_shape = [
-            jax.ShapeDtypeStruct((padded, block), F32),
-            jax.ShapeDtypeStruct((vocab, padded), F32),
-        ]
-    if mode == "first":
-        out_shape.append(pltpu.VMEM((hidden_width, block), F32))
-    elif mode == "sum":
-        out_shape.append(jax.ShapeDtypeStruct((hidden_width, block), F32))
-    elif mode == "other":
-        out_shape.append(jax.ShapeDtypeStruct((near, rows_dev, block), BF16))
+    if mode == "own":
+        more = [little[0]]
+        out_shape, out_specs = [], []
     else:
-        out_shape.append(jax.ShapeDtypeStruct((near, rows_dev, block), F32))
+        more = [embedded, win] + list(little)
+        out_shape = [in_hbm(v.shape, F32) for v in little]
+        out_specs = [IN_VMEM] * 2
+    if mode == "sum":
+        out_shape.append(in_hbm((hidden_width, block), F32))
+        out_specs.append(pl.BlockSpec((tile, block), lambda i: (i, 0)))
+    else:
+        rows = rows_dev + padded // (near * sizes[2])
+        kind = BF16 if mode == "other" else F32
+        out_shape.append(jax.ShapeDtypeStruct((near, rows, block), kind))
+        out_specs.append(pl.BlockSpec((1, rows, block), lambda i: (i, 0, 0)))
     return pl.pallas_call(
-        functools.partial(grow_kernel, tuple(spec), mode, sizes),
-        in_specs=specs,
-        out_specs=[IN_VMEM] * len(out_shape),
+        functools.partial(grow_kernel, tuple(spec), mode, sizes, blocks, early),
+        grid=(blocks,),
+        in_specs=specs + [IN_VMEM] * len(more),
+        out_specs=out_specs,
         out_shape=out_shape,
         scratch_shapes=[
+            pltpu.VMEM((2, positions, tile), BF16),
+            pltpu.VMEM((positions, block), BF16),
+            pltpu.SemaphoreType.DMA((2, len(spec))),
             pltpu.SemaphoreType.DMA((len(spec),)),
-            pltpu.SemaphoreType.DMA((len(spec),)),
-            pltpu.VMEM((positions, hidden_width), BF16),
-            pltpu.VMEM((positions, block), BF16),
         ],
-        compiler_params=pltpu.CompilerParams(vmem_limit_bytes=36 * MIB),
+        compiler_params=pltpu.CompilerParams(
+            vmem_limit_bytes=28 * MIB, dimension_semantics=("arbitrary",)
+        ),
+        cost_estimate=LITTLE,
         name="weight_gradient",
-    )(*operands)
+    )(*operands, *more)
 
 
 def first_sum_kernel(kept, moved, send_a, keep_a, send_b, keep_b):
@@ -827,88 +1030,215 @@
         send[...] = (keep[1] + moved[1].astype(F32)).astype(BF16)
 
 
-def last_sum_kernel(last_a, moved_a, last_b, moved_b, out):
-    width = out.shape[2]
+def last_sum_kernel(last_a, moved_a, last_b, moved_b, out, small):
+    rows, _, width = out.shape
     for index, (last, moved) in enumerate(((last_a, moved_a), (last_b, moved_b))):
         for part in range(2):
             at = slice(part * width, (part + 1) * width)
-            out[:, 2 * index + part, :] = last[:, at] + moved[:, at].astype(F32)
-
-
-def run_sum(kernel, out_shape, *operands):
+            total = last[:, at] + moved[:, at].astype(F32)
+            out[:, 2 * index + part, :] = total[:rows, :]
+            to = slice((2 * index + part) * width, (2 * index + part + 1) * width)
+            small[:, to] = total[rows:, :].astype(BF16)
+
+
+def run_sum(kernel, out_shape, *operands, ties=()):
+    count = len(operands)
+
+    def tied(*refs):
+        kernel(*refs[:count], *refs[count + len(ties) :])
+
     return pl.pallas_call(
-        kernel,
-        in_specs=[IN_VMEM] * len(operands),
+        tied,
+        in_specs=[IN_VMEM] * count + [ANYWHERE] * len(ties),
         out_specs=[IN_VMEM] * len(out_shape),
         out_shape=out_shape,
-        compiler_params=pltpu.CompilerParams(vmem_limit_bytes=40 * MIB),
+        compiler_params=pltpu.CompilerParams(vmem_limit_bytes=30 * MIB),
         name="sum_rows",
-    )(*operands)
-
-
-def reduce_rows(kept, sent, sizes):
-    _, rows_dev, block = kept.shape
+    )(*operands, *ties)
+
+
+def reduce_rows(kept, sent, sizes, rows_dev, beside, ties):
+    _, rows, block = kept.shape
     half = block // 2
-    pair = jax.ShapeDtypeStruct((2, rows_dev, half), BF16)
-    pair_sum = jax.ShapeDtypeStruct((2, rows_dev, half), F32)
-    one = jax.ShapeDtypeStruct((rows_dev, half), BF16)
-    one_sum = jax.ShapeDtypeStruct((rows_dev, half), F32)
+    pair = jax.ShapeDtypeStruct((2, rows, half), BF16)
+    pair_sum = jax.ShapeDtypeStruct((2, rows, half), F32)
+    one = jax.ShapeDtypeStruct((rows, half), BF16)
+    one_sum = jax.ShapeDtypeStruct((rows, half), F32)
     moved = send_rows(sent, sizes, 2, 1)
     send_a, keep_a, send_b, keep_b = run_sum(
-        first_sum_kernel, [pair, pair_sum, pair, pair_sum], kept, moved
+        first_sum_kernel, [pair, pair_sum, pair, pair_sum], kept, moved, ties=ties
     )
     moved_a = send_rows(send_a, sizes, 1, 1)
     moved_b = send_rows(send_b, sizes, 0, 1)
-    send_a, last_a, send_b, last_b = run_sum(
-        second_sum_kernel, [one, one_sum, one, one_sum], keep_a, moved_a, keep_b, moved_b
-    )
-    moved_a = send_rows(send_a, sizes, 0, 1)
-    moved_b = send_rows(send_b, sizes, 1, 1)
-    (out,) = run_sum(
+    results = [beside[0](send_a)]
+    send_c, last_a, send_d, last_b = run_sum(
+        second_sum_kernel, [one, one_sum, one, one_sum], keep_a, moved_a, keep_b, moved_b,
+        ties=results[0][1],
+    )
+    moved_a = send_rows(send_c, sizes, 0, 1)
+    moved_b = send_rows(send_d, sizes, 1, 1)
+    results.append(beside[1](send_c, results[0][0]))
+    out, small = run_sum(
         last_sum_kernel,
-        [jax.ShapeDtypeStruct((rows_dev, 4, block // 4), F32)],
+        [
+            jax.ShapeDtypeStruct((rows_dev, 4, block // 4), F32),
+            jax.ShapeDtypeStruct((rows - rows_dev, block), BF16),
+        ],
         last_a, moved_a, last_b, moved_b,
-    )
-    return out
-
-
-def show_kernel(chunks, *refs):
+        ties=results[1][1],
+    )
+    return out, small, results[0][0], results[1][0]
+
+
+def spread_kernel(parts, *refs):
+    where, blocks, (mine, other, packed) = refs[0], refs[1:9], refs[9:12]
+    loss, embedding, grad, bias, decoder, decoder_bias, held = refs[12:]
+    tile = blocks[0].shape[0]
+    rows, _, width = grad.shape
+    for bits, block in enumerate(blocks):
+        first = pl.multiple_of(jnp.bitwise_xor(where[0], bits) * tile, tile)
+        held[pl.ds(first, tile), :] = block[...].astype(F32)
+    for gate in range(4):
+        at = slice(gate * width, (gate + 1) * width)
+        grad[:, gate, :] = held[:rows, at]
+        bias[gate : gate + 1, :] = held[rows : rows + 1, at]
+    vocab = decoder.shape[1]
+    half = mine.shape[1]
+    me_c = lax.rem(where[0], 2)
+    for block, place in ((mine, me_c), (other, 1 - me_c)):
+        at = pl.ds(pl.multiple_of(place * half, half), half)
+        decoder[at, :] = block[...].astype(F32).T[:, :vocab]
+    pack = packed[...]
+    embedding[...] = pack[:vocab, : embedding.shape[1]]
+    first = packed.shape[0] - EXTRA_ROWS
+    row = jnp.concatenate([pack[first + i : first + i + 1, :] for i in range(parts)], axis=1)
+    decoder_bias[...] = row[:, :vocab]
+    loss[...] = pack[first + parts : first + parts + 1, :1]
+
+
+def spread_small(where, small, block_sum, packed, sizes, rows, embed_shape):
+    tile, block = small.shape
+    vocab, embed_width = embed_shape
+    unit_width = block // 4
+    blocks = [small]
+    for axis in (0, 1):
+        moved = [send_rows(value, sizes, axis, 1) for value in [packed] + blocks]
+        packed, block_sum, blocks = sum_and_choose(
+            where, 1 - axis, packed, block_sum, moved[0], send_rows(block_sum, sizes, 1 - axis, 1),
+            blocks + moved[1:],
+        )
+    blocks = blocks + [send_rows(value, sizes, 2, 1) for value in blocks]
+    other = send_rows(block_sum, sizes, 2, 1)
+    order = [4 * (i & 1) + 2 * ((i >> 1) & 1) + (i >> 2) for i in range(8)]
+    blocks = [blocks[order.index(bits)] for bits in range(8)]
+    return pl.pallas_call(
+        functools.partial(spread_kernel, -(-vocab // LANES)),
+        in_specs=[IN_SMEM] + [IN_VMEM] * 11,
+        out_specs=[IN_VMEM] * 6,
+        out_shape=[
+            jax.ShapeDtypeStruct((1, 1), F32),
+            jax.ShapeDtypeStruct((vocab, embed_width), F32),
+            jax.ShapeDtypeStruct((rows, 4, unit_width), F32),
+            jax.ShapeDtypeStruct((4, unit_width), F32),
+            jax.ShapeDtypeStruct((unit_width, vocab), F32),
+            jax.ShapeDtypeStruct((1, vocab), F32),
+        ],
+        scratch_shapes=[pltpu.VMEM((8 * tile, block), F32)],
+        compiler_params=pltpu.CompilerParams(vmem_limit_bytes=12 * MIB),
+        name="spread_small",
+    )(where, *blocks, block_sum, other, packed)
+
+
+def cut_ends_kernel(count, *refs):
+    where, arrays, outs, sems = refs[0], refs[1 : 1 + count], refs[-5:-1], refs[-1]
+    seqs = arrays[0].shape[0]
+    width = outs[0].shape[1]
+    copies = []
+    for bits, out in enumerate(outs):
+        z = jnp.bitwise_xor(where[1], bits)
+        at = pl.ds(pl.multiple_of(z * width, width), width)
+        for index, array in enumerate(arrays):
+            to = out.at[pl.ds(index * seqs, seqs)]
+            copies.append(pltpu.make_async_copy(array.at[:, at], to, sems.at[bits, index]))
+    wait_or_start("start", copies, [], None)
+    wait_or_start("wait", copies, [], None)
+
+
+def join_ends_kernel(count, *refs):
+    where, pieces, (mine, other) = refs[0], refs[1:5], refs[5:7]
+    outs, total = refs[-1 - count : -1], refs[-1]
+    seqs = outs[0].shape[0] // len(pieces)
+    for bits, piece in enumerate(pieces):
+        z = jnp.bitwise_xor(where[1], bits)
+        at = pl.ds(pl.multiple_of(z * seqs, seqs), seqs)
+        for index, out in enumerate(outs):
+            out[at, :] = piece[index * seqs : (index + 1) * seqs, :]
+    total[...] = mine[...] + other[...]
+
+
+def exchange_ends(where, arrays, packed, ties=()):
+    units = 4
+    seqs, hidden_width = arrays[0].shape
+    count = len(arrays)
+    width = hidden_width // units
+    pieces = pl.pallas_call(
+        functools.partial(cut_ends_kernel, count),
+        in_specs=[IN_SMEM] + [ANYWHERE] * count,
+        out_specs=[IN_VMEM] * units,
+        out_shape=[jax.ShapeDtypeStruct((count * seqs, width), F32)] * units,
+        scratch_shapes=[pltpu.SemaphoreType.DMA((units, count))],
+        compiler_params=pltpu.CompilerParams(vmem_limit_bytes=4 * MIB),
+        cost_estimate=LITTLE,
+        name="cut_ends",
+    )(where, *[keep_far(v) for v in arrays])
+    pieces = [pieces[0]] + [swap_units(pieces[bits], bits) for bits in range(1, units)]
+    out = pl.pallas_call(
+        functools.partial(join_ends_kernel, count),
+        in_specs=[IN_SMEM] + [IN_VMEM] * (units + 2) + [ANYWHERE] * len(ties),
+        out_specs=[IN_VMEM] * (count + 1),
+        out_shape=[jax.ShapeDtypeStruct((units * seqs, width), F32)] * count
+        + [jax.ShapeDtypeStruct(packed.shape, F32)],
+        compiler_params=pltpu.CompilerParams(vmem_limit_bytes=4 * MIB),
+        cost_estimate=LITTLE,
+        name="join_ends",
+    )(where, *pieces, packed, swap_units(packed, 2), *ties)
+    return out[:count], out[count]
+
+
+def show_kernel(chunks, window, *refs):
     where, last = refs[:2]
     befores, out, held, sems = refs[2:-3], refs[-3], refs[-2], refs[-1]
-    units, window, seqs, width = held.shape
+    units, local, width = held.shape
+    seqs = local // window
     me_z = where[1]
-    outer = jnp.logical_or(me_z == 0, me_z == 3)
     lanes = pl.ds(pl.multiple_of(me_z * width, width), width)
     always, pairs = [], []
     start = 0
     for chunk, steps in enumerate(chunks):
-        own, near, inner, far = befores[4 * chunk : 4 * chunk + 4]
-        at = pl.ds(start, steps)
+        sources = befores[6 * chunk : 6 * chunk + 6]
+        rows = steps * seqs
 
         def copy(source, bits):
             return pltpu.make_async_copy(
-                source.at[:, :, lanes], held.at[bits, at], sems.at[chunk, bits]
+                source.at[pl.ds(0, rows), lanes],
+                held.at[bits, pl.ds(start, rows)],
+                sems.at[chunk, bits],
             )
 
-        always += [copy(own, 0), copy(near, 1)]
-        for bits in (2, 3):
-            pairs.append((copy(inner.at[3 - bits], bits), copy(far.at[bits - 2], bits)))
-        start += steps
-    for one in always:
-        one.start()
-    for inner_copy, outer_copy in pairs:
-        pl.when(outer)(outer_copy.start)
-        pl.when(jnp.logical_not(outer))(inner_copy.start)
-    for one in always:
-        one.wait()
-    for inner_copy, outer_copy in pairs:
-        pl.when(outer)(outer_copy.wait)
-        pl.when(jnp.logical_not(outer))(inner_copy.wait)
+        for bits, by_place in enumerate(SOURCES):
+            options = [copy(sources[place], bits) for place in by_place]
+            if len(options) == 1:
+                always.append(options[0])
+            else:
+                pairs.append(options)
+        start += rows
+    wait_or_start("start", always, pairs, is_outer(me_z))
+    wait_or_start("wait", always, pairs, is_outer(me_z))
     for bits in range(units):
         first = pl.multiple_of(jnp.bitwise_xor(me_z, bits) * seqs, seqs)
         rows = pl.ds(first, seqs)
-        shown = jnp.swapaxes(held[bits].astype(F32), 0, 1)
-        out[rows, : window - 1, :] = shown[:, 1:, :]
+        shown = held[bits].astype(F32).reshape(window, seqs, width)
+        out[rows, : window - 1, :] = jnp.swapaxes(shown, 0, 1)[:, 1:, :]
         out[rows, window - 1, :] = last[rows, :]
 
 
@@ -918,48 +1248,17 @@
     window = sum(chunks)
     flat = [keep_far(v) for before in befores for v in before]
     return pl.pallas_call(
-        functools.partial(show_kernel, chunks),
+        functools.partial(show_kernel, chunks, window),
         in_specs=[IN_SMEM, IN_VMEM] + [ANYWHERE] * len(flat),
         out_specs=IN_VMEM,
-        out_shape=jax.ShapeDtypeStruct((sequences, window, width), F32),
+        out_shape=in_hbm((sequences, window, width), F32),
         scratch_shapes=[
-            pltpu.VMEM((units, window, seqs, width), BF16),
+            pltpu.VMEM((units, window * seqs, width), BF16),
             pltpu.SemaphoreType.DMA((len(chunks), units)),
         ],
         compiler_params=pltpu.CompilerParams(vmem_limit_bytes=40 * MIB),
         name="show_hidden",
     )(where, last, *flat)
-
-
-def by_place(mine, other, here):
-    return jnp.where(here == 0, jnp.stack([mine, other]), jnp.stack([other, mine]))
-
-
-def sum_rows(value, me_r, sizes):
-    if sizes != (2, 2, 2):
-        return lax.psum(value, "rows")
-    me = (me_r // 4, (me_r // 2) % 2, me_r % 2)
-    count, width = value.shape
-    held = value.reshape(2, 2, 2, count // 8, width)
-    for axis in (2, 1, 0):
-        keep = lax.dynamic_index_in_dim(held, me[axis], axis, keepdims=False)
-        send = lax.dynamic_index_in_dim(held, 1 - me[axis], axis, keepdims=False)
-        held = keep + send_rows(send.astype(BF16), sizes, axis, 1).astype(F32)
-    held = held.astype(BF16)
-    for axis in (0, 1, 2):
-        held = by_place(held, send_rows(held, sizes, axis, 1), me[axis])
-    return held.transpose(2, 1, 0, 3, 4).reshape(count, width).astype(F32)
-
-
-def sum_all(value, sizes):
-    units = lax.axis_size("units")
-    if sizes != (2, 2, 2) or units != 4:
-        return lax.psum(value, ("rows", "units"))
-    for bits in (1, 2):
-        value = value + swap_units(value, bits)
-    for axis in (2, 1, 0):
-        value = value + send_rows(value, sizes, axis, 1)
-    return value
 
 
 def on_device(
@@ -1015,7 +1314,7 @@
         axis=1,
     )
     vocab_padded = -(-vocab_size // LANES) * LANES
-    decoder_own = jnp.pad(decoder_weight, ((0, 0), (0, vocab_padded - vocab_size)))
+    vocab_rows = -(-vocab_size // 8) * 8
 
     def share(value, bits, axis=0):
         origin = jnp.bitwise_xor(me_z, bits)
@@ -1032,8 +1331,9 @@
     active = jnp.arange(window)[:, None] < lengths_own[:, 0][None, :]
     active = active.astype(F32).reshape(local, 1)
     bias_row = jnp.pad(decoder_bias, (0, vocab_padded - vocab_size)).reshape(1, vocab_padded)
+    decoder_packed = pack_decoder(decoder_weight, units)
     ready = [
-        embedded, embedded_own, lengths_own, target_own, active, bias_row, win_own, decoder_own
+        embedded, embedded_own, lengths_own, target_own, active, bias_row, win_own, decoder_packed
     ]
     own_weight = recurrent_weight.reshape(rows_dev, block)
     shape = (units, hidden_width, block)
@@ -1057,151 +1357,191 @@
     chunks = []
     befores = []
     lows = []
-    decoders = [decoder_own]
-    started = []
-
-    def due():
-        return [keep_far(v) for v in started[-2]] if len(started) > 1 else []
-
-    def pass_on():
+    started = {}
+
+    def due(*names):
+        return [v for name in names for v in started.get(name, [])]
+
+    def pass_on(latest, numbers):
         launched = []
-        for before in befores:
-            if len(before) == 1:
+        onward = [n for n in numbers if n in range(len(befores)) and len(befores[n]) in (3, 5)]
+        old = [v for n in onward for v in befores[n][1:3] + befores[n][3:4]]
+        if old:
+            new = hold(old, [latest])
+            for values in list(started.values()) + [befores[n] for n in onward]:
+                values[:] = [
+                    next((w for u, w in zip(old, new) if u is v), v) for v in values
+                ]
+        for number in numbers:
+            if number not in range(len(befores)):
+                continue
+            before = befores[number]
+            had = len(before)
+            if had == 1:
                 before.append(swap_units(before[0], 1))
-            elif len(before) == 2:
-                (joined,) = assemble(where, [[(before[0][None], 0), (before[1][None], 0)]])
-                before.append(lax.ppermute(joined, "units", [(1, 2), (2, 1)]))
-            elif len(before) == 3:
+                before.append(lax.ppermute(before[0], "units", [(1, 2), (2, 1)]))
+            elif had == 3:
+                before.append(lax.ppermute(before[1], "units", [(1, 2), (2, 1)]))
                 before.append(lax.ppermute(before[2], "units", [(1, 0), (2, 3)]))
-            else:
-                continue
-            launched.append(before[-1])
+            elif had == 5:
+                before.append(lax.ppermute(before[3], "units", [(1, 0), (2, 3)]))
+            launched += before[had:]
         return launched
 
-    for steps in FORWARD_CHUNKS:
+    count = len(FORWARD_CHUNKS)
+    for number, steps in enumerate(FORWARD_CHUNKS):
         preact, cells, before, low, hidden, cell = run_forward(
-            lengths_own, embedded_own, hidden, cell, win, weight, start, steps, due()
+            lengths_own, embedded_own, hidden, cell, win, weight, start, steps,
+            due(("forward", number - 2)),
         )
+        before = before.reshape(steps * seqs, hidden_width)
+        if number == 0:
+            before = join_rows([before, decoder_packed])
         befores.append([before])
-        launched = pass_on()
-        if start == 0:
-            decoders += [swap_units(decoder_own, bits) for bits in others]
-            launched += decoders[1:]
-        started.append(launched)
+        started["forward", number] = pass_on(hidden, (number, number - 1, number - 2))
         chunks.append((start, steps, preact, cells))
         lows.append(low.reshape(steps * seqs, hidden_width))
         start += steps
     final_hidden, final_cell = hidden, cell
 
     out = run_decoder(
-        where, decoders, bias_row, target_own, active, lows, loss_scale, vocab_size, weight
-    )
-    turned, back_grad, loss_part, bias_part, decoder_mine = out[:5]
-    decoder_parts = out[5:]
+        where, befores[0], FORWARD_CHUNKS[0] * seqs, bias_row, target_own, active, lows, loss_scale,
+        vocab_size, weight, rows_dev, square,
+    )
+    turned, back_grad, extras, decoder_sent, decoder_kept = out
     back_grad = back_grad.reshape(window, seqs, hidden_width)
+    started["decoder"] = pass_on(extras, (count - 2, count - 1))
+    moved = None
+    if square:
+        moved = send_rows(decoder_sent, sizes, 2, 1)
+        started["decoder"].append(moved)
 
     grads = None
     end = window
     dpres = []
     pairs = []
+    def runs_of(numbers):
+        runs = []
+        for number in numbers:
+            first, end, offset, which = pairs[number]
+            for bits in range(units):
+                choices = [befores[which][place] for place in SOURCES[bits]]
+                dpre = dpres[number][bits].reshape(-1, block)
+                runs.append((choices, offset * seqs, dpre, bits * local + first * seqs))
+        return runs
+
     for number, steps in enumerate(BACKWARD_CHUNKS):
         first = end - steps
         for which, (offset, size, preact, cells) in enumerate(chunks):
             if offset <= first and end <= offset + size:
                 break
+        names = {
+            0: [("forward", count - 2)],
+            1: [("forward", count - 1), "decoder"],
+        }.get(number, [("backward", number - 2)])
+        ties = due(*names) + ([decoder_kept] if square and number in (1, 2) else [])
         out = run_backward(
-            where, lengths_own, preact, cells, offset, back_grad, grads, turned, first, steps, due()
+            where, lengths_own, preact, cells, offset, back_grad, grads, turned, first, steps, ties
         )
         grads = out[units:]
         dpres.append([out[0]] + [swap_units(out[bits], bits) for bits in others])
-        started.append(dpres[-1][1:] + pass_on())
+        launched = dpres[-1][1:]
+        names = [("backward", number - 1)] if number else [("forward", count - 1), "decoder"]
+        if number == 0:
+            launched = launched + pass_on(grads[0], (count - 1,))
+        if square and number < 2:
+            ties = [grads[0]] + due(*names)
+            decoder_sent, decoder_kept = add_parts(decoder_kept, moved, number <= 1, ties)
+            if number == 1:
+                decoder_sent, decoder_kept = decoder_sent[0], decoder_kept[0]
+            moved = [
+                lambda v: send_rows(v, sizes, 1, 1),
+                lambda v: send_rows(v, sizes, 0, 1),
+            ][number](decoder_sent)
+            launched = launched + [moved]
+        started["backward", number] = launched
         pairs.append((first, end, first - offset, which))
         end = first
 
-    flat = sum(befores, []) + list(decoder_parts)
-    flat += [where, embedded, decoder_mine, bias_part, loss_part, final_hidden, final_cell, win_own]
-    flat = hold(flat, [grads[0]])
-    befores = [flat[i * 4 : (i + 1) * 4] for i in range(len(befores))]
-    flat = flat[len(befores) * 4 :]
-    decoder_parts, flat = flat[: units - 1], flat[units - 1 :]
-    where, embedded, decoder_mine, bias_part, loss_part = flat[:5]
-    final_hidden, final_cell, win_own = flat[5:]
-    me_r, me_z = where[0], where[1]
-
-    def grow(numbers, totals, mode):
-        runs = []
-        for number in numbers:
-            first, end, offset, which = pairs[number]
-            own, near, inner, far = [
-                v.reshape(v.shape[:-3] + (-1, hidden_width)) for v in befores[which]
-            ]
-            for bits in range(units):
-                choices = [
-                    [(own, None)],
-                    [(near, None)],
-                    [(inner, 1), (far, 0)],
-                    [(inner, 0), (far, 1)],
-                ][bits]
-                dpre = dpres[number][bits].reshape(-1, block)
-                runs.append((choices, offset * seqs, dpre, bits * local + first * seqs))
-        return run_grow(
-            where, runs, embedded, win_own, totals, mode, sizes, rows_dev, vocab_padded
+    flat = hold(sum(befores, []) + [where, embedded, win_own], [grads[0]])
+    befores = [flat[i * 6 : (i + 1) * 6] for i in range(count)]
+    where, embedded, win_own = flat[6 * count :]
+
+    number = len(BACKWARD_CHUNKS) - 1
+    runs = runs_of(range(number + 1))
+    early = units * (window - BACKWARD_CHUNKS[-1]) * seqs
+    little = run_little(
+        runs_of(range(number)), embedded, win_own, extras, vocab_rows, [grads[0]]
+    )
+
+    def grow(little, mode):
+        return run_grow(where, runs, early, embedded, win_own, little, mode, sizes, rows_dev)
+
+    late_arrays = [where, final_hidden, final_cell] + list(grads)
+
+    def show(tie, last):
+        (here,) = hold([where], [tie])
+        return show_hidden(here, last, befores, FORWARD_CHUNKS, seqs)
+
+    if square:
+        small, hot_sum, sent = grow(little, "other")
+        (kept,) = grow([small], "own")
+        hot_sum = hot_sum + swap_units(hot_sum, 1)
+
+        def finish(tie):
+            flat = hold(late_arrays + [decoder_kept, moved], [tie])
+            block, kept = add_parts(flat[5], flat[6])
+            across = swap_units(block, 1)
+            block, kept = add_parts(kept, across)
+            ends, packed = exchange_ends(flat[0], flat[1:5], hot_sum, [block])
+            packed = packed + send_rows(packed, sizes, 2, 1)
+            block_sum, _ = add_parts(kept, swap_units(block, 2))
+            return (ends, packed, block_sum), [packed, block_sum]
+
+        def show_last(tie, done):
+            shown = show(tie, done[0][0])
+            return shown, [shown]
+
+        recurrent_grad, small, (ends, packed, block_sum), hidden_out = reduce_rows(
+            kept, sent, sizes, rows_dev, [finish, show_last], [hot_sum]
         )
-
-    numbers = range(len(BACKWARD_CHUNKS))
-    early, late = numbers[:-LAST_CHUNKS], numbers[-LAST_CHUNKS:]
-    small, hot_sum, total = grow(early, None, "first")
-    if square:
-        (sent,) = grow(late, (total,), "other")
-        small, hot_sum, kept = grow(late, (total, small, hot_sum), "own")
-        recurrent_grad = reduce_rows(kept, sent, sizes)
+        packed, block_sum = hold([packed, block_sum], [small])
+        total_loss, embed_grad, input_grad, bias_grad, decoder_out, decoder_bias_grad = spread_small(
+            where, small, block_sum, packed, sizes, embed_width, embedding.shape
+        )
+        total_loss, decoder_bias_grad = total_loss[0, 0], decoder_bias_grad[0]
     else:
-        small, hot_sum, total = grow(late, (total, small, hot_sum), "sum")
+        small, hot_sum, total = grow(little, "sum")
         recurrent_grad = lax.psum_scatter(
             total.astype(BF16), "rows", scatter_dimension=0, tiled=True
         )
         recurrent_grad = recurrent_grad.astype(F32).reshape(rows_dev, 4, unit_width)
-    decoder_sum = decoder_mine
-    for bits in others:
-        decoder_sum = decoder_sum + swap_units(decoder_parts[bits - 1], bits).astype(F32)
-
-    small = jnp.concatenate([small, decoder_sum.reshape(-1, block)], axis=0)
-    small = sum_rows(small, me_r, sizes)
-    decoder_out = small[padded:].reshape(unit_width, vocab_padded)[:, :vocab_size]
-    column = lax.broadcasted_iota(jnp.int32, hot_sum.shape, 1)
-    pack = jnp.where(column < embed_width, hot_sum, bias_part.T)
-    pack = jnp.where(column == embed_width + 1, loss_part, pack)
-    pack = sum_all(pack, sizes)
-
-    ends = jnp.stack([final_hidden, final_cell] + list(grads))
-    shares = []
-    for bits in range(units):
-        to = jnp.bitwise_xor(me_z, bits)
-        piece = lax.dynamic_slice_in_dim(ends, to * unit_width, unit_width, 2)
-        shares.append(piece if bits == 0 else swap_units(piece, bits))
-    shares = jnp.stack(shares)
-
-    def ordered(value):
-        return [
-            lax.dynamic_index_in_dim(value, jnp.bitwise_xor(me_z, z), 0, keepdims=False)
-            for z in range(units)
-        ]
-
-    ends = jnp.concatenate(ordered(shares), axis=1)
-
-    hidden_out = show_hidden(where, ends[0], befores, FORWARD_CHUNKS, seqs)
+        small = lax.psum(small, "rows")
+        input_grad = small[:embed_width].reshape(embed_width, 4, unit_width)
+        bias_grad = small[embed_width].reshape(4, unit_width)
+        flat = hold(late_arrays, [total])
+        ends, _ = exchange_ends(flat[0], flat[1:], hot_sum)
+        hidden_out = show(total, ends[0])
+        decoder_out = lax.psum(decoder_kept, ("rows", "units"))
+        decoder_out = lax.dynamic_slice_in_dim(decoder_out, me_z * unit_width, unit_width, 0)
+        decoder_out = decoder_out[:, :vocab_size]
+        pack = lax.psum(hot_sum, ("rows", "units"))
+        last = vocab_rows + vocab_padded // LANES
+        total_loss = pack[last, 0]
+        embed_grad = pack[:vocab_size, :embed_width]
+        decoder_bias_grad = pack[vocab_rows:last].reshape(-1)[:vocab_size]
 
     return (
-        pack[0, embed_width + 1],
+        total_loss,
         hidden_out,
         ends[0],
         ends[1],
-        pack[:vocab_size, :embed_width],
-        small[:embed_width].reshape(embed_width, 4, unit_width),
+        embed_grad,
+        input_grad,
         recurrent_grad,
-        small[embed_width].reshape(4, unit_width),
+        bias_grad,
         decoder_out,
-        pack[:vocab_size, embed_width],
+        decoder_bias_grad,
         ends[2],
         ends[3],
     )

time: 901 us -> 780 us (0.87)
  waiting for transfers between devices: 256 us -> 145 us
  starting transfers between devices: 119 us -> 146 us
  Pallas kernels: 425 us -> 413 us
  other arithmetic: 15.8 us -> 5.15 us
    ppermute x33 -> x29, waiting for transfers between devices: 126 us -> 33.1 us  [swap_units(): return lax.ppermute(value, 'units', [(z, z ^ bits) for z in range(count)])]
    ppermute x30 -> x37, waiting for transfers between devices: 83.1 us -> 66.4 us  [send_rows(): return lax.ppermute(value, 'rows', row_shift(sizes, axis, step))]
    ppermute x33 -> x29, starting transfers between devices: 77.3 us -> 93.5 us  [swap_units(): return lax.ppermute(value, 'units', [(z, z ^ bits) for z in range(count)])]
    unnamed x237 -> x263, local copies, waits for them, and re-layouts: 30 us -> 46.1 us
    pallas_call x10 -> x6, Pallas kernels: 18.1 us -> 12 us  [assemble(): pl.pallas_call(functools.partial(assemble_kernel, tuple(plan), len(source...]
    ppermute x30 -> x37, starting transfers between devices: 23.5 us -> 27.6 us  [send_rows(): return lax.ppermute(value, 'rows', row_shift(sizes, axis, step))]
    pallas_call x8 -> x19, Pallas kernels: 78.3 us -> 74.9 us  [the longest x2 31 us: run_grow(): pl.pallas_call(functools.partial(grow_kernel, tuple(spec), mode, sizes, b...]
  transfers between devices with their start and end apart: 75 -> 86, of which waited for: 32 -> 31; matrix products, arithmetic and copies ran while one was open for 6% -> 3% of each run, Pallas kernels for 38% -> 43%
where the time goes in v2:
time: 780 us; the launch traced here: 774 us
  Pallas kernels  413 us (53%)
  starting transfers between devices  146 us (19%)
  waiting for transfers between devices  145 us (19%)
  local copies, waits for them, and re-layouts  60.2 us (8%)
    pallas_call x4, Pallas kernels, run_forward(): pl.pallas_call(functools.partial(forward_kernel, start, len(ties)), grid=...  160 us
    pallas_call x5, Pallas kernels, run_backward(): pl.pallas_call(functools.partial(backward_kernel, first_step, steps, len(...  157 us
    ppermute x29, starting transfers between devices, swap_units(): return lax.ppermute(value, 'units', [(z, z ^ bits) for z in range(count)])  93.5 us
    ppermute x37, waiting for transfers between devices, send_rows(): return lax.ppermute(value, 'rows', row_shift(sizes, axis, step))  66.4 us
    unnamed x263, local copies, waits for them, and re-layouts  46.1 us
    ppermute x29, waiting for transfers between devices, swap_units(): return lax.ppermute(value, 'units', [(z, z ^ bits) for z in range(count)])  33.1 us
    pallas_call x2, Pallas kernels, run_grow(): pl.pallas_call(functools.partial(grow_kernel, tuple(spec), mode, sizes, b...  31 us
    ppermute x2, waiting for transfers between devices, send_units(): lax.ppermute(value, 'units', [(z, (z + step) % count) for z in range(coun...  28.5 us
  transfers between devices with their start and end apart: 86, of which 31 were waited for; matrix products, arithmetic and copies ran while one was open for 3% of the time, Pallas kernels for 43%

profile of v2, /device:TPU:0, one launch (start us, length us, event | category | flops | bytes accessed | tf_op | source)
XLA Modules:
  0.0 773.6 jit_solution(4668294542714319092)
XLA Ops:
  21.8 9.2 %collective-permute-done.1.refs_3_.refs_1_.refs_2_ = bf16[2,128,2048]{2,1,0:T(8,128)(2,1)} collective-permute-done((bf16[2,128,2048]{2,1,0:T(8,128)(2,1)S(1)}, bf16[2,128,2048]{2,1,0:T(8,128)(2,1)}, u32[]{:S(2)}, u32[]{:S(2)}) %collective-permute-start.1) | collective-permute-done | bytes 1048608 | tf_op jit(solution)/shard_map/ppermute | solution.py:58
  42.8 19.3 %collective-permute-done.3.refs_3_.refs_1_.refs_5_ = bf16[2,128,2048]{2,1,0:T(8,128)(2,1)S(1)} collective-permute-done((bf16[2,128,2048]{2,1,0:T(8,128)(2,1)S(1)}, bf16[2,128,2048]{2,1,0:T(8,128)(2,1)S(1)}, u32[]{:S(2)}, u32[]{:S(2)}) %collective-permute-start.3) | collective-permute-done | bytes 1048608 | tf_op jit(solution)/shard_map/ppermute | solution.py:58
  62.1 7.8 %collective-permute-done.4.refs_2_.refs_7_ = bf16[3,128,2048]{2,1,0:T(8,128)(2,1)S(1)} collective-permute-done((bf16[3,128,2048]{2,1,0:T(8,128)(2,1)S(1)}, bf16[3,128,2048]{2,1,0:T(8,128)(2,1)S(1)}, u32[]{:S(2)}, u32[]{:S(2)}) %collective-permute-start.4) | collective-permute-done | bytes 1572896 | tf_op jit(solution)/shard_map/ppermute | solution.py:53
  88.6 17.0 %collective-permute-done.7.refs_3_ = bf16[2,128,2048]{2,1,0:T(8,128)(2,1)} collective-permute-done((bf16[2,128,2048]{2,1,0:T(8,128)(2,1)S(1)}, bf16[2,128,2048]{2,1,0:T(8,128)(2,1)}, u32[]{:S(2)}, u32[]{:S(2)}) %collective-permute-start.7) | collective-permute-done | bytes 1048608 | tf_op jit(solution)/shard_map/ppermute | solution.py:259
  120.0 12.2 %collective-permute-done.12.refs_4_.refs_5_ = bf16[96,2048]{1,0:T(8,128)(2,1)S(1)} collective-permute-done((bf16[96,2048]{1,0:T(8,128)(2,1)}, bf16[96,2048]{1,0:T(8,128)(2,1)S(1)}, u32[]{:S(2)}, u32[]{:S(2)}) %collective-permute-start.12) | collective-permute-done | bytes 393248 | tf_op jit(solution)/shard_map/ppermute | solution.py:63
  132.2 12.7 %collective-permute-start.10 = (bf16[96,2048]{1,0:T(8,128)(2,1)}, bf16[96,2048]{1,0:T(8,128)(2,1)S(1)}, u32[]{:S(2)}, u32[]{:S(2)}) collective-permute-start(bf16[96,2048]{1,0:T(8,128)(2,1)} %hold.12), channel_id=1, source_target_pairs={{0,1},{1,0},{2,3},{3,2},{4,5},{5,4},{6,7},{7,6},{8,9},{9,8},{10,11... | collective-permute-start | bytes 1179656 | tf_op jit(solution)/shard_map/ppermute | solution.py:63
  156.3 19.3 %collective-permute-done.19.refs_1_.refs_16_ = bf16[2,128,2048]{2,1,0:T(8,128)(2,1)S(1)} collective-permute-done((bf16[2,128,2048]{2,1,0:T(8,128)(2,1)S(1)}, bf16[2,128,2048]{2,1,0:T(8,128)(2,1)S(1)}, u32[]{:S(2)}, u32[]{:S(2)}) %collective-permute-start.19) | collective-permute-done | bytes 1048608 | tf_op jit(solution)/shard_map/ppermute | solution.py:53
  187.5 7.9 %load_pieces.1.refs_5_.refs_14_ = bf16[4,2048,2048]{2,1,0:T(8,128)(2,1)S(1)} custom-call(s32[2]{0:T(128)S(1)} %pad_add_fusion.1.refs_0_.refs_24_, bf16[2,128,2048]{2,1,0:T(8,128)(2,1)S(1)} %copy-done.16, bf16[2,128,2048]{2,1,0:T(8,128)(2,1)} %collective-permute-done.1.refs_3_.refs_1_.refs_2_, bf16[1,128,2048]{2,1,0:T(8,128)(2,1)S(1)} %copy-done.52, ...), custom_call_target="tpu_custom_call" | custom-call | bytes 1024 | tf_op jit(solution)/shard_map/load_pieces/pallas_call | solution.py:193
  195.4 44.8 %forward_steps.4 = (f32[9,4,16,2048]{3,2,1,0:T(8,128)}, f32[9,16,2048]{2,1,0:T(8,128)}, bf16[9,16,2048]{2,1,0:T(8,128)(2,1)}, bf16[9,16,2048]{2,1,0:T(8,128)(2,1...) custom-call(s32[16,1]{1,0:T(8,128)} %copy-done.63, bf16[32,16,128]{2,1,0:T(8,128)(2,1)} %bitcast.134, f32[16,2048]{1,0:T(8,128)} %copy-done.74, ...), custom_call_target="tpu_custom_call" | custom-call | bytes 150994944 | tf_op jit(solution)/shard_map/forward_steps/pallas_call | solution.py:464
  242.3 44.8 %forward_steps.5 = (f32[9,4,16,2048]{3,2,1,0:T(8,128)}, f32[9,16,2048]{2,1,0:T(8,128)}, bf16[9,16,2048]{2,1,0:T(8,128)(2,1)}, bf16[9,16,2048]{2,1,0:T(8,128)(2,1...) custom-call(s32[16,1]{1,0:T(8,128)} %copy-done.63, bf16[32,16,128]{2,1,0:T(8,128)(2,1)} %bitcast.135, ...), custom_call_target="tpu_custom_call" | custom-call | bytes 150994944 | tf_op jit(solution)/shard_map/forward_steps/pallas_call | solution.py:464
  298.6 35.3 %forward_steps.6 = (f32[7,4,16,2048]{3,2,1,0:T(8,128)}, f32[7,16,2048]{2,1,0:T(8,128)}, bf16[7,16,2048]{2,1,0:T(8,128)(2,1)}, bf16[7,16,2048]{2,1,0:T(8,128)(2,1...) custom-call(s32[16,1]{1,0:T(8,128)} %copy-done.63, bf16[32,16,128]{2,1,0:T(8,128)(2,1)} %bitcast.136, ...), custom_call_target="tpu_custom_call" | custom-call | bytes 117440512 | tf_op jit(solution)/shard_map/forward_steps/pallas_call | solution.py:464
  345.7 35.3 %forward_steps.7 = (f32[7,4,16,2048]{3,2,1,0:T(8,128)}, f32[7,16,2048]{2,1,0:T(8,128)}, bf16[7,16,2048]{2,1,0:T(8,128)(2,1)}, bf16[7,16,2048]{2,1,0:T(8,128)(2,1...) custom-call(s32[16,1]{1,0:T(8,128)} %copy-done.63, bf16[32,16,128]{2,1,0:T(8,128)(2,1)} %bitcast.137, ...), custom_call_target="tpu_custom_call" | custom-call | bytes 117440512 | tf_op jit(solution)/shard_map/forward_steps/pallas_call | solution.py:464
  389.5 15.7 %decoder.1 = (bf16[4,2048,2048]{2,1,0:T(8,128)(2,1)S(1)}, bf16[512,2048]{1,0:T(8,128)(2,1)}, f32[8,128]{1,0:T(8,128)}, bf16[4,288,256]{2,1,0:T(8,128)(2,1)}, f32[4,288,256]{2,1,0:T(8,128)}) custom-call(s32[2]{0:T(128)} %copy-done.70, f32[1,384]{1,0:T(1,128)} %copy-done.77, s32[512,1]{1,0:T(8,128)} %copy-done.43, ...), custom_call_target="tpu_custom_call", output_to_operand_aliasing={{0}: (14, {})} | custom-call | tf_op jit(solution)/shard_map/decoder/pallas_call | solution.py:715
  410.8 34.1 %backward_steps.5 = (bf16[7,16,2048]{2,1,0:T(8,128)(2,1)}, bf16[7,16,2048]{2,1,0:T(8,128)(2,1)}, bf16[7,16,2048]{2,1,0:T(8,128)(2,1)}, bf16[7,16,2048]{2,1,0:T(8...) custom-call(s32[2]{0:T(128)} %copy-done.70, s32[16,1]{1,0:T(8,128)} %copy-done.63, ...), custom_call_target="tpu_custom_call" | custom-call | bytes 117440512 | tf_op jit(solution)/shard_map/backward_steps/pallas_call | solution.py:552
  445.0 7.1 collective-permute-start.43
  463.7 34.2 %backward_steps.6 = (bf16[7,16,2048]{2,1,0:T(8,128)(2,1)}, bf16[7,16,2048]{2,1,0:T(8,128)(2,1)}, bf16[7,16,2048]{2,1,0:T(8,128)(2,1)}, bf16[7,16,2048]{2,1,0:T(8...) custom-call(s32[2]{0:T(128)} %copy-done.70, s32[16,1]{1,0:T(8,128)} %copy-done.63, ...), custom_call_target="tpu_custom_call" | custom-call | bytes 117440512 | tf_op jit(solution)/shard_map/backward_steps/pallas_call | solution.py:552
  505.1 43.4 %backward_steps.7 = (bf16[9,16,2048]{2,1,0:T(8,128)(2,1)}, bf16[9,16,2048]{2,1,0:T(8,128)(2,1)}, bf16[9,16,2048]{2,1,0:T(8,128)(2,1)}, bf16[9,16,2048]{2,1,0:T(8...) custom-call(s32[2]{0:T(128)} %copy-done.70, s32[16,1]{1,0:T(8,128)} %copy-done.63, ...), custom_call_target="tpu_custom_call" | custom-call | bytes 150994944 | tf_op jit(solution)/shard_map/backward_steps/pallas_call | solution.py:552
  558.8 29.7 %backward_steps.8 = (bf16[6,16,2048]{2,1,0:T(8,128)(2,1)}, bf16[6,16,2048]{2,1,0:T(8,128)(2,1)}, bf16[6,16,2048]{2,1,0:T(8,128)(2,1)}, bf16[6,16,2048]{2,1,0:T(8...) custom-call(s32[2]{0:T(128)} %copy-done.70, s32[16,1]{1,0:T(8,128)} %copy-done.63, ...), custom_call_target="tpu_custom_call" | custom-call | bytes 100663296 | tf_op jit(solution)/shard_map/backward_steps/pallas_call | solution.py:552
  593.9 15.9 %backward_steps.9 = (bf16[3,16,2048]{2,1,0:T(8,128)(2,1)}, bf16[3,16,2048]{2,1,0:T(8,128)(2,1)}, bf16[3,16,2048]{2,1,0:T(8,128)(2,1)}, bf16[3,16,2048]{2,1,0:T(8...) custom-call(s32[2]{0:T(128)} %copy-done.70, s32[16,1]{1,0:T(8,128)} %copy-done.63, ...), custom_call_target="tpu_custom_call" | custom-call | bytes 50331648 | tf_op jit(solution)/shard_map/backward_steps/pallas_call | solution.py:552
  609.9 29.2 %collective-permute-start.58 = (bf16[3,16,2048]{2,1,0:T(8,128)(2,1)}, bf16[3,16,2048]{2,1,0:T(8,128)(2,1)S(1)}, u32[]{:S(2)}, u32[]{:S(2)}) collective-permute-start(bf16[3,16,2048]{2,1,0:T(8,128)(2,1)} %get-tuple-element.319), channel_id=1, source_target_pairs={{0,1},{1,0},{2,3},{3,2},{4,5},{5,4},{6,7},{7,6},{8,9},{9,8},{10,11... | collective-permute-start | bytes 589832 | tf_op jit(solution)/shard_map/ppermute | solution.py:63
  645.5 9.6 %little_gradients.1 = (f32[128,2048]{1,0:T(8,128)}, f32[288,128]{1,0:T(8,128)}) custom-call(bf16[112,2048]{1,0:T(8,128)(2,1)} %bitcast.176, bf16[112,2048]{1,0:T(8,128)(2,1)} %bitcast.125, bf16[112,2048]{1,0:T(8,128)(2,1)} %bitcast.128, bf16[112,2048]{1,0:T(8,128)(2,1)} %bitcast.131, bf16[112,2048]{1,0:T(8,128)(2,1)} %bitcast.179, ...), custom_call_target="tpu_custom_call" | custom-call | bytes 1024 | tf_op jit(solution)/shard_map/little_gradients/pallas_call | solution.py:848
  658.1 16.0 %weight_gradient.2 = (f32[128,2048]{1,0:T(8,128)}, f32[288,128]{1,0:T(8,128)}, bf16[4,272,2048]{2,1,0:T(8,128)(2,1)S(1)}) custom-call(s32[2]{0:T(128)S(1)} %copy-done.71, bf16[112,2048]{1,0:T(8,128)(2,1)} %get-tuple-element.287.refs_1_.refs_20_, bf16[112,2048]{1,0:T(8,128)(2,1)} %get-tuple-element.288.refs_2_.refs_21_, ...), custom_call_target="tpu_custom_call" | custom-call | bytes 1024 | tf_op jit(solution)/shard_map/weight_gradient/pallas_call | solution.py:988
  676.4 15.0 %weight_gradient.3.refs_0_ = f32[4,272,2048]{2,1,0:T(8,128)S(1)} custom-call(s32[2]{0:T(128)S(1)} %copy-done.71, bf16[112,2048]{1,0:T(8,128)(2,1)} %get-tuple-element.287.refs_1_.refs_20_, bf16[112,2048]{1,0:T(8,128)(2,1)} %get-tuple-element.288.refs_2_.refs_21_, bf16[112,2048]{1,0:T(8,128)(2,1)} %get-tuple-element.289.refs_3_.refs_23_, ...), custom_call_target="tpu_custom_call" | custom-call | bytes 1024 | tf_op jit(solution)/shard_map/weight_gradient/pallas_call | solution.py:988
  720.4 7.9 %collective-permute-done.69.moved = bf16[288,256]{1,0:T(8,128)(2,1)S(1)} collective-permute-done((bf16[288,256]{1,0:T(8,128)(2,1)}, bf16[288,256]{1,0:T(8,128)(2,1)S(1)}, u32[]{:S(2)}, u32[]{:S(2)}) %collective-permute-start.69) | collective-permute-done | bytes 147488 | tf_op jit(solution)/shard_map/ppermute | solution.py:63
  (510 shorter events, 247.6 us)
Async XLA Ops:
  119.8 59.4 %collective-permute-start.15 = (bf16[8,128,2048]{2,1,0:T(8,128)(2,1)S(1)}, bf16[8,128,2048]{2,1,0:T(8,128)(2,1)S(1)}, u32[]{:S(2)}, u32[]{:S(2)}) collective-permute-start(bf16[8,128,2048]{2,1,0:T(8,128)(2,1)S(1)} %copy-done.81), channel_id=1, source_target_pairs={{0,4},{4,0},{8,12},{12,8},{16,20},{20,16},{24,28},{28,24},{1,5},{5... | collective-permute-start | bytes 12582920 | tf_op jit(solution)/shard_map/ppermute | solution.py:53
  241.4 45.8 %collective-permute-start.25 = (bf16[224,2048]{1,0:T(8,128)(2,1)S(1)}, bf16[224,2048]{1,0:T(8,128)(2,1)S(1)}, u32[]{:S(2)}, u32[]{:S(2)}) collective-permute-start(bf16[224,2048]{1,0:T(8,128)(2,1)S(1)} %join_rows.1.refs_8_.refs_0_), channel_id=1, source_target_pairs={{0,1},{1,0},{2,3},{3,2},{4,5},{5,4},{6,7},{7,6},{8,9},{9,8},{10,11... | collective-permute-start | bytes 2752520 | tf_op jit(solution)/shard_map/ppermute | solution.py:63
  241.4 45.8 %collective-permute-start.26 = (bf16[224,2048]{1,0:T(8,128)(2,1)S(1)}, bf16[224,2048]{1,0:T(8,128)(2,1)S(1)}, u32[]{:S(2)}, u32[]{:S(2)}) collective-permute-start(bf16[224,2048]{1,0:T(8,128)(2,1)S(1)} %join_rows.1.refs_8_.refs_0_), channel_id=1, source_target_pairs={{1,2},{2,1},{5,6},{6,5},{9,10},{10,9},{13,14},{14,13},{17,18},{18,... | collective-permute-start | bytes 2752520 | tf_op jit(solution)/shard_map/ppermute | solution.py:1382
  289.4 44.6 %collective-permute-start.27 = (bf16[224,2048]{1,0:T(8,128)(2,1)}, bf16[224,2048]{1,0:T(8,128)(2,1)S(1)}, u32[]{:S(2)}, u32[]{:S(2)}) collective-permute-start(bf16[224,2048]{1,0:T(8,128)(2,1)} %get-tuple-element.219.refs_6_.refs_2_), channel_id=1, source_target_pairs={{1,2},{2,1},{5,6},{6,5},{9,10},{10,9},{13,14},{14,13},{17,18},{18,... | collective-permute-start | bytes 2752520 | tf_op jit(solution)/shard_map/ppermute | solution.py:1384
  290.1 43.9 %collective-permute-start.28 = (bf16[224,2048]{1,0:T(8,128)(2,1)}, bf16[224,2048]{1,0:T(8,128)(2,1)S(1)}, u32[]{:S(2)}, u32[]{:S(2)}) collective-permute-start(bf16[224,2048]{1,0:T(8,128)(2,1)} %get-tuple-element.220.refs_7_.refs_3_), channel_id=1, source_target_pairs={{1,0},{2,3},{5,4},{6,7},{9,8},{10,11},{13,12},{14,15},{17,16},{18,... | collective-permute-start | bytes 2752520 | tf_op jit(solution)/shard_map/ppermute | solution.py:1385
  336.2 52.0 %collective-permute-start.29 = (bf16[224,2048]{1,0:T(8,128)(2,1)}, bf16[224,2048]{1,0:T(8,128)(2,1)S(1)}, u32[]{:S(2)}, u32[]{:S(2)}) collective-permute-start(bf16[224,2048]{1,0:T(8,128)(2,1)} %get-tuple-element.225.refs_8_.refs_11_.refs_3_), channel_id=1, source_target_pairs={{1,0},{2,3},{5,4},{6,7},{9,8},{10,11},{13,12},{14,15},{17,16},{18,... | collective-permute-start | bytes 2752520 | tf_op jit(solution)/shard_map/ppermute | solution.py:1387
  337.5 47.0 %collective-permute-start.32 = (bf16[144,2048]{1,0:T(8,128)(2,1)}, bf16[144,2048]{1,0:T(8,128)(2,1)S(1)}, u32[]{:S(2)}, u32[]{:S(2)}) collective-permute-start(bf16[144,2048]{1,0:T(8,128)(2,1)} %get-tuple-element.227.refs_6_.refs_2_), channel_id=1, source_target_pairs={{1,2},{2,1},{5,6},{6,5},{9,10},{10,9},{13,14},{14,13},{17,18},{18,... | collective-permute-start | bytes 1769480 | tf_op jit(solution)/shard_map/ppermute | solution.py:1384
  338.2 46.3 %collective-permute-start.33 = (bf16[144,2048]{1,0:T(8,128)(2,1)}, bf16[144,2048]{1,0:T(8,128)(2,1)}, u32[]{:S(2)}, u32[]{:S(2)}) collective-permute-start(bf16[144,2048]{1,0:T(8,128)(2,1)} %get-tuple-element.228.refs_7_.refs_3_), channel_id=1, source_target_pairs={{1,0},{2,3},{5,4},{6,7},{9,8},{10,11},{13,12},{14,15},{17,16},{18,... | collective-permute-start | bytes 1769480 | tf_op jit(solution)/shard_map/ppermute | solution.py:1385
  388.2 56.7 %collective-permute-start.34 = (bf16[144,2048]{1,0:T(8,128)(2,1)}, bf16[144,2048]{1,0:T(8,128)(2,1)S(1)}, u32[]{:S(2)}, u32[]{:S(2)}) collective-permute-start(bf16[144,2048]{1,0:T(8,128)(2,1)} %get-tuple-element.233.refs_8_.refs_9_), channel_id=1, source_target_pairs={{1,0},{2,3},{5,4},{6,7},{9,8},{10,11},{13,12},{14,15},{17,16},{18,... | collective-permute-start | bytes 1769480 | tf_op jit(solution)/shard_map/ppermute | solution.py:1387
  407.0 45.0 %collective-permute-start.40 = (bf16[112,2048]{1,0:T(8,128)(2,1)}, bf16[112,2048]{1,0:T(8,128)(2,1)S(1)}, u32[]{:S(2)}, u32[]{:S(2)}) collective-permute-start(bf16[112,2048]{1,0:T(8,128)(2,1)} %get-tuple-element.245.refs_0_), channel_id=1, source_target_pairs={{1,2},{2,1},{5,6},{6,5},{9,10},{10,9},{13,14},{14,13},{17,18},{18,... | collective-permute-start | bytes 1376264 | tf_op jit(solution)/shard_map/ppermute | solution.py:1384
  407.7 45.0 %collective-permute-start.41 = (bf16[112,2048]{1,0:T(8,128)(2,1)}, bf16[112,2048]{1,0:T(8,128)(2,1)S(1)}, u32[]{:S(2)}, u32[]{:S(2)}) collective-permute-start(bf16[112,2048]{1,0:T(8,128)(2,1)} %get-tuple-element.246.refs_1_), channel_id=1, source_target_pairs={{1,0},{2,3},{5,4},{6,7},{9,8},{10,11},{13,12},{14,15},{17,16},{18,... | collective-permute-start | bytes 1376264 | tf_op jit(solution)/shard_map/ppermute | solution.py:1385
  409.0 46.4 %collective-permute-start.39 = (bf16[112,2048]{1,0:T(8,128)(2,1)}, bf16[112,2048]{1,0:T(8,128)(2,1)S(1)}, u32[]{:S(2)}, u32[]{:S(2)}) collective-permute-start(bf16[112,2048]{1,0:T(8,128)(2,1)} %get-tuple-element.244.refs_3_.refs_8_.refs_15_), channel_id=1, source_target_pairs={{1,0},{2,3},{5,4},{6,7},{9,8},{10,11},{13,12},{14,15},{17,16},{18,... | collective-permute-start | bytes 1376264 | tf_op jit(solution)/shard_map/ppermute | solution.py:1387
  410.7 46.0 %collective-permute-start.46 = (bf16[4,288,256]{2,1,0:T(8,128)(2,1)}, bf16[4,288,256]{2,1,0:T(8,128)(2,1)S(1)}, u32[]{:S(2)}, u32[]{:S(2)}) collective-permute-start(bf16[4,288,256]{2,1,0:T(8,128)(2,1)} %get-tuple-element.263), channel_id=1, source_target_pairs={{0,4},{4,0},{8,12},{12,8},{16,20},{20,16},{24,28},{28,24},{1,5},{5... | collective-permute-start | bytes 1769480 | tf_op jit(solution)/shard_map/ppermute | solution.py:53
  445.0 52.9 %collective-permute-start.43 = (bf16[7,16,2048]{2,1,0:T(8,128)(2,1)}, bf16[7,16,2048]{2,1,0:T(8,128)(2,1)S(1)}, u32[]{:S(2)}, u32[]{:S(2)}) collective-permute-start(bf16[7,16,2048]{2,1,0:T(8,128)(2,1)} %get-tuple-element.259), channel_id=1, source_target_pairs={{0,1},{1,0},{2,3},{3,2},{4,5},{5,4},{6,7},{7,6},{8,9},{9,8},{10,11... | collective-permute-start | bytes 1376264 | tf_op jit(solution)/shard_map/ppermute | solution.py:63
  452.0 48.6 %collective-permute-start.44 = (bf16[7,16,2048]{2,1,0:T(8,128)(2,1)}, bf16[7,16,2048]{2,1,0:T(8,128)(2,1)S(1)}, u32[]{:S(2)}, u32[]{:S(2)}) collective-permute-start(bf16[7,16,2048]{2,1,0:T(8,128)(2,1)} %get-tuple-element.260), channel_id=1, source_target_pairs={{0,2},{1,3},{2,0},{3,1},{4,6},{5,7},{6,4},{7,5},{8,10},{9,11},{10,... | collective-permute-start | bytes 1376264 | tf_op jit(solution)/shard_map/ppermute | solution.py:63
  452.7 48.6 %collective-permute-start.45 = (bf16[7,16,2048]{2,1,0:T(8,128)(2,1)}, bf16[7,16,2048]{2,1,0:T(8,128)(2,1)S(1)}, u32[]{:S(2)}, u32[]{:S(2)}) collective-permute-start(bf16[7,16,2048]{2,1,0:T(8,128)(2,1)} %get-tuple-element.261), channel_id=1, source_target_pairs={{0,3},{1,2},{2,1},{3,0},{4,7},{5,6},{6,5},{7,4},{8,11},{9,10},{10,... | collective-permute-start | bytes 1376264 | tf_op jit(solution)/shard_map/ppermute | solution.py:63
  455.4 47.7 %collective-permute-start.42 = (bf16[112,2048]{1,0:T(8,128)(2,1)}, bf16[112,2048]{1,0:T(8,128)(2,1)S(1)}, u32[]{:S(2)}, u32[]{:S(2)}) collective-permute-start(bf16[112,2048]{1,0:T(8,128)(2,1)} %get-tuple-element.254.refs_7_.refs_12_.refs_21_), channel_id=1, source_target_pairs={{1,0},{2,3},{5,4},{6,7},{9,8},{10,11},{13,12},{14,15},{17,16},{18,... | collective-permute-start | bytes 1376264 | tf_op jit(solution)/shard_map/ppermute | solution.py:1387
  497.9 53.2 %collective-permute-start.51 = (bf16[7,16,2048]{2,1,0:T(8,128)(2,1)}, bf16[7,16,2048]{2,1,0:T(8,128)(2,1)S(1)}, u32[]{:S(2)}, u32[]{:S(2)}) collective-permute-start(bf16[7,16,2048]{2,1,0:T(8,128)(2,1)} %get-tuple-element.275), channel_id=1, source_target_pairs={{0,1},{1,0},{2,3},{3,2},{4,5},{5,4},{6,7},{7,6},{8,9},{9,8},{10,11... | collective-permute-start | bytes 1376264 | tf_op jit(solution)/shard_map/ppermute | solution.py:63
  500.6 52.3 %collective-permute-start.52 = (bf16[7,16,2048]{2,1,0:T(8,128)(2,1)}, bf16[7,16,2048]{2,1,0:T(8,128)(2,1)S(1)}, u32[]{:S(2)}, u32[]{:S(2)}) collective-permute-start(bf16[7,16,2048]{2,1,0:T(8,128)(2,1)} %get-tuple-element.276), channel_id=1, source_target_pairs={{0,2},{1,3},{2,0},{3,1},{4,6},{5,7},{6,4},{7,5},{8,10},{9,11},{10,... | collective-permute-start | bytes 1376264 | tf_op jit(solution)/shard_map/ppermute | solution.py:63
  501.3 52.9 %collective-permute-start.53 = (bf16[7,16,2048]{2,1,0:T(8,128)(2,1)}, bf16[7,16,2048]{2,1,0:T(8,128)(2,1)S(1)}, u32[]{:S(2)}, u32[]{:S(2)}) collective-permute-start(bf16[7,16,2048]{2,1,0:T(8,128)(2,1)} %get-tuple-element.277), channel_id=1, source_target_pairs={{0,3},{1,2},{2,1},{3,0},{4,7},{5,6},{6,5},{7,4},{8,11},{9,10},{10,... | collective-permute-start | bytes 1376264 | tf_op jit(solution)/shard_map/ppermute | solution.py:63
  588.4 51.3 %collective-permute-start.55 = (bf16[6,16,2048]{2,1,0:T(8,128)(2,1)}, bf16[6,16,2048]{2,1,0:T(8,128)(2,1)S(1)}, u32[]{:S(2)}, u32[]{:S(2)}) collective-permute-start(bf16[6,16,2048]{2,1,0:T(8,128)(2,1)} %get-tuple-element.315), channel_id=1, source_target_pairs={{0,1},{1,0},{2,3},{3,2},{4,5},{5,4},{6,7},{7,6},{8,9},{9,8},{10,11... | collective-permute-start | bytes 1179656 | tf_op jit(solution)/shard_map/ppermute | solution.py:63
  588.7 53.8 %collective-permute-start.56 = (bf16[6,16,2048]{2,1,0:T(8,128)(2,1)}, bf16[6,16,2048]{2,1,0:T(8,128)(2,1)S(1)}, u32[]{:S(2)}, u32[]{:S(2)}) collective-permute-start(bf16[6,16,2048]{2,1,0:T(8,128)(2,1)} %get-tuple-element.316), channel_id=1, source_target_pairs={{0,2},{1,3},{2,0},{3,1},{4,6},{5,7},{6,4},{7,5},{8,10},{9,11},{10,... | collective-permute-start | bytes 1179656 | tf_op jit(solution)/shard_map/ppermute | solution.py:63
  591.1 51.3 %collective-permute-start.57 = (bf16[6,16,2048]{2,1,0:T(8,128)(2,1)}, bf16[6,16,2048]{2,1,0:T(8,128)(2,1)S(1)}, u32[]{:S(2)}, u32[]{:S(2)}) collective-permute-start(bf16[6,16,2048]{2,1,0:T(8,128)(2,1)} %get-tuple-element.317), channel_id=1, source_target_pairs={{0,3},{1,2},{2,1},{3,0},{4,7},{5,6},{6,5},{7,4},{8,11},{9,10},{10,... | collective-permute-start | bytes 1179656 | tf_op jit(solution)/shard_map/ppermute | solution.py:63
  609.9 45.2 %collective-permute-start.58 = (bf16[3,16,2048]{2,1,0:T(8,128)(2,1)}, bf16[3,16,2048]{2,1,0:T(8,128)(2,1)S(1)}, u32[]{:S(2)}, u32[]{:S(2)}) collective-permute-start(bf16[3,16,2048]{2,1,0:T(8,128)(2,1)} %get-tuple-element.319), channel_id=1, source_target_pairs={{0,1},{1,0},{2,3},{3,2},{4,5},{5,4},{6,7},{7,6},{8,9},{9,8},{10,11... | collective-permute-start | bytes 589832 | tf_op jit(solution)/shard_map/ppermute | solution.py:63
  (190 other events, 2811.4 us)

commit v3 on v2

--- a/solution.py
+++ b/solution.py
@@ -18,8 +18,9 @@
 BACK_VMEM = 26 * MIB
 LOAD_VMEM = 4 * MIB
 ASSEMBLE_VMEM = 16 * MIB
-FORWARD_CHUNKS = (9, 9, 7, 7)
-BACKWARD_CHUNKS = (7, 7, 9, 6, 3)
+BESIDE_VMEM = 8 * MIB
+FORWARD_CHUNKS = (7, 7, 7, 11)
+BACKWARD_CHUNKS = (5, 6, 7, 7, 5, 2)
 ANYWHERE = pl.BlockSpec(memory_space=pl.ANY)
 IN_VMEM = pl.BlockSpec(memory_space=pltpu.VMEM)
 IN_SMEM = pl.BlockSpec(memory_space=pltpu.SMEM)
@@ -113,7 +114,7 @@
                     out[index] = sources[high][high_at]
 
 
-def assemble(where, outs, ties=()):
+def assemble(where, outs, ties=(), weight_there=False):
     sources, plan = [], []
     for blocks in outs:
         entry = []
@@ -131,6 +132,8 @@
     shape, dtype = sources[0].shape[1:], sources[0].dtype
     total = len(sources) + sum(len(blocks) for blocks in outs)
     vmem = min(ASSEMBLE_VMEM, MIB + total * math.prod(shape) * 4)
+    if weight_there:
+        vmem = BESIDE_VMEM
     return pl.pallas_call(
         functools.partial(assemble_kernel, tuple(plan), len(sources), len(ties)),
         in_specs=[IN_SMEM] + [IN_VMEM] * len(sources) + [ANYWHERE] * len(ties),
@@ -170,10 +173,11 @@
 def load_kernel(count, config, *refs):
     places, sizes, units, rows_dev = config
     where, arrays = refs[0], refs[1 : 1 + count]
-    target, sems = refs[-2:]
+    target, token, sems = refs[-3:]
     copies = piece_copies(where, sizes, units, rows_dev, places, arrays, target, sems)
     for _, copy in copies:
         copy.start()
+    token[...] = jnp.zeros_like(token)
     for _, copy in copies:
         copy.wait()
 
@@ -193,19 +197,20 @@
     return pl.pallas_call(
         functools.partial(load_kernel, count, (places, sizes, shape[0], rows_dev)),
         in_specs=specs,
-        out_specs=IN_VMEM,
-        out_shape=pltpu.VMEM(shape, BF16),
+        out_specs=[IN_VMEM] * 2,
+        out_shape=[pltpu.VMEM(shape, BF16), in_hbm((8, LANES), F32)],
         input_output_aliases=aliases,
         scratch_shapes=[pltpu.SemaphoreType.DMA((total,))],
-        compiler_params=pltpu.CompilerParams(vmem_limit_bytes=MIB),
+        compiler_params=pltpu.CompilerParams(vmem_limit_bytes=STEP_VMEM),
         cost_estimate=LITTLE,
         name="load_pieces",
     )(*operands)
 
 
-def gather_weight(own, where, sizes, shape, ready, pack, seqs):
+def gather_weight(own, where, sizes, shape, ready, pack, words):
     rows_dev, block = own.shape
     half = rows_dev // 2
+    seqs = words.shape[1]
     both = own.reshape(2, half, block)
     offsets = (0, half)
 
@@ -238,11 +243,13 @@
             [(both, 0), (x1[0], 0), (z1[0], 1)],
             blocks(*arrived),
         ],
+        ready,
     )
     x2 = swap(1, (x_next, places(0, (1,)) + y1[1] + places(1, (0,))))
     y2 = swap(0, (y_next, places(0, (0,)) + x1[1] + places(1, (1,))))
     z3 = (send_units(both2, 3), places(3))
     c2 = swap(2, (c_next, all_places(*arrived)))
+    packs = [pack[0], swap_units(hold([pack[1]], [z1[0]])[0], 1)]
     found = list(arrived)
     arrived = [z3, x2, y2]
     x_next, y_next, c_next = assemble(
@@ -252,6 +259,7 @@
             [(z1[0], 0), (x2[0], 2), (z3[0], 1)],
             blocks(*arrived),
         ],
+        [c2[0], packs[1]],
     )
     x3 = swap(1, (x_next, places(1, (1,)) + y2[1][2:] + places(3, (0,))))
     y3 = swap(0, (y_next, places(1, (0,)) + x2[1][2:] + places(3, (1,))))
@@ -269,36 +277,37 @@
             blocks(*arrived) + [z2_top, z2_low],
             [z2_top, z2_low],
         ],
-        ready,
+        [c3[0]],
     )
     z2 = (z2_next, places(2))
     arrived.append(z2)
     x4 = swap(1, (x_next, places(3, (1,)) + y3[1][2:] + places(2, (0,))))
     y4 = swap(0, (y_next, places(3, (0,)) + x3[1][2:] + places(2, (1,))))
     c4 = swap(2, (c_next, all_places(*arrived)))
-    packs = [pack[0]]
-    for bits in range(1, shape[0]):
-        packs.append(swap_units(hold([pack[bits]], [z2_next])[0], bits))
+    held = hold(pack[2:], [z2_next])
+    packs += [swap_units(value, bits) for value, bits in zip(held, (2, 3))]
     found += arrived + [c3]
     arrived = [x4, y4]
     x_next, y_next, c_next = assemble(
         where,
         [[(z2[0], 1), (y4[0], 2)], [(z2[0], 0), (x4[0], 2)], blocks(*arrived)],
+        [c4[0]] + packs[2:],
     )
     x5 = swap(1, (x_next, places(2, (1,)) + y4[1][2:]))
     y5 = swap(0, (y_next, places(2, (0,)) + x4[1][2:]))
     c5 = swap(2, (c_next, all_places(*arrived)))
-    found += arrived + [c4]
-    arrived = [x5, y5]
-    (c_next,) = assemble(where, [blocks(*arrived)], packs[1:])
-    c6 = swap(2, (c_next, all_places(*arrived)))
-    found += arrived + [c5]
-    found.append(c6)
+    found += arrived[:0] + [c4]
     win_rows = pack[0].shape[0] - 2 * seqs
     others = send_rows(jnp.stack([v[:win_rows] for v in packs]), sizes, 2, 1)
-    win, hidden, cell = join_packs(where, packs, others, seqs)
-    weight = load_pieces(None, shape, where, found, sizes, rows_dev, [win])
-    return weight, win, hidden, cell
+    drive, hidden, cell = join_packs(where, packs, others, words)
+    weight, token = load_pieces(None, shape, where, found, sizes, rows_dev, [hidden])
+    found = list(arrived)
+    found += [x5, y5]
+    (c_next,) = assemble(where, [blocks(x5, y5)], [token], True)
+    c6 = swap(2, (c_next, all_places(x5, y5)))
+    weight, _ = load_pieces(weight, shape, where, found + [c5], sizes, rows_dev)
+    weight, _ = load_pieces(weight, shape, where, [c6], sizes, rows_dev)
+    return weight, drive, hidden, cell
 
 
 def load_whole_kernel(source, target, sems):
@@ -344,35 +353,43 @@
 
 def join_kernel(halves, *refs):
     where = refs[0]
-    win, hidden, cell = refs[-4:-1]
-    sems = refs[-1]
-    packs, others = refs[1:-4], ()
-    if halves == 2:
-        packs, others = refs[1:-5], refs[-5]
+    packs = refs[1:5]
+    others = refs[5] if halves == 2 else None
+    words, drive, hidden, cell, win, sems = refs[-6:]
+    step = pl.program_id(0)
     rows = win.shape[1] // halves
     width = win.shape[2] // 4
-    copies = []
-    for bits, pack in enumerate(packs):
-        z = jnp.bitwise_xor(where[1], bits)
-        first = 0 if halves == 1 else lax.rem(where[0], 2) * rows
-        to = win.at[z, pl.ds(pl.multiple_of(first, rows), rows)]
-        copies.append(pltpu.make_async_copy(pack.at[pl.ds(0, rows)], to, sems.at[len(copies)]))
-        if halves == 2:
-            to = win.at[z, pl.ds(pl.multiple_of(rows - first, rows), rows)]
-            copies.append(pltpu.make_async_copy(others.at[bits], to, sems.at[len(copies)]))
-    for copy in copies:
-        copy.start()
-    for bits, pack in enumerate(packs):
-        z = jnp.bitwise_xor(where[1], bits)
-        at = pl.ds(pl.multiple_of(z * width, width), width)
-        seqs = hidden.shape[0]
-        upper = pack[rows : rows + seqs, :].astype(F32)
-        lower = pack[rows + seqs : rows + 2 * seqs, : 2 * width].astype(F32)
-        sums = upper[:, : 2 * width] + upper[:, 2 * width :] + lower
-        hidden[:, at] = sums[:, :width]
-        cell[:, at] = sums[:, width:]
-    for copy in copies:
-        copy.wait()
+    seqs = hidden.shape[0]
+
+    @pl.when(step == 0)
+    def _():
+        copies = []
+        for bits, pack in enumerate(packs):
+            z = jnp.bitwise_xor(where[1], bits)
+            first = 0 if halves == 1 else lax.rem(where[0], 2) * rows
+            to = win.at[z, pl.ds(pl.multiple_of(first, rows), rows)]
+            copies.append(
+                pltpu.make_async_copy(pack.at[pl.ds(0, rows)], to, sems.at[len(copies)])
+            )
+            if halves == 2:
+                to = win.at[z, pl.ds(pl.multiple_of(rows - first, rows), rows)]
+                copies.append(pltpu.make_async_copy(others.at[bits], to, sems.at[len(copies)]))
+        wait_or_start("start", copies, [], None)
+        for bits, pack in enumerate(packs):
+            z = jnp.bitwise_xor(where[1], bits)
+            at = pl.ds(pl.multiple_of(z * width, width), width)
+            upper = pack[rows : rows + seqs, :].astype(F32)
+            lower = pack[rows + seqs : rows + 2 * seqs, : 2 * width].astype(F32)
+            sums = upper[:, : 2 * width] + upper[:, 2 * width :] + lower
+            hidden[:, at] = sums[:, :width]
+            cell[:, at] = sums[:, width:]
+        wait_or_start("wait", copies, [], None)
+
+    count = words.shape[0]
+    flat = words[...].reshape(count * seqs, words.shape[2])
+    for z in range(win.shape[0]):
+        part = jnp.dot(flat, win[z], preferred_element_type=F32)
+        drive[:, z] = part.reshape(count, seqs, win.shape[2])
 
 
 def pack_state(win_rows, state):
@@ -387,27 +404,36 @@
     return jnp.concatenate([win_rows, upper, lower], axis=0)
 
 
-def join_packs(where, packs, others, seqs):
+def join_packs(where, packs, others, words):
     units = len(packs)
+    window, seqs, padded = words.shape
     block = packs[0].shape[1]
     halves = 1 if others is None else 2
-    padded = halves * (packs[0].shape[0] - 2 * seqs)
     shape = (seqs, units * block // 4)
     extra = [] if others is None else [others]
+    some = 4
     return pl.pallas_call(
         functools.partial(join_kernel, halves),
-        in_specs=[IN_SMEM] + [IN_VMEM] * (units + len(extra)),
-        out_specs=[IN_VMEM] * 3,
+        grid=(window // some,),
+        in_specs=[IN_SMEM]
+        + [IN_VMEM] * (units + len(extra))
+        + [pl.BlockSpec((some, seqs, padded), lambda t: (t, 0, 0))],
+        out_specs=[pl.BlockSpec((some, units, seqs, block), lambda t: (t, 0, 0, 0))] + [IN_VMEM] * 2,
         out_shape=[
-            pltpu.VMEM((units, padded, block), BF16),
+            in_hbm((window, units, seqs, block), F32),
             jax.ShapeDtypeStruct(shape, F32),
             jax.ShapeDtypeStruct(shape, F32),
         ],
-        scratch_shapes=[pltpu.SemaphoreType.DMA((units * halves,))],
-        compiler_params=pltpu.CompilerParams(vmem_limit_bytes=8 * MIB),
+        scratch_shapes=[
+            pltpu.VMEM((units, padded, block), BF16),
+            pltpu.SemaphoreType.DMA((units * halves,)),
+        ],
+        compiler_params=pltpu.CompilerParams(
+            vmem_limit_bytes=16 * MIB, dimension_semantics=("arbitrary",)
+        ),
         cost_estimate=LITTLE,
         name="join_packs",
-    )(where, *packs, *extra)
+    )(where, *packs, *extra, words)
 
 
 def gates_of(acc, unit_width):
@@ -420,8 +446,8 @@
 
 
 def forward_kernel(start, ties, *refs):
-    lengths, embedded, hidden0, cell0, win, weight = refs[:6]
-    preact_o, cells_o, before_o, low_o, hidden, cell = refs[6 + ties :]
+    lengths, drive, hidden0, cell0, weight = refs[:5]
+    preact_o, cells_o, before_o, low_o, hidden, cell = refs[5 + ties :]
     step = pl.program_id(0)
     units, _, block = weight.shape
     unit_width = block // 4
@@ -434,11 +460,9 @@
     alive = (start + step < lengths[...]).astype(F32)
     before_o[0] = hidden[...].astype(BF16)
     low = before_o[0]
-    now = embedded[0]
     for z in range(units):
         at = slice(z * unit_width, (z + 1) * unit_width)
-        acc = jnp.dot(low, weight[z], preferred_element_type=F32)
-        acc = acc + jnp.dot(now, win[z], preferred_element_type=F32)
+        acc = drive[0, z] + jnp.dot(low, weight[z], preferred_element_type=F32)
         preact_o[0, z] = acc
         gate_in, gate_forget, gate_cell, gate_out = gates_of(acc, unit_width)
         cell_prev = cell[:, at]
@@ -456,15 +480,15 @@
     return pl.CostEstimate(flops=0, bytes_accessed=steps * 16 * MIB, transcendentals=0)
 
 
-def run_forward(lengths, embedded, hidden, cell, win, weight, start, steps, ties):
+def run_forward(lengths, drive, hidden, cell, weight, start, steps, ties):
     seqs, hidden_width = hidden.shape
-    units, _, block = win.shape
+    units, _, block = weight.shape
     stepped = lambda *shape: pl.BlockSpec((1,) + shape, lambda t: (t,) + (0,) * len(shape))
     later = lambda *shape: pl.BlockSpec((1,) + shape, lambda t: (t + start,) + (0,) * len(shape))
     return pl.pallas_call(
         functools.partial(forward_kernel, start, len(ties)),
         grid=(steps,),
-        in_specs=[IN_VMEM, later(seqs, embedded.shape[2])] + [IN_VMEM] * 4 + [ANYWHERE] * len(ties),
+        in_specs=[IN_VMEM, later(units, seqs, block)] + [IN_VMEM] * 3 + [ANYWHERE] * len(ties),
         out_specs=[
             stepped(units, seqs, block),
             stepped(seqs, hidden_width),
@@ -487,7 +511,7 @@
         cost_estimate=step_cost(steps),
         name="forward_steps",
     )(
-        lengths, keep_far(embedded), hidden, cell, keep_near(win), keep_near(weight),
+        lengths, keep_far(drive), hidden, cell, keep_near(weight),
         *ties,
     )
 
@@ -764,7 +788,7 @@
         compiler_params=pltpu.CompilerParams(vmem_limit_bytes=8 * MIB),
         cost_estimate=LITTLE,
         name="add_parts",
-    )(kept, moved, *ties)
+    )(keep_far(kept), moved, *ties)
 
 
 def sum_and_choose_kernel(axis, passed, where, mine, block, other, other_block, *refs):
@@ -825,7 +849,8 @@
 def little_kernel(spec, ties, *refs):
     dpres, refs = refs[: len(spec)], refs[len(spec) :]
     embedded, win, extras = refs[:3]
-    small, hot_sum, dpre, sems = refs[3 + ties :]
+    early, refs = refs[3 : 3 + ties[0]], refs[3 + sum(ties) :]
+    small, hot_sum, dpre, sems = refs
     copies = []
     first = 0
     for number, (rows, _) in enumerate(spec):
@@ -836,18 +861,22 @@
     wait_or_start("wait", copies, [], None)
     words = jnp.concatenate([embedded[e : e + n, :] for n, e in spec], axis=0)
     rows = hot_sum.shape[0] - EXTRA_ROWS
-    small[...], hot_sum[:rows, :] = little_sums(words, dpre[...], win[...], rows)
+    part, hot = little_sums(words, dpre[...], win[...], rows)
+    if early:
+        part, hot = part + early[0][...], hot + early[1][:rows, :]
+    small[...] = part
+    hot_sum[:rows, :] = hot
     hot_sum[rows:, :] = extras[...]
 
 
-def run_little(runs, embedded, win, extras, vocab, ties):
+def run_little(runs, embedded, win, extras, early, vocab, ties):
     spec = tuple((dpre.shape[0], word) for _, _, dpre, word in runs)
     positions = sum(n for n, _ in spec)
     block = win.shape[1]
     padded = embedded.shape[1]
     return pl.pallas_call(
-        functools.partial(little_kernel, spec, len(ties)),
-        in_specs=[ANYWHERE] * len(runs) + [IN_VMEM] * 3 + [ANYWHERE] * len(ties),
+        functools.partial(little_kernel, spec, (len(early), len(ties))),
+        in_specs=[ANYWHERE] * len(runs) + [IN_VMEM] * (3 + len(early)) + [ANYWHERE] * len(ties),
         out_specs=[IN_VMEM] * 2,
         out_shape=[in_hbm((padded, block), F32), in_hbm((vocab + EXTRA_ROWS, padded), F32)],
         scratch_shapes=[
@@ -857,7 +886,10 @@
         compiler_params=pltpu.CompilerParams(vmem_limit_bytes=24 * MIB),
         cost_estimate=LITTLE,
         name="little_gradients",
-    )(*[keep_far(run[2]) for run in runs], embedded, win, extras, *ties)
+    )(
+        *[keep_far(run[2]) for run in runs], keep_far(embedded), keep_far(win), keep_far(extras),
+        *[keep_far(v) for v in early], *ties,
+    )
 
 
 def grow_kernel(spec, mode, sizes, blocks, early, *refs):
@@ -865,6 +897,9 @@
     where = refs.pop(0)
     arrays = [[refs.pop(0) for _ in range(count)] for count, _, _, _ in spec]
     dpres = [refs.pop(0) for _ in spec]
+    if mode in ("other", "own"):
+        total_in, totals, total_sems = refs[0], refs[-2], refs[-1]
+        refs = refs[1:-2]
     column, dpre, column_sems, dpre_sems = refs[-4:]
     refs = refs[:-4]
     out, refs = refs[-1], refs[:-1]
@@ -878,7 +913,7 @@
     tile = column.shape[2]
 
     def place(index):
-        if mode == "sum":
+        if mode in ("first", "sum"):
             return index
         dy = lax.div(index, size_x)
         dx = lax.rem(index, size_x)
@@ -905,6 +940,10 @@
             else:
                 pairs.append(options)
             first += rows
+        if mode in ("other", "own"):
+            copies.append(
+                pltpu.make_async_copy(total_in.at[lanes], totals.at[slot], total_sems.at[slot])
+            )
         wait_or_start(method, copies, pairs, outer)
 
     @pl.when(step == 0)
@@ -926,7 +965,8 @@
         column_copies("start", step + 1)
 
     if mode != "own":
-        embedded, win, small_in, hot_in = refs[:4]
+        embedded, win = refs[:2]
+        small_in, hot_in = refs[2:4] if mode != "first" else (None, None)
         small, hot_sum = refs[-2:]
 
         @pl.when(step == 0)
@@ -939,24 +979,33 @@
             words = jnp.concatenate(words, axis=0)
             rows = hot_sum.shape[0] - EXTRA_ROWS
             part, hot = little_sums(words, dpre[early:, :], win[...], rows)
-            small[...] = part + small_in[...]
-            hot_sum[:rows, :] = hot + hot_in[:rows, :]
-            hot_sum[rows:, :] = hot_in[rows:, :]
+            if small_in is None:
+                small[...] = part
+                hot_sum[:rows, :] = hot
+                hot_sum[rows:, :] = jnp.zeros((EXTRA_ROWS, LANES), F32)
+            else:
+                small[...] = part + small_in[...]
+                hot_sum[:rows, :] = hot + hot_in[:rows, :]
+                hot_sum[rows:, :] = hot_in[rows:, :]
     else:
         small = refs[0]
 
     column_copies("wait", step)
-    part = contract(column[lax.rem(step, 2)], dpre[...], 0, 0)
-    if mode == "sum":
+    slot = lax.rem(step, 2)
+    part = contract(column[slot], dpre[...], 0, 0)
+    if mode in ("first", "sum"):
         out[...] = part
     else:
+        part = part + totals[slot]
         small_tile = out.shape[1] - tile
         small_at = pl.multiple_of(place(step) * small_tile, small_tile)
         out[0, :tile, :] = part.astype(out.dtype)
         out[0, tile:, :] = small[pl.ds(small_at, small_tile), :].astype(out.dtype)
 
 
-def run_grow(where, runs, early, embedded, win, little, mode, sizes, rows_dev):
+def run_grow(
+    where, runs, early, embedded, win, little, total, mode, sizes, rows_dev, vocab, ties, beside=None
+):
     spec, arrays, dpres = [], [], []
     for choices, row, dpre, word in runs:
         spec.append((len(choices), row, dpre.shape[0], word))
@@ -966,18 +1015,25 @@
     block, hidden_width = dpres[0].shape[1], runs[0][0][0].shape[-1]
     padded = embedded.shape[1]
     near = sizes[0] * sizes[1]
-    tile = 256 if mode == "sum" else rows_dev
-    blocks = hidden_width // tile if mode == "sum" else near
+    stays = [] if beside is None else [keep_near(beside)]
+    whole = mode in ("first", "sum")
+    tile = 256 if whole else rows_dev
+    blocks = hidden_width // tile if whole else near
     operands = [where] + arrays + dpres
     specs = [IN_SMEM] + [ANYWHERE] * (len(operands) - 1)
+    scratch = []
+    if not whole:
+        operands.append(keep_far(total))
+        specs.append(ANYWHERE)
+        scratch = [pltpu.VMEM((2, tile, block), F32), pltpu.SemaphoreType.DMA((2,))]
     if mode == "own":
-        more = [little[0]]
+        more = [keep_far(little[0])]
         out_shape, out_specs = [], []
     else:
-        more = [embedded, win] + list(little)
-        out_shape = [in_hbm(v.shape, F32) for v in little]
+        more = [keep_far(v) for v in [embedded, win] + list(little or [])]
+        out_shape = [in_hbm((padded, block), F32), in_hbm((vocab + EXTRA_ROWS, LANES), F32)]
         out_specs = [IN_VMEM] * 2
-    if mode == "sum":
+    if whole:
         out_shape.append(in_hbm((hidden_width, block), F32))
         out_specs.append(pl.BlockSpec((tile, block), lambda i: (i, 0)))
     else:
@@ -988,7 +1044,7 @@
     return pl.pallas_call(
         functools.partial(grow_kernel, tuple(spec), mode, sizes, blocks, early),
         grid=(blocks,),
-        in_specs=specs + [IN_VMEM] * len(more),
+        in_specs=specs + [IN_VMEM] * len(more) + [ANYWHERE] * len(ties) + [IN_VMEM] * len(stays),
         out_specs=out_specs,
         out_shape=out_shape,
         scratch_shapes=[
@@ -996,13 +1052,15 @@
             pltpu.VMEM((positions, block), BF16),
             pltpu.SemaphoreType.DMA((2, len(spec))),
             pltpu.SemaphoreType.DMA((len(spec),)),
-        ],
+        ]
+        + scratch,
         compiler_params=pltpu.CompilerParams(
-            vmem_limit_bytes=28 * MIB, dimension_semantics=("arbitrary",)
+            vmem_limit_bytes=(STEP_VMEM if mode == "first" else 32 * MIB),
+            dimension_semantics=("arbitrary",),
         ),
         cost_estimate=LITTLE,
         name="weight_gradient",
-    )(*operands, *more)
+    )(*operands, *more, *ties, *stays)
 
 
 def first_sum_kernel(kept, moved, send_a, keep_a, send_b, keep_b):
@@ -1102,12 +1160,12 @@
         at = slice(gate * width, (gate + 1) * width)
         grad[:, gate, :] = held[:rows, at]
         bias[gate : gate + 1, :] = held[rows : rows + 1, at]
-    vocab = decoder.shape[1]
+    vocab = decoder.shape[0]
     half = mine.shape[1]
     me_c = lax.rem(where[0], 2)
     for block, place in ((mine, me_c), (other, 1 - me_c)):
         at = pl.ds(pl.multiple_of(place * half, half), half)
-        decoder[at, :] = block[...].astype(F32).T[:, :vocab]
+        decoder[:, at] = block[...].astype(F32)[:vocab, :]
     pack = packed[...]
     embedding[...] = pack[:vocab, : embedding.shape[1]]
     first = packed.shape[0] - EXTRA_ROWS
@@ -1140,7 +1198,7 @@
             jax.ShapeDtypeStruct((vocab, embed_width), F32),
             jax.ShapeDtypeStruct((rows, 4, unit_width), F32),
             jax.ShapeDtypeStruct((4, unit_width), F32),
-            jax.ShapeDtypeStruct((unit_width, vocab), F32),
+            jax.ShapeDtypeStruct((vocab, unit_width), F32),
             jax.ShapeDtypeStruct((1, vocab), F32),
         ],
         scratch_shapes=[pltpu.VMEM((8 * tile, block), F32)],
@@ -1165,44 +1223,42 @@
 
 
 def join_ends_kernel(count, *refs):
-    where, pieces, (mine, other) = refs[0], refs[1:5], refs[5:7]
-    outs, total = refs[-1 - count : -1], refs[-1]
+    where, pieces, outs = refs[0], refs[1:5], refs[-count:]
     seqs = outs[0].shape[0] // len(pieces)
     for bits, piece in enumerate(pieces):
         z = jnp.bitwise_xor(where[1], bits)
         at = pl.ds(pl.multiple_of(z * seqs, seqs), seqs)
         for index, out in enumerate(outs):
             out[at, :] = piece[index * seqs : (index + 1) * seqs, :]
-    total[...] = mine[...] + other[...]
-
-
-def exchange_ends(where, arrays, packed, ties=()):
-    units = 4
+
+
+def cut_ends(where, arrays, units, ties):
     seqs, hidden_width = arrays[0].shape
     count = len(arrays)
     width = hidden_width // units
-    pieces = pl.pallas_call(
+    return pl.pallas_call(
         functools.partial(cut_ends_kernel, count),
-        in_specs=[IN_SMEM] + [ANYWHERE] * count,
+        in_specs=[IN_SMEM] + [ANYWHERE] * (count + len(ties)),
         out_specs=[IN_VMEM] * units,
         out_shape=[jax.ShapeDtypeStruct((count * seqs, width), F32)] * units,
         scratch_shapes=[pltpu.SemaphoreType.DMA((units, count))],
         compiler_params=pltpu.CompilerParams(vmem_limit_bytes=4 * MIB),
         cost_estimate=LITTLE,
         name="cut_ends",
-    )(where, *[keep_far(v) for v in arrays])
-    pieces = [pieces[0]] + [swap_units(pieces[bits], bits) for bits in range(1, units)]
-    out = pl.pallas_call(
+    )(where, *[keep_far(v) for v in arrays], *ties)
+
+
+def join_ends(where, pieces, count, ties):
+    rows, width = pieces[0].shape
+    return pl.pallas_call(
         functools.partial(join_ends_kernel, count),
-        in_specs=[IN_SMEM] + [IN_VMEM] * (units + 2) + [ANYWHERE] * len(ties),
-        out_specs=[IN_VMEM] * (count + 1),
-        out_shape=[jax.ShapeDtypeStruct((units * seqs, width), F32)] * count
-        + [jax.ShapeDtypeStruct(packed.shape, F32)],
+        in_specs=[IN_SMEM] + [IN_VMEM] * len(pieces) + [ANYWHERE] * len(ties),
+        out_specs=[IN_VMEM] * count,
+        out_shape=[jax.ShapeDtypeStruct((len(pieces) * rows // count, width), F32)] * count,
         compiler_params=pltpu.CompilerParams(vmem_limit_bytes=4 * MIB),
         cost_estimate=LITTLE,
         name="join_ends",
-    )(where, *pieces, packed, swap_units(packed, 2), *ties)
-    return out[:count], out[count]
+    )(where, *pieces, *ties)
 
 
 def show_kernel(chunks, window, *refs):
@@ -1345,13 +1401,13 @@
         )
     pack = [pack_state(win_rows, share(states, bits, 1)) for bits in range(units)]
     if square:
-        weight, win, hidden, cell = gather_weight(
-            own_weight, where, sizes, shape, ready + pack, pack, seqs
+        weight, drive, hidden, cell = gather_weight(
+            own_weight, where, sizes, shape, ready + pack, pack, embedded_own
         )
     else:
         weight = load_whole(lax.all_gather(own_weight, ("units", "rows"), axis=0), shape)
         packs = [pack[0]] + [swap_units(pack[bits], bits) for bits in others]
-        win, hidden, cell = join_packs(where, packs, None, seqs)
+        drive, hidden, cell = join_packs(where, packs, None, embedded_own)
 
     start = 0
     chunks = []
@@ -1391,7 +1447,7 @@
     count = len(FORWARD_CHUNKS)
     for number, steps in enumerate(FORWARD_CHUNKS):
         preact, cells, before, low, hidden, cell = run_forward(
-            lengths_own, embedded_own, hidden, cell, win, weight, start, steps,
+            lengths_own, drive, hidden, cell, weight, start, steps,
             due(("forward", number - 2)),
         )
         before = before.reshape(steps * seqs, hidden_width)
@@ -1417,6 +1473,7 @@
         started["decoder"].append(moved)
 
     grads = None
+    first_little, total = [], None
     end = window
     dpres = []
     pairs = []
@@ -1440,6 +1497,12 @@
             1: [("forward", count - 1), "decoder"],
         }.get(number, [("backward", number - 2)])
         ties = due(*names) + ([decoder_kept] if square and number in (1, 2) else [])
+        if square and number == len(BACKWARD_CHUNKS) - 1:
+            *first_little, total = run_grow(
+                where, runs_of(range(number - 2)), 0, embedded, win_own, None, None, "first", sizes,
+                rows_dev, vocab_rows, [grads[0]], turned,
+            )
+            ties = ties + [total]
         out = run_backward(
             where, lengths_own, preact, cells, offset, back_grad, grads, turned, first, steps, ties
         )
@@ -1468,48 +1531,58 @@
     where, embedded, win_own = flat[6 * count :]
 
     number = len(BACKWARD_CHUNKS) - 1
-    runs = runs_of(range(number + 1))
-    early = units * (window - BACKWARD_CHUNKS[-1]) * seqs
+    late = range(number - 2 if square else 0, number + 1)
+    runs = runs_of(late)
+    early = units * sum(BACKWARD_CHUNKS[n] for n in late[:-1]) * seqs
     little = run_little(
-        runs_of(range(number)), embedded, win_own, extras, vocab_rows, [grads[0]]
-    )
-
-    def grow(little, mode):
-        return run_grow(where, runs, early, embedded, win_own, little, mode, sizes, rows_dev)
-
-    late_arrays = [where, final_hidden, final_cell] + list(grads)
+        runs_of(late[:-1]), embedded, win_own, extras, first_little, vocab_rows, [grads[0]]
+    )
+
+    def grow(little, mode, ties=()):
+        return run_grow(
+            where, runs, early, embedded, win_own, little, total, mode, sizes, rows_dev, vocab_rows,
+            ties,
+        )
+
+    late_arrays = [final_hidden, final_cell] + list(grads)
+    pieces = cut_ends(where, late_arrays, units, [little[0]])
+
+    def join(ties):
+        moved = [swap_units(pieces[bits], bits) for bits in others]
+        return join_ends(where, [pieces[0]] + moved, len(late_arrays), ties)
 
     def show(tie, last):
         (here,) = hold([where], [tie])
         return show_hidden(here, last, befores, FORWARD_CHUNKS, seqs)
 
     if square:
-        small, hot_sum, sent = grow(little, "other")
+        small, hot_sum, sent = grow(little, "other", [pieces[0]])
         (kept,) = grow([small], "own")
-        hot_sum = hot_sum + swap_units(hot_sum, 1)
+        ends = join([kept])
 
         def finish(tie):
-            flat = hold(late_arrays + [decoder_kept, moved], [tie])
-            block, kept = add_parts(flat[5], flat[6])
-            across = swap_units(block, 1)
-            block, kept = add_parts(kept, across)
-            ends, packed = exchange_ends(flat[0], flat[1:5], hot_sum, [block])
+            flat = hold([hot_sum, decoder_kept, moved], [tie])
+            block, kept = add_parts(flat[1], flat[2])
+            packed = flat[0] + swap_units(flat[0], 1)
+            block, kept = add_parts(kept, swap_units(block, 1))
+            packed = packed + swap_units(packed, 2)
             packed = packed + send_rows(packed, sizes, 2, 1)
             block_sum, _ = add_parts(kept, swap_units(block, 2))
-            return (ends, packed, block_sum), [packed, block_sum]
+            return (packed, block_sum), [packed, block_sum]
 
         def show_last(tie, done):
-            shown = show(tie, done[0][0])
-            return shown, [shown]
-
-        recurrent_grad, small, (ends, packed, block_sum), hidden_out = reduce_rows(
-            kept, sent, sizes, rows_dev, [finish, show_last], [hot_sum]
+            shown = show(tie, ends[0])
+            return shown, [keep_far(shown)]
+
+        recurrent_grad, small, (packed, block_sum), hidden_out = reduce_rows(
+            kept, sent, sizes, rows_dev, [finish, show_last], [ends[0]]
         )
         packed, block_sum = hold([packed, block_sum], [small])
         total_loss, embed_grad, input_grad, bias_grad, decoder_out, decoder_bias_grad = spread_small(
             where, small, block_sum, packed, sizes, embed_width, embedding.shape
         )
-        total_loss, decoder_bias_grad = total_loss[0, 0], decoder_bias_grad[0]
+        total_loss = total_loss.reshape(())
+        decoder_out, decoder_bias_grad = decoder_out.T, decoder_bias_grad.reshape(vocab_size)
     else:
         small, hot_sum, total = grow(little, "sum")
         recurrent_grad = lax.psum_scatter(
@@ -1519,8 +1592,7 @@
         small = lax.psum(small, "rows")
         input_grad = small[:embed_width].reshape(embed_width, 4, unit_width)
         bias_grad = small[embed_width].reshape(4, unit_width)
-        flat = hold(late_arrays, [total])
-        ends, _ = exchange_ends(flat[0], flat[1:], hot_sum)
+        ends = join([total])
         hidden_out = show(total, ends[0])
         decoder_out = lax.psum(decoder_kept, ("rows", "units"))
         decoder_out = lax.dynamic_slice_in_dim(decoder_out, me_z * unit_width, unit_width, 0)

time: 780 us -> 751 us (0.963)
  starting transfers between devices: 146 us -> 108 us
  Pallas kernels: 413 us -> 439 us
  local copies, waits for them, and re-layouts: 60.2 us -> 45.9 us
    ppermute x29 -> x32, waiting for transfers between devices: 33.1 us -> 75.1 us  [swap_units(): return lax.ppermute(value, 'units', [(z, z ^ bits) for z in range(count)])]
    ppermute x29 -> x32, starting transfers between devices: 93.5 us -> 57 us  [swap_units(): return lax.ppermute(value, 'units', [(z, z ^ bits) for z in range(count)])]
    ppermute x37, waiting for transfers between devices: 66.4 us -> 30.9 us  [send_rows(): return lax.ppermute(value, 'rows', row_shift(sizes, axis, step))]
    ppermute x2, waiting for transfers between devices: 28.5 us -> 2.3 us  [send_units(): lax.ppermute(value, 'units', [(z, (z + step) % count) for z in range(coun...]
    unnamed x263 -> x223, local copies, waits for them, and re-layouts: 46.1 us -> 31.7 us
    pallas_call x2 -> x3, Pallas kernels: 31 us -> 44.2 us  [run_grow(): pl.pallas_call(functools.partial(grow_kernel, tuple(spec), mode, sizes, b...]
    pallas_call x1 -> x3, Pallas kernels: 7.86 us -> 17 us  [load_pieces(): pl.pallas_call(functools.partial(load_kernel, count, (places, sizes, shap...]
    ppermute x1, waiting for transfers between devices: 17 us -> 26.1 us  [gather_weight(): down = lax.ppermute(z3[0], 'units', [(2, 1), (1, 0)])]
  transfers between devices with their start and end apart: 86 -> 89, of which waited for: 31 -> 30; matrix products, arithmetic and copies ran while one was open for 3% -> 3% of each run, Pallas kernels for 43% -> 51%
where the time goes in v3:
time: 751 us; the launch traced here: 744 us
  Pallas kernels  439 us (58%)
  waiting for transfers between devices  141 us (19%)
  starting transfers between devices  108 us (14%)
  local copies, waits for them, and re-layouts  45.9 us (6%)
    pallas_call x6, Pallas kernels, run_backward(): pl.pallas_call(functools.partial(backward_kernel, first_step, steps, len(...  159 us
    pallas_call x4, Pallas kernels, run_forward(): pl.pallas_call(functools.partial(forward_kernel, start, len(ties)), grid=...  152 us
    ppermute x32, waiting for transfers between devices, swap_units(): return lax.ppermute(value, 'units', [(z, z ^ bits) for z in range(count)])  75.1 us
    ppermute x32, starting transfers between devices, swap_units(): return lax.ppermute(value, 'units', [(z, z ^ bits) for z in range(count)])  57 us
    pallas_call x3, Pallas kernels, run_grow(): pl.pallas_call(functools.partial(grow_kernel, tuple(spec), mode, sizes, b...  44.2 us
    unnamed x223, local copies, waits for them, and re-layouts  31.7 us
    ppermute x37, waiting for transfers between devices, send_rows(): return lax.ppermute(value, 'rows', row_shift(sizes, axis, step))  30.9 us
    ppermute x37, starting transfers between devices, send_rows(): return lax.ppermute(value, 'rows', row_shift(sizes, axis, step))  27.1 us
  transfers between devices with their start and end apart: 89, of which 30 were waited for; matrix products, arithmetic and copies ran while one was open for 3% of the time, Pallas kernels for 51%

profile of v3, /device:TPU:0, one launch (start us, length us, event | category | flops | bytes accessed | tf_op | source)
XLA Modules:
  0.0 743.5 jit_solution(16173491659715209899)
XLA Ops:
  38.2 31.3 %collective-permute-done.1.refs_6_.refs_2_ = bf16[96,2048]{1,0:T(8,128)(2,1)S(1)} collective-permute-done((bf16[96,2048]{1,0:T(8,128)(2,1)}, bf16[96,2048]{1,0:T(8,128)(2,1)S(1)}, u32[]{:S(2)}, u32[]{:S(2)}) %collective-permute-start.1) | collective-permute-done | bytes 393248 | tf_op jit(solution)/shard_map/ppermute | solution.py:64
  77.6 26.1 %collective-permute-done.9.refs_3_ = bf16[2,128,2048]{2,1,0:T(8,128)(2,1)S(1)} collective-permute-done((bf16[2,128,2048]{2,1,0:T(8,128)(2,1)S(1)}, bf16[2,128,2048]{2,1,0:T(8,128)(2,1)S(1)}, u32[]{:S(2)}, u32[]{:S(2)}) %collective-permute-start.9) | collective-permute-done | bytes 1048608 | tf_op jit(solution)/shard_map/ppermute | solution.py:267
  103.7 6.4 collective-permute-done.11.refs_5_.refs_9_
  117.5 10.4 %collective-permute-done.14.refs_4_.refs_6_ = bf16[96,2048]{1,0:T(8,128)(2,1)S(1)} collective-permute-done((bf16[96,2048]{1,0:T(8,128)(2,1)}, bf16[96,2048]{1,0:T(8,128)(2,1)S(1)}, u32[]{:S(2)}, u32[]{:S(2)}) %collective-permute-start.14) | collective-permute-done | bytes 393248 | tf_op jit(solution)/shard_map/ppermute | solution.py:64
  128.0 22.7 %collective-permute-done.13.refs_3_.refs_5_ = bf16[96,2048]{1,0:T(8,128)(2,1)S(1)} collective-permute-done((bf16[96,2048]{1,0:T(8,128)(2,1)}, bf16[96,2048]{1,0:T(8,128)(2,1)S(1)}, u32[]{:S(2)}, u32[]{:S(2)}) %collective-permute-start.13) | collective-permute-done | bytes 393248 | tf_op jit(solution)/shard_map/ppermute | solution.py:64
  158.7 8.8 %join_packs.1 = (f32[32,4,16,2048]{3,2,1,0:T(8,128)}, f32[16,2048]{1,0:T(8,128)S(1)}, f32[16,2048]{1,0:T(8,128)S(1)}) custom-call(s32[2]{0:T(128)S(1)} %pad_add_fusion.1.refs_0_.refs_24_, bf16[96,2048]{1,0:T(8,128)(2,1)S(1)} %get-tuple-element.409.refs_13_.refs_1_, bf16[96,2048]{1,0:T(8,128)(2,1)S(1)} %collective-permute-done.1.refs_6_.refs_2_, ...), custom_call_target="tpu_custom_call" | custom-call | bytes 1024 | tf_op jit(solution)/shard_map/join_packs/pallas_call | solution.py:415
  168.8 9.4 %load_pieces.3 = (bf16[4,2048,2048]{2,1,0:T(8,128)(2,1)S(1)}, f32[8,128]{1,0:T(8,128)}) custom-call(s32[2]{0:T(128)} %copy-done.64, bf16[2,128,2048]{2,1,0:T(8,128)(2,1)} %copy-done.15, bf16[2,128,2048]{2,1,0:T(8,128)(2,1)} %copy-done.12, bf16[1,128,2048]{2,1,0:T(8,128)(2,1)} %collective-permute-done.3.refs_4_.refs_3_, ...), custom_call_target="tpu_custom_call" | custom-call | bytes 1024 | tf_op jit(solution)/shard_map/load_pieces/pallas_call | solution.py:197
  192.1 33.5 %forward_steps.4 = (f32[7,4,16,2048]{3,2,1,0:T(8,128)}, f32[7,16,2048]{2,1,0:T(8,128)}, bf16[7,16,2048]{2,1,0:T(8,128)(2,1)}, bf16[7,16,2048]{2,1,0:T(8,128)(2,1...) custom-call(s32[16,1]{1,0:T(8,128)} %copy-done.55, f32[32,4,16,2048]{3,2,1,0:T(8,128)} %get-tuple-element.217.refs_1_, ...), custom_call_target="tpu_custom_call" | custom-call | bytes 117440512 | tf_op jit(solution)/shard_map/forward_steps/pallas_call | solution.py:488
  227.5 33.5 %forward_steps.5 = (f32[7,4,16,2048]{3,2,1,0:T(8,128)}, f32[7,16,2048]{2,1,0:T(8,128)}, bf16[7,16,2048]{2,1,0:T(8,128)(2,1)}, bf16[7,16,2048]{2,1,0:T(8,128)(2,1...) custom-call(s32[16,1]{1,0:T(8,128)} %copy-done.55, f32[32,4,16,2048]{3,2,1,0:T(8,128)} %get-tuple-element.217.refs_1_, ...), custom_call_target="tpu_custom_call" | custom-call | bytes 117440512 | tf_op jit(solution)/shard_map/forward_steps/pallas_call | solution.py:488
  265.1 6.5 collective-permute-start.23
  272.5 33.5 %forward_steps.6 = (f32[7,4,16,2048]{3,2,1,0:T(8,128)}, f32[7,16,2048]{2,1,0:T(8,128)}, bf16[7,16,2048]{2,1,0:T(8,128)(2,1)}, bf16[7,16,2048]{2,1,0:T(8,128)(2,1...) custom-call(s32[16,1]{1,0:T(8,128)} %copy-done.55, f32[32,4,16,2048]{3,2,1,0:T(8,128)} %get-tuple-element.217.refs_1_, ...), custom_call_target="tpu_custom_call" | custom-call | bytes 117440512 | tf_op jit(solution)/shard_map/forward_steps/pallas_call | solution.py:488
  314.6 51.5 %forward_steps.7 = (f32[11,4,16,2048]{3,2,1,0:T(8,128)}, f32[11,16,2048]{2,1,0:T(8,128)}, bf16[11,16,2048]{2,1,0:T(8,128)(2,1)}, bf16[11,16,2048]{2,1,0:T(8,128)...) custom-call(s32[16,1]{1,0:T(8,128)} %copy-done.55, f32[32,4,16,2048]{3,2,1,0:T(8,128)} %get-tuple-element.217.refs_1_, ...), custom_call_target="tpu_custom_call" | custom-call | bytes 184549376 | tf_op jit(solution)/shard_map/forward_steps/pallas_call | solution.py:488
  376.3 15.8 %decoder.1 = (bf16[4,2048,2048]{2,1,0:T(8,128)(2,1)S(1)}, bf16[512,2048]{1,0:T(8,128)(2,1)}, f32[8,128]{1,0:T(8,128)}, bf16[4,288,256]{2,1,0:T(8,128)(2,1)}, f32[4,288,256]{2,1,0:T(8,128)}) custom-call(s32[2]{0:T(128)} %copy-done.64, f32[1,384]{1,0:T(1,128)} %copy-done.69, s32[512,1]{1,0:T(8,128)} %reshape.344.refs_8_.refs_2_, ...), custom_call_target="tpu_custom_call", output_to_operand_aliasing={{0}: (14, {})} | custom-call | tf_op jit(solution)/shard_map/decoder/pallas_call | solution.py:739
  401.5 24.8 %backward_steps.6 = (bf16[5,16,2048]{2,1,0:T(8,128)(2,1)}, bf16[5,16,2048]{2,1,0:T(8,128)(2,1)}, bf16[5,16,2048]{2,1,0:T(8,128)(2,1)}, bf16[5,16,2048]{2,1,0:T(8...) custom-call(s32[2]{0:T(128)} %copy-done.64, s32[16,1]{1,0:T(8,128)} %copy-done.55, ...), custom_call_target="tpu_custom_call" | custom-call | bytes 83886080 | tf_op jit(solution)/shard_map/backward_steps/pallas_call | solution.py:576
  429.9 6.7 collective-permute-start.48
  449.6 29.5 %backward_steps.7 = (bf16[6,16,2048]{2,1,0:T(8,128)(2,1)}, bf16[6,16,2048]{2,1,0:T(8,128)(2,1)}, bf16[6,16,2048]{2,1,0:T(8,128)(2,1)}, bf16[6,16,2048]{2,1,0:T(8...) custom-call(s32[2]{0:T(128)} %copy-done.64, s32[16,1]{1,0:T(8,128)} %copy-done.55, ...), custom_call_target="tpu_custom_call" | custom-call | bytes 100663296 | tf_op jit(solution)/shard_map/backward_steps/pallas_call | solution.py:576
  486.6 34.2 %backward_steps.8 = (bf16[7,16,2048]{2,1,0:T(8,128)(2,1)}, bf16[7,16,2048]{2,1,0:T(8,128)(2,1)}, bf16[7,16,2048]{2,1,0:T(8,128)(2,1)}, bf16[7,16,2048]{2,1,0:T(8...) custom-call(s32[2]{0:T(128)} %copy-done.64, s32[16,1]{1,0:T(8,128)} %copy-done.55, ...), custom_call_target="tpu_custom_call" | custom-call | bytes 117440512 | tf_op jit(solution)/shard_map/backward_steps/pallas_call | solution.py:576
  527.3 34.3 %backward_steps.9 = (bf16[7,16,2048]{2,1,0:T(8,128)(2,1)}, bf16[7,16,2048]{2,1,0:T(8,128)(2,1)}, bf16[7,16,2048]{2,1,0:T(8,128)(2,1)}, bf16[7,16,2048]{2,1,0:T(8...) custom-call(s32[2]{0:T(128)} %copy-done.64, s32[16,1]{1,0:T(8,128)} %copy-done.55, ...), custom_call_target="tpu_custom_call" | custom-call | bytes 117440512 | tf_op jit(solution)/shard_map/backward_steps/pallas_call | solution.py:576
  567.0 24.9 %backward_steps.10 = (bf16[5,16,2048]{2,1,0:T(8,128)(2,1)}, bf16[5,16,2048]{2,1,0:T(8,128)(2,1)}, bf16[5,16,2048]{2,1,0:T(8,128)(2,1)}, bf16[5,16,2048]{2,1,0:T(...) custom-call(s32[2]{0:T(128)} %copy-done.64, s32[16,1]{1,0:T(8,128)} %copy-done.55, ...), custom_call_target="tpu_custom_call" | custom-call | bytes 83886080 | tf_op jit(solution)/shard_map/backward_steps/pallas_call | solution.py:576
  596.4 22.5 %weight_gradient.3 = (f32[128,2048]{1,0:T(8,128)}, f32[288,128]{1,0:T(8,128)}, f32[2048,2048]{1,0:T(8,128)}) custom-call(s32[2]{0:T(128)} %copy-done.64, bf16[176,2048]{1,0:T(8,128)(2,1)} %bitcast.146, bf16[176,2048]{1,0:T(8,128)(2,1)} %get-tuple-element.268.refs_1_.refs_6_.refs_2_.refs_8_.refs_19_, ...), custom_call_target="tpu_custom_call" | custom-call | bytes 1024 | tf_op jit(solution)/shard_map/weight_gradient/pallas_call | solution.py:1044
  619.8 11.1 %backward_steps.11 = (bf16[2,16,2048]{2,1,0:T(8,128)(2,1)}, bf16[2,16,2048]{2,1,0:T(8,128)(2,1)}, bf16[2,16,2048]{2,1,0:T(8,128)(2,1)}, bf16[2,16,2048]{2,1,0:T(...) custom-call(s32[2]{0:T(128)} %copy-done.64, s32[16,1]{1,0:T(8,128)} %copy-done.55, ...), custom_call_target="tpu_custom_call" | custom-call | bytes 33554432 | tf_op jit(solution)/shard_map/backward_steps/pallas_call | solution.py:576
  637.3 7.6 %little_gradients.1 = (f32[128,2048]{1,0:T(8,128)}, f32[288,128]{1,0:T(8,128)}) custom-call(bf16[112,2048]{1,0:T(8,128)(2,1)} %bitcast.161, bf16[112,2048]{1,0:T(8,128)(2,1)} %bitcast.152, bf16[112,2048]{1,0:T(8,128)(2,1)} %bitcast.155, bf16[112,2048]{1,0:T(8,128)(2,1)} %bitcast.158, bf16[80,2048]{1,0:T(8,128)(2,1)} %bitcast.168, ...), custom_call_target="tpu_custom_call" | custom-call | bytes 1024 | tf_op jit(solution)/shard_map/little_gradients/pallas_call | solution.py:877
  648.6 11.3 %weight_gradient.4 = (f32[128,2048]{1,0:T(8,128)}, f32[288,128]{1,0:T(8,128)}, bf16[4,272,2048]{2,1,0:T(8,128)(2,1)S(1)}) custom-call(s32[2]{0:T(128)S(1)} %copy-done.66, bf16[112,2048]{1,0:T(8,128)(2,1)} %get-tuple-element.310.refs_1_.refs_8_, bf16[112,2048]{1,0:T(8,128)(2,1)} %get-tuple-element.311.refs_2_.refs_9_, ...), custom_call_target="tpu_custom_call" | custom-call | bytes 1024 | tf_op jit(solution)/shard_map/weight_gradient/pallas_call | solution.py:1044
  664.4 10.5 %weight_gradient.5.refs_5_.refs_0_ = f32[4,272,2048]{2,1,0:T(8,128)S(1)} custom-call(s32[2]{0:T(128)S(1)} %copy-done.66, bf16[112,2048]{1,0:T(8,128)(2,1)} %get-tuple-element.310.refs_1_.refs_8_, bf16[112,2048]{1,0:T(8,128)(2,1)} %get-tuple-element.311.refs_2_.refs_9_, bf16[112,2048]{1,0:T(8,128)(2,1)} %get-tuple-element.312.refs_3_.refs_11_, ...), custom_call_target="tpu_custom_call" | custom-call | bytes 1024 | tf_op jit(solution)/shard_map/weight_gradient/pallas_call | solution.py:1044
  (480 shorter events, 234.0 us)
Async XLA Ops:
  263.1 46.1 %collective-permute-start.27 = (bf16[192,2048]{1,0:T(8,128)(2,1)}, bf16[192,2048]{1,0:T(8,128)(2,1)S(1)}, u32[]{:S(2)}, u32[]{:S(2)}) collective-permute-start(bf16[192,2048]{1,0:T(8,128)(2,1)} %get-tuple-element.235.refs_5_.refs_2_), channel_id=1, source_target_pairs={{1,2},{2,1},{5,6},{6,5},{9,10},{10,9},{13,14},{14,13},{17,18},{18,... | collective-permute-start | bytes 2359304 | tf_op jit(solution)/shard_map/ppermute | solution.py:1440
  263.8 45.4 %collective-permute-start.28 = (bf16[192,2048]{1,0:T(8,128)(2,1)}, bf16[192,2048]{1,0:T(8,128)(2,1)S(1)}, u32[]{:S(2)}, u32[]{:S(2)}) collective-permute-start(bf16[192,2048]{1,0:T(8,128)(2,1)} %get-tuple-element.236.refs_6_.refs_3_), channel_id=1, source_target_pairs={{1,0},{2,3},{5,4},{6,7},{9,8},{10,11},{13,12},{14,15},{17,16},{18,... | collective-permute-start | bytes 2359304 | tf_op jit(solution)/shard_map/ppermute | solution.py:1441
  265.1 43.4 %collective-permute-start.23 = (bf16[112,2048]{1,0:T(8,128)(2,1)}, bf16[112,2048]{1,0:T(8,128)(2,1)S(1)}, u32[]{:S(2)}, u32[]{:S(2)}) collective-permute-start(bf16[112,2048]{1,0:T(8,128)(2,1)} %bitcast.149), channel_id=1, source_target_pairs={{0,1},{1,0},{2,3},{3,2},{4,5},{5,4},{6,7},{7,6},{8,9},{9,8},{10,11... | collective-permute-start | bytes 1376264 | tf_op jit(solution)/shard_map/ppermute | solution.py:64
  306.0 60.1 %collective-permute-start.30 = (bf16[112,2048]{1,0:T(8,128)(2,1)}, bf16[112,2048]{1,0:T(8,128)(2,1)S(1)}, u32[]{:S(2)}, u32[]{:S(2)}) collective-permute-start(bf16[112,2048]{1,0:T(8,128)(2,1)} %bitcast.164), channel_id=1, source_target_pairs={{0,1},{1,0},{2,3},{3,2},{4,5},{5,4},{6,7},{7,6},{8,9},{9,8},{10,11... | collective-permute-start | bytes 1376264 | tf_op jit(solution)/shard_map/ppermute | solution.py:64
  308.5 62.3 %collective-permute-start.31 = (bf16[112,2048]{1,0:T(8,128)(2,1)}, bf16[112,2048]{1,0:T(8,128)(2,1)S(1)}, u32[]{:S(2)}, u32[]{:S(2)}) collective-permute-start(bf16[112,2048]{1,0:T(8,128)(2,1)} %bitcast.165), channel_id=1, source_target_pairs={{1,2},{2,1},{5,6},{6,5},{9,10},{10,9},{13,14},{14,13},{17,18},{18,... | collective-permute-start | bytes 1376264 | tf_op jit(solution)/shard_map/ppermute | solution.py:1438
  311.3 60.2 %collective-permute-start.32 = (bf16[112,2048]{1,0:T(8,128)(2,1)}, bf16[112,2048]{1,0:T(8,128)(2,1)S(1)}, u32[]{:S(2)}, u32[]{:S(2)}) collective-permute-start(bf16[112,2048]{1,0:T(8,128)(2,1)} %get-tuple-element.243.refs_5_.refs_2_), channel_id=1, source_target_pairs={{1,2},{2,1},{5,6},{6,5},{9,10},{10,9},{13,14},{14,13},{17,18},{18,... | collective-permute-start | bytes 1376264 | tf_op jit(solution)/shard_map/ppermute | solution.py:1440
  312.0 59.5 %collective-permute-start.33 = (bf16[112,2048]{1,0:T(8,128)(2,1)}, bf16[112,2048]{1,0:T(8,128)(2,1)S(1)}, u32[]{:S(2)}, u32[]{:S(2)}) collective-permute-start(bf16[112,2048]{1,0:T(8,128)(2,1)} %get-tuple-element.244.refs_6_.refs_3_), channel_id=1, source_target_pairs={{1,0},{2,3},{5,4},{6,7},{9,8},{10,11},{13,12},{14,15},{17,16},{18,... | collective-permute-start | bytes 1376264 | tf_op jit(solution)/shard_map/ppermute | solution.py:1441
  313.3 62.1 %collective-permute-start.29 = (bf16[192,2048]{1,0:T(8,128)(2,1)}, bf16[192,2048]{1,0:T(8,128)(2,1)S(1)}, u32[]{:S(2)}, u32[]{:S(2)}) collective-permute-start(bf16[192,2048]{1,0:T(8,128)(2,1)} %get-tuple-element.241.refs_7_.refs_11_.refs_3_), channel_id=1, source_target_pairs={{1,0},{2,3},{5,4},{6,7},{9,8},{10,11},{13,12},{14,15},{17,16},{18,... | collective-permute-start | bytes 2359304 | tf_op jit(solution)/shard_map/ppermute | solution.py:1443
  401.4 41.0 %collective-permute-start.43 = (bf16[4,288,256]{2,1,0:T(8,128)(2,1)S(1)}, bf16[4,288,256]{2,1,0:T(8,128)(2,1)S(1)}, u32[]{:S(2)}, u32[]{:S(2)}) collective-permute-start(bf16[4,288,256]{2,1,0:T(8,128)(2,1)S(1)} %copy-done.105), channel_id=1, source_target_pairs={{0,4},{4,0},{8,12},{12,8},{16,20},{20,16},{24,28},{28,24},{1,5},{5... | collective-permute-start | bytes 1769480 | tf_op jit(solution)/shard_map/ppermute | solution.py:54
  428.1 55.5 %collective-permute-start.42 = (bf16[176,2048]{1,0:T(8,128)(2,1)}, bf16[176,2048]{1,0:T(8,128)(2,1)S(1)}, u32[]{:S(2)}, u32[]{:S(2)}) collective-permute-start(bf16[176,2048]{1,0:T(8,128)(2,1)} %get-tuple-element.270.refs_7_.refs_12_.refs_3_.refs_9_.refs_21_), channel_id=1, source_target_pairs={{1,0},{2,3},{5,4},{6,7},{9,8},{10,11},{13,12},{14,15},{17,16},{18,... | collective-permute-start | bytes 2162696 | tf_op jit(solution)/shard_map/ppermute | solution.py:1443
  429.9 49.2 %collective-permute-start.48 = (bf16[5,16,2048]{2,1,0:T(8,128)(2,1)}, bf16[5,16,2048]{2,1,0:T(8,128)(2,1)S(1)}, u32[]{:S(2)}, u32[]{:S(2)}) collective-permute-start(bf16[5,16,2048]{2,1,0:T(8,128)(2,1)} %get-tuple-element.284), channel_id=1, source_target_pairs={{0,1},{1,0},{2,3},{3,2},{4,5},{5,4},{6,7},{7,6},{8,9},{9,8},{10,11... | collective-permute-start | bytes 983048 | tf_op jit(solution)/shard_map/ppermute | solution.py:64
  436.6 42.6 %collective-permute-start.49 = (bf16[5,16,2048]{2,1,0:T(8,128)(2,1)}, bf16[5,16,2048]{2,1,0:T(8,128)(2,1)S(1)}, u32[]{:S(2)}, u32[]{:S(2)}) collective-permute-start(bf16[5,16,2048]{2,1,0:T(8,128)(2,1)} %get-tuple-element.285), channel_id=1, source_target_pairs={{0,2},{1,3},{2,0},{3,1},{4,6},{5,7},{6,4},{7,5},{8,10},{9,11},{10,... | collective-permute-start | bytes 983048 | tf_op jit(solution)/shard_map/ppermute | solution.py:64
  440.3 41.2 %collective-permute-start.50 = (bf16[5,16,2048]{2,1,0:T(8,128)(2,1)}, bf16[5,16,2048]{2,1,0:T(8,128)(2,1)S(1)}, u32[]{:S(2)}, u32[]{:S(2)}) collective-permute-start(bf16[5,16,2048]{2,1,0:T(8,128)(2,1)} %get-tuple-element.286), channel_id=1, source_target_pairs={{0,3},{1,2},{2,1},{3,0},{4,7},{5,6},{6,5},{7,4},{8,11},{9,10},{10,... | collective-permute-start | bytes 983048 | tf_op jit(solution)/shard_map/ppermute | solution.py:64
  479.1 43.0 %collective-permute-start.44 = (bf16[6,16,2048]{2,1,0:T(8,128)(2,1)}, bf16[6,16,2048]{2,1,0:T(8,128)(2,1)S(1)}, u32[]{:S(2)}, u32[]{:S(2)}) collective-permute-start(bf16[6,16,2048]{2,1,0:T(8,128)(2,1)} %get-tuple-element.279), channel_id=1, source_target_pairs={{0,1},{1,0},{2,3},{3,2},{4,5},{5,4},{6,7},{7,6},{8,9},{9,8},{10,11... | collective-permute-start | bytes 1179656 | tf_op jit(solution)/shard_map/ppermute | solution.py:64
  479.2 45.2 %collective-permute-start.45 = (bf16[6,16,2048]{2,1,0:T(8,128)(2,1)}, bf16[6,16,2048]{2,1,0:T(8,128)(2,1)S(1)}, u32[]{:S(2)}, u32[]{:S(2)}) collective-permute-start(bf16[6,16,2048]{2,1,0:T(8,128)(2,1)} %get-tuple-element.280), channel_id=1, source_target_pairs={{0,2},{1,3},{2,0},{3,1},{4,6},{5,7},{6,4},{7,5},{8,10},{9,11},{10,... | collective-permute-start | bytes 1179656 | tf_op jit(solution)/shard_map/ppermute | solution.py:64
  481.5 45.0 %collective-permute-start.46 = (bf16[6,16,2048]{2,1,0:T(8,128)(2,1)}, bf16[6,16,2048]{2,1,0:T(8,128)(2,1)S(1)}, u32[]{:S(2)}, u32[]{:S(2)}) collective-permute-start(bf16[6,16,2048]{2,1,0:T(8,128)(2,1)} %get-tuple-element.281), channel_id=1, source_target_pairs={{0,3},{1,2},{2,1},{3,0},{4,7},{5,6},{6,5},{7,4},{8,11},{9,10},{10,... | collective-permute-start | bytes 1179656 | tf_op jit(solution)/shard_map/ppermute | solution.py:64
  520.8 43.2 %collective-permute-start.55 = (bf16[7,16,2048]{2,1,0:T(8,128)(2,1)}, bf16[7,16,2048]{2,1,0:T(8,128)(2,1)S(1)}, u32[]{:S(2)}, u32[]{:S(2)}) collective-permute-start(bf16[7,16,2048]{2,1,0:T(8,128)(2,1)} %get-tuple-element.300), channel_id=1, source_target_pairs={{0,1},{1,0},{2,3},{3,2},{4,5},{5,4},{6,7},{7,6},{8,9},{9,8},{10,11... | collective-permute-start | bytes 1376264 | tf_op jit(solution)/shard_map/ppermute | solution.py:64
  522.2 43.9 %collective-permute-start.56 = (bf16[7,16,2048]{2,1,0:T(8,128)(2,1)}, bf16[7,16,2048]{2,1,0:T(8,128)(2,1)S(1)}, u32[]{:S(2)}, u32[]{:S(2)}) collective-permute-start(bf16[7,16,2048]{2,1,0:T(8,128)(2,1)} %get-tuple-element.301), channel_id=1, source_target_pairs={{0,2},{1,3},{2,0},{3,1},{4,6},{5,7},{6,4},{7,5},{8,10},{9,11},{10,... | collective-permute-start | bytes 1376264 | tf_op jit(solution)/shard_map/ppermute | solution.py:64
  524.4 41.7 %collective-permute-start.57 = (bf16[7,16,2048]{2,1,0:T(8,128)(2,1)}, bf16[7,16,2048]{2,1,0:T(8,128)(2,1)S(1)}, u32[]{:S(2)}, u32[]{:S(2)}) collective-permute-start(bf16[7,16,2048]{2,1,0:T(8,128)(2,1)} %get-tuple-element.302), channel_id=1, source_target_pairs={{0,3},{1,2},{2,1},{3,0},{4,7},{5,6},{6,5},{7,4},{8,11},{9,10},{10,... | collective-permute-start | bytes 1376264 | tf_op jit(solution)/shard_map/ppermute | solution.py:64
  563.0 55.8 %collective-permute-start.53 = (bf16[7,16,2048]{2,1,0:T(8,128)(2,1)}, bf16[7,16,2048]{2,1,0:T(8,128)(2,1)S(1)}, u32[]{:S(2)}, u32[]{:S(2)}) collective-permute-start(bf16[7,16,2048]{2,1,0:T(8,128)(2,1)} %get-tuple-element.295), channel_id=1, source_target_pairs={{0,2},{1,3},{2,0},{3,1},{4,6},{5,7},{6,4},{7,5},{8,10},{9,11},{10,... | collective-permute-start | bytes 1376264 | tf_op jit(solution)/shard_map/ppermute | solution.py:64
  564.0 54.9 %collective-permute-start.54 = (bf16[7,16,2048]{2,1,0:T(8,128)(2,1)}, bf16[7,16,2048]{2,1,0:T(8,128)(2,1)S(1)}, u32[]{:S(2)}, u32[]{:S(2)}) collective-permute-start(bf16[7,16,2048]{2,1,0:T(8,128)(2,1)} %get-tuple-element.296), channel_id=1, source_target_pairs={{0,3},{1,2},{2,1},{3,0},{4,7},{5,6},{6,5},{7,4},{8,11},{9,10},{10,... | collective-permute-start | bytes 1376264 | tf_op jit(solution)/shard_map/ppermute | solution.py:64
  591.9 41.4 %collective-permute-start.58 = (bf16[5,16,2048]{2,1,0:T(8,128)(2,1)}, bf16[5,16,2048]{2,1,0:T(8,128)(2,1)S(1)}, u32[]{:S(2)}, u32[]{:S(2)}) collective-permute-start(bf16[5,16,2048]{2,1,0:T(8,128)(2,1)} %get-tuple-element.324), channel_id=1, source_target_pairs={{0,1},{1,0},{2,3},{3,2},{4,5},{5,4},{6,7},{7,6},{8,9},{9,8},{10,11... | collective-permute-start | bytes 983048 | tf_op jit(solution)/shard_map/ppermute | solution.py:64
  592.5 43.8 %collective-permute-start.59 = (bf16[5,16,2048]{2,1,0:T(8,128)(2,1)}, bf16[5,16,2048]{2,1,0:T(8,128)(2,1)S(1)}, u32[]{:S(2)}, u32[]{:S(2)}) collective-permute-start(bf16[5,16,2048]{2,1,0:T(8,128)(2,1)} %get-tuple-element.325), channel_id=1, source_target_pairs={{0,2},{1,3},{2,0},{3,1},{4,6},{5,7},{6,4},{7,5},{8,10},{9,11},{10,... | collective-permute-start | bytes 983048 | tf_op jit(solution)/shard_map/ppermute | solution.py:64
  594.3 42.0 %collective-permute-start.60 = (bf16[5,16,2048]{2,1,0:T(8,128)(2,1)}, bf16[5,16,2048]{2,1,0:T(8,128)(2,1)S(1)}, u32[]{:S(2)}, u32[]{:S(2)}) collective-permute-start(bf16[5,16,2048]{2,1,0:T(8,128)(2,1)} %get-tuple-element.326), channel_id=1, source_target_pairs={{0,3},{1,2},{2,1},{3,0},{4,7},{5,6},{6,5},{7,4},{8,11},{9,10},{10,... | collective-permute-start | bytes 983048 | tf_op jit(solution)/shard_map/ppermute | solution.py:64
  (174 other events, 2308.1 us)

commit v4 on v3

--- a/solution.py
+++ b/solution.py
@@ -19,8 +19,8 @@
 LOAD_VMEM = 4 * MIB
 ASSEMBLE_VMEM = 16 * MIB
 BESIDE_VMEM = 8 * MIB
-FORWARD_CHUNKS = (7, 7, 7, 11)
-BACKWARD_CHUNKS = (5, 6, 7, 7, 5, 2)
+FORWARD_CHUNKS = (8, 8, 8, 8)
+BACKWARD_CHUNKS = (8, 8, 8, 6, 2)
 ANYWHERE = pl.BlockSpec(memory_space=pl.ANY)
 IN_VMEM = pl.BlockSpec(memory_space=pltpu.VMEM)
 IN_SMEM = pl.BlockSpec(memory_space=pltpu.SMEM)
@@ -79,17 +79,18 @@
     pass
 
 
-def hold(values, ties):
+def hold(values, ties, anywhere=False):
+    kind = jax.ShapeDtypeStruct if anywhere else in_hbm
     return pl.pallas_call(
         hold_kernel,
         in_specs=[ANYWHERE] * (len(values) + len(ties)),
         out_specs=[ANYWHERE] * len(values),
-        out_shape=[in_hbm(v.shape, v.dtype) for v in values],
+        out_shape=[kind(v.shape, v.dtype) for v in values],
         input_output_aliases={i: i for i in range(len(values))},
         compiler_params=pltpu.CompilerParams(vmem_limit_bytes=MIB),
         cost_estimate=LITTLE,
         name="hold",
-    )(*[keep_far(v) for v in values], *ties)
+    )(*[v if anywhere else keep_far(v) for v in values], *ties)
 
 
 def assemble_kernel(plan, count, ties, *refs):
@@ -297,7 +298,7 @@
     y5 = swap(0, (y_next, places(2, (0,)) + x4[1][2:]))
     c5 = swap(2, (c_next, all_places(*arrived)))
     found += arrived[:0] + [c4]
-    win_rows = pack[0].shape[0] - 2 * seqs
+    win_rows = pack[0].shape[0] - seqs
     others = send_rows(jnp.stack([v[:win_rows] for v in packs]), sizes, 2, 1)
     drive, hidden, cell = join_packs(where, packs, others, words)
     weight, token = load_pieces(None, shape, where, found, sizes, rows_dev, [hidden])
@@ -378,9 +379,8 @@
         for bits, pack in enumerate(packs):
             z = jnp.bitwise_xor(where[1], bits)
             at = pl.ds(pl.multiple_of(z * width, width), width)
-            upper = pack[rows : rows + seqs, :].astype(F32)
-            lower = pack[rows + seqs : rows + 2 * seqs, : 2 * width].astype(F32)
-            sums = upper[:, : 2 * width] + upper[:, 2 * width :] + lower
+            terms = pack[rows : rows + seqs, :].astype(F32)
+            sums = terms[:, : 2 * width] + terms[:, 2 * width :]
             hidden[:, at] = sums[:, :width]
             cell[:, at] = sums[:, width:]
         wait_or_start("wait", copies, [], None)
@@ -393,15 +393,10 @@
 
 
 def pack_state(win_rows, state):
-    terms = []
-    for _ in range(3):
-        term = state.astype(BF16)
-        terms += [term[0], term[1]]
-        state = state - term.astype(F32)
-    width = state.shape[2]
-    upper = jnp.concatenate(terms[:4], axis=1)
-    lower = jnp.concatenate(terms[4:] + [jnp.zeros_like(terms[0])] * 2, axis=1)
-    return jnp.concatenate([win_rows, upper, lower], axis=0)
+    high = state.astype(BF16)
+    low = (state - high.astype(F32)).astype(BF16)
+    terms = jnp.concatenate([high[0], high[1], low[0], low[1]], axis=1)
+    return jnp.concatenate([win_rows, terms], axis=0)
 
 
 def join_packs(where, packs, others, words):
@@ -788,7 +783,7 @@
         compiler_params=pltpu.CompilerParams(vmem_limit_bytes=8 * MIB),
         cost_estimate=LITTLE,
         name="add_parts",
-    )(keep_far(kept), moved, *ties)
+    )(keep_far(kept), moved, *[keep_far(tie) for tie in ties])
 
 
 def sum_and_choose_kernel(axis, passed, where, mine, block, other, other_block, *refs):
@@ -1174,16 +1169,20 @@
     loss[...] = pack[first + parts : first + parts + 1, :1]
 
 
-def spread_small(where, small, block_sum, packed, sizes, rows, embed_shape):
+def start_small(packed, block_sum, sizes, axis):
+    return [send_rows(packed, sizes, axis, 1), send_rows(block_sum, sizes, 1 - axis, 1)]
+
+
+def spread_small(where, small, block_sum, packed, early, sizes, rows, embed_shape):
     tile, block = small.shape
     vocab, embed_width = embed_shape
     unit_width = block // 4
     blocks = [small]
     for axis in (0, 1):
-        moved = [send_rows(value, sizes, axis, 1) for value in [packed] + blocks]
+        moved = early if axis == 0 else start_small(packed, block_sum, sizes, axis)
+        blocks = blocks + [send_rows(value, sizes, axis, 1) for value in blocks]
         packed, block_sum, blocks = sum_and_choose(
-            where, 1 - axis, packed, block_sum, moved[0], send_rows(block_sum, sizes, 1 - axis, 1),
-            blocks + moved[1:],
+            where, 1 - axis, packed, block_sum, moved[0], moved[1], blocks
         )
     blocks = blocks + [send_rows(value, sizes, 2, 1) for value in blocks]
     other = send_rows(block_sum, sizes, 2, 1)
@@ -1514,7 +1513,7 @@
             launched = launched + pass_on(grads[0], (count - 1,))
         if square and number < 2:
             ties = [grads[0]] + due(*names)
-            decoder_sent, decoder_kept = add_parts(decoder_kept, moved, number <= 1, ties)
+            decoder_sent, decoder_kept = add_parts(decoder_kept, moved, True, ties)
             if number == 1:
                 decoder_sent, decoder_kept = decoder_sent[0], decoder_kept[0]
             moved = [
@@ -1572,14 +1571,15 @@
 
         def show_last(tie, done):
             shown = show(tie, ends[0])
-            return shown, [keep_far(shown)]
-
-        recurrent_grad, small, (packed, block_sum), hidden_out = reduce_rows(
+            packed, block_sum = hold(done, [tie], True)
+            early = start_small(packed, block_sum, sizes, 0)
+            return (shown, packed, block_sum, early), [keep_far(shown)]
+
+        recurrent_grad, small, _, (hidden_out, packed, block_sum, early) = reduce_rows(
             kept, sent, sizes, rows_dev, [finish, show_last], [ends[0]]
         )
-        packed, block_sum = hold([packed, block_sum], [small])
         total_loss, embed_grad, input_grad, bias_grad, decoder_out, decoder_bias_grad = spread_small(
-            where, small, block_sum, packed, sizes, embed_width, embedding.shape
+            where, small, block_sum, packed, early, sizes, embed_width, embedding.shape
         )
         total_loss = total_loss.reshape(())
         decoder_out, decoder_bias_grad = decoder_out.T, decoder_bias_grad.reshape(vocab_size)

time: 751 us -> 741 us (0.987)
  local copies, waits for them, and re-layouts: 45.9 us -> 37.4 us
    ppermute x32 -> x29, waiting for transfers between devices: 75.1 us -> 67.1 us  [swap_units(): return lax.ppermute(value, 'units', [(z, z ^ bits) for z in range(count)])]
    unnamed x223 -> x219, local copies, waits for them, and re-layouts: 31.7 us -> 24.3 us
    ppermute x32 -> x29, starting transfers between devices: 57 us -> 63.3 us  [swap_units(): return lax.ppermute(value, 'units', [(z, z ^ bits) for z in range(count)])]
    pallas_call x6 -> x5, Pallas kernels: 159 us -> 157 us  [run_backward(): pl.pallas_call(functools.partial(backward_kernel, first_step, steps, len(...]
  transfers between devices with their start and end apart: 89 -> 86, of which waited for: 30 -> 30; matrix products, arithmetic and copies ran while one was open for 3% -> 2% of each run, Pallas kernels for 51% -> 51%
where the time goes in v4:
time: 741 us; the launch traced here: 733 us
  Pallas kernels  435 us (59%)
  waiting for transfers between devices  137 us (18%)
  starting transfers between devices  115 us (16%)
  local copies, waits for them, and re-layouts  37.4 us (5%)
    pallas_call x5, Pallas kernels, run_backward(): pl.pallas_call(functools.partial(backward_kernel, first_step, steps, len(...  157 us
    pallas_call x4, Pallas kernels, run_forward(): pl.pallas_call(functools.partial(forward_kernel, start, len(ties)), grid=...  152 us
    ppermute x29, waiting for transfers between devices, swap_units(): return lax.ppermute(value, 'units', [(z, z ^ bits) for z in range(count)])  67.1 us
    ppermute x29, starting transfers between devices, swap_units(): return lax.ppermute(value, 'units', [(z, z ^ bits) for z in range(count)])  63.3 us
    pallas_call x3, Pallas kernels, run_grow(): pl.pallas_call(functools.partial(grow_kernel, tuple(spec), mode, sizes, b...  42.5 us
    ppermute x37, waiting for transfers between devices, send_rows(): return lax.ppermute(value, 'rows', row_shift(sizes, axis, step))  37.5 us
    ppermute x37, starting transfers between devices, send_rows(): return lax.ppermute(value, 'rows', row_shift(sizes, axis, step))  27.9 us
    ppermute x1, waiting for transfers between devices, gather_weight(): down = lax.ppermute(z3[0], 'units', [(2, 1), (1, 0)])  26.1 us
  transfers between devices with their start and end apart: 86, of which 30 were waited for; matrix products, arithmetic and copies ran while one was open for 2% of the time, Pallas kernels for 51%

profile of v4, /device:TPU:0, one launch (start us, length us, event | category | flops | bytes accessed | tf_op | source)
XLA Modules:
  0.0 733.4 jit_solution(11689290354539688821)
XLA Ops:
  38.2 29.9 %collective-permute-done.1.refs_6_.refs_2_ = bf16[80,2048]{1,0:T(8,128)(2,1)S(1)} collective-permute-done((bf16[80,2048]{1,0:T(8,128)(2,1)}, bf16[80,2048]{1,0:T(8,128)(2,1)S(1)}, u32[]{:S(2)}, u32[]{:S(2)}) %collective-permute-start.1) | collective-permute-done | bytes 327712 | tf_op jit(solution)/shard_map/ppermute | solution.py:64
  77.7 26.1 %collective-permute-done.9.refs_3_ = bf16[2,128,2048]{2,1,0:T(8,128)(2,1)S(1)} collective-permute-done((bf16[2,128,2048]{2,1,0:T(8,128)(2,1)S(1)}, bf16[2,128,2048]{2,1,0:T(8,128)(2,1)S(1)}, u32[]{:S(2)}, u32[]{:S(2)}) %collective-permute-start.9) | collective-permute-done | bytes 1048608 | tf_op jit(solution)/shard_map/ppermute | solution.py:268
  117.4 9.2 %collective-permute-done.14.refs_4_.refs_6_ = bf16[80,2048]{1,0:T(8,128)(2,1)S(1)} collective-permute-done((bf16[80,2048]{1,0:T(8,128)(2,1)}, bf16[80,2048]{1,0:T(8,128)(2,1)S(1)}, u32[]{:S(2)}, u32[]{:S(2)}) %collective-permute-start.14) | collective-permute-done | bytes 327712 | tf_op jit(solution)/shard_map/ppermute | solution.py:64
  126.6 17.9 %collective-permute-done.13.refs_3_.refs_5_ = bf16[80,2048]{1,0:T(8,128)(2,1)S(1)} collective-permute-done((bf16[80,2048]{1,0:T(8,128)(2,1)}, bf16[80,2048]{1,0:T(8,128)(2,1)S(1)}, u32[]{:S(2)}, u32[]{:S(2)}) %collective-permute-start.13) | collective-permute-done | bytes 327712 | tf_op jit(solution)/shard_map/ppermute | solution.py:64
  144.8 7.5 %collective-permute-done.16.refs_2_ = bf16[3,128,2048]{2,1,0:T(8,128)(2,1)S(1)} collective-permute-done((bf16[3,128,2048]{2,1,0:T(8,128)(2,1)S(1)}, bf16[3,128,2048]{2,1,0:T(8,128)(2,1)S(1)}, u32[]{:S(2)}, u32[]{:S(2)}) %collective-permute-start.16) | collective-permute-done | bytes 1572896 | tf_op jit(solution)/shard_map/ppermute | solution.py:54
  158.2 8.6 %join_packs.1 = (f32[32,4,16,2048]{3,2,1,0:T(8,128)}, f32[16,2048]{1,0:T(8,128)S(1)}, f32[16,2048]{1,0:T(8,128)S(1)}) custom-call(s32[2]{0:T(128)S(1)} %copy-done.40, bf16[80,2048]{1,0:T(8,128)(2,1)S(1)} %maximum_maximum_fusion.refs_13_.refs_1_, bf16[80,2048]{1,0:T(8,128)(2,1)S(1)} %collective-permute-done.1.refs_6_.refs_2_, ...), custom_call_target="tpu_custom_call" | custom-call | bytes 1024 | tf_op jit(solution)/shard_map/join_packs/pallas_call | solution.py:410
  168.1 9.4 %load_pieces.3 = (bf16[4,2048,2048]{2,1,0:T(8,128)(2,1)S(1)}, f32[8,128]{1,0:T(8,128)}) custom-call(s32[2]{0:T(128)} %copy-done.39, bf16[2,128,2048]{2,1,0:T(8,128)(2,1)} %copy-done.6, bf16[2,128,2048]{2,1,0:T(8,128)(2,1)} %copy-done.7, bf16[1,128,2048]{2,1,0:T(8,128)(2,1)} %collective-permute-done.3.refs_4_.refs_3_, ...), custom_call_target="tpu_custom_call" | custom-call | bytes 1024 | tf_op jit(solution)/shard_map/load_pieces/pallas_call | solution.py:198
  191.4 38.0 %forward_steps.4 = (f32[8,4,16,2048]{3,2,1,0:T(8,128)}, f32[8,16,2048]{2,1,0:T(8,128)}, bf16[8,16,2048]{2,1,0:T(8,128)(2,1)}, bf16[8,16,2048]{2,1,0:T(8,128)(2,1...) custom-call(s32[16,1]{1,0:T(8,128)} %copy-done.31, f32[32,4,16,2048]{3,2,1,0:T(8,128)} %get-tuple-element.211.refs_1_, ...), custom_call_target="tpu_custom_call" | custom-call | bytes 134217728 | tf_op jit(solution)/shard_map/forward_steps/pallas_call | solution.py:483
  231.4 38.0 %forward_steps.5 = (f32[8,4,16,2048]{3,2,1,0:T(8,128)}, f32[8,16,2048]{2,1,0:T(8,128)}, bf16[8,16,2048]{2,1,0:T(8,128)(2,1)}, bf16[8,16,2048]{2,1,0:T(8,128)(2,1...) custom-call(s32[16,1]{1,0:T(8,128)} %copy-done.31, f32[32,4,16,2048]{3,2,1,0:T(8,128)} %get-tuple-element.211.refs_1_, ...), custom_call_target="tpu_custom_call" | custom-call | bytes 134217728 | tf_op jit(solution)/shard_map/forward_steps/pallas_call | solution.py:483
  273.5 6.5 collective-permute-start.23
  280.9 38.0 %forward_steps.6 = (f32[8,4,16,2048]{3,2,1,0:T(8,128)}, f32[8,16,2048]{2,1,0:T(8,128)}, bf16[8,16,2048]{2,1,0:T(8,128)(2,1)}, bf16[8,16,2048]{2,1,0:T(8,128)(2,1...) custom-call(s32[16,1]{1,0:T(8,128)} %copy-done.31, f32[32,4,16,2048]{3,2,1,0:T(8,128)} %get-tuple-element.211.refs_1_, ...), custom_call_target="tpu_custom_call" | custom-call | bytes 134217728 | tf_op jit(solution)/shard_map/forward_steps/pallas_call | solution.py:483
  327.5 38.0 %forward_steps.7 = (f32[8,4,16,2048]{3,2,1,0:T(8,128)}, f32[8,16,2048]{2,1,0:T(8,128)}, bf16[8,16,2048]{2,1,0:T(8,128)(2,1)}, bf16[8,16,2048]{2,1,0:T(8,128)(2,1...) custom-call(s32[16,1]{1,0:T(8,128)} %copy-done.31, f32[32,4,16,2048]{3,2,1,0:T(8,128)} %get-tuple-element.211.refs_1_, ...), custom_call_target="tpu_custom_call" | custom-call | bytes 134217728 | tf_op jit(solution)/shard_map/forward_steps/pallas_call | solution.py:483
  376.4 15.7 %decoder.1 = (bf16[4,2048,2048]{2,1,0:T(8,128)(2,1)S(1)}, bf16[512,2048]{1,0:T(8,128)(2,1)}, f32[8,128]{1,0:T(8,128)}, bf16[4,288,256]{2,1,0:T(8,128)(2,1)}, f32[4,288,256]{2,1,0:T(8,128)}) custom-call(s32[2]{0:T(128)} %copy-done.39, f32[1,384]{1,0:T(1,128)} %copy-done.45, s32[512,1]{1,0:T(8,128)} %reshape.328.refs_8_.refs_2_, ...), custom_call_target="tpu_custom_call", output_to_operand_aliasing={{0}: (14, {})} | custom-call | tf_op jit(solution)/shard_map/decoder/pallas_call | solution.py:734
  398.7 38.6 %backward_steps.5 = (bf16[8,16,2048]{2,1,0:T(8,128)(2,1)}, bf16[8,16,2048]{2,1,0:T(8,128)(2,1)}, bf16[8,16,2048]{2,1,0:T(8,128)(2,1)}, bf16[8,16,2048]{2,1,0:T(8...) custom-call(s32[2]{0:T(128)} %copy-done.39, s32[16,1]{1,0:T(8,128)} %copy-done.31, ...), custom_call_target="tpu_custom_call" | custom-call | bytes 134217728 | tf_op jit(solution)/shard_map/backward_steps/pallas_call | solution.py:571
  452.2 38.7 %backward_steps.6 = (bf16[8,16,2048]{2,1,0:T(8,128)(2,1)}, bf16[8,16,2048]{2,1,0:T(8,128)(2,1)}, bf16[8,16,2048]{2,1,0:T(8,128)(2,1)}, bf16[8,16,2048]{2,1,0:T(8...) custom-call(s32[2]{0:T(128)} %copy-done.39, s32[16,1]{1,0:T(8,128)} %copy-done.31, ...), custom_call_target="tpu_custom_call" | custom-call | bytes 134217728 | tf_op jit(solution)/shard_map/backward_steps/pallas_call | solution.py:571
  499.0 38.7 %backward_steps.7 = (bf16[8,16,2048]{2,1,0:T(8,128)(2,1)}, bf16[8,16,2048]{2,1,0:T(8,128)(2,1)}, bf16[8,16,2048]{2,1,0:T(8,128)(2,1)}, bf16[8,16,2048]{2,1,0:T(8...) custom-call(s32[2]{0:T(128)} %copy-done.39, s32[16,1]{1,0:T(8,128)} %copy-done.31, ...), custom_call_target="tpu_custom_call" | custom-call | bytes 134217728 | tf_op jit(solution)/shard_map/backward_steps/pallas_call | solution.py:571
  544.6 29.7 %backward_steps.8 = (bf16[6,16,2048]{2,1,0:T(8,128)(2,1)}, bf16[6,16,2048]{2,1,0:T(8,128)(2,1)}, bf16[6,16,2048]{2,1,0:T(8,128)(2,1)}, bf16[6,16,2048]{2,1,0:T(8...) custom-call(s32[2]{0:T(128)} %copy-done.39, s32[16,1]{1,0:T(8,128)} %copy-done.31, ...), custom_call_target="tpu_custom_call" | custom-call | bytes 100663296 | tf_op jit(solution)/shard_map/backward_steps/pallas_call | solution.py:571
  578.8 20.2 %weight_gradient.3 = (f32[128,2048]{1,0:T(8,128)}, f32[288,128]{1,0:T(8,128)}, f32[2048,2048]{1,0:T(8,128)}) custom-call(s32[2]{0:T(128)} %copy-done.39, bf16[128,2048]{1,0:T(8,128)(2,1)} %bitcast.144, bf16[128,2048]{1,0:T(8,128)(2,1)} %get-tuple-element.262.refs_1_.refs_6_.refs_2_.refs_19_, ...), custom_call_target="tpu_custom_call" | custom-call | bytes 1024 | tf_op jit(solution)/shard_map/weight_gradient/pallas_call | solution.py:1039
  600.1 11.4 %backward_steps.9 = (bf16[2,16,2048]{2,1,0:T(8,128)(2,1)}, bf16[2,16,2048]{2,1,0:T(8,128)(2,1)}, bf16[2,16,2048]{2,1,0:T(8,128)(2,1)}, bf16[2,16,2048]{2,1,0:T(8...) custom-call(s32[2]{0:T(128)} %copy-done.39, s32[16,1]{1,0:T(8,128)} %copy-done.31, ...), custom_call_target="tpu_custom_call" | custom-call | bytes 33554432 | tf_op jit(solution)/shard_map/backward_steps/pallas_call | solution.py:571
  611.4 7.9 %collective-permute-start.58 = (bf16[2,16,2048]{2,1,0:T(8,128)(2,1)}, bf16[2,16,2048]{2,1,0:T(8,128)(2,1)S(1)}, u32[]{:S(2)}, u32[]{:S(2)}) collective-permute-start(bf16[2,16,2048]{2,1,0:T(8,128)(2,1)} %get-tuple-element.316), channel_id=1, source_target_pairs={{0,1},{1,0},{2,3},{3,2},{4,5},{5,4},{6,7},{7,6},{8,9},{9,8},{10,11... | collective-permute-start | bytes 393224 | tf_op jit(solution)/shard_map/ppermute | solution.py:64
  623.7 8.4 %little_gradients.1 = (f32[128,2048]{1,0:T(8,128)}, f32[288,128]{1,0:T(8,128)}) custom-call(bf16[128,2048]{1,0:T(8,128)(2,1)} %bitcast.132, bf16[128,2048]{1,0:T(8,128)(2,1)} %bitcast.120, bf16[128,2048]{1,0:T(8,128)(2,1)} %bitcast.123, bf16[128,2048]{1,0:T(8,128)(2,1)} %bitcast.126, bf16[96,2048]{1,0:T(8,128)(2,1)} %bitcast.146, ...), custom_call_target="tpu_custom_call" | custom-call | bytes 1024 | tf_op jit(solution)/shard_map/little_gradients/pallas_call | solution.py:872
  635.8 11.2 %weight_gradient.4 = (f32[128,2048]{1,0:T(8,128)}, f32[288,128]{1,0:T(8,128)}, bf16[4,272,2048]{2,1,0:T(8,128)(2,1)S(1)}) custom-call(s32[2]{0:T(128)S(1)} %copy-done.42, bf16[128,2048]{1,0:T(8,128)(2,1)} %get-tuple-element.298.refs_1_.refs_8_, bf16[128,2048]{1,0:T(8,128)(2,1)} %get-tuple-element.299.refs_2_.refs_9_, ...), custom_call_target="tpu_custom_call" | custom-call | bytes 1024 | tf_op jit(solution)/shard_map/weight_gradient/pallas_call | solution.py:1039
  647.1 6.5 collective-permute-start.62
  656.1 11.0 %weight_gradient.5.refs_5_.refs_0_ = f32[4,272,2048]{2,1,0:T(8,128)S(1)} custom-call(s32[2]{0:T(128)S(1)} %copy-done.42, bf16[128,2048]{1,0:T(8,128)(2,1)} %get-tuple-element.298.refs_1_.refs_8_, bf16[128,2048]{1,0:T(8,128)(2,1)} %get-tuple-element.299.refs_2_.refs_9_, bf16[128,2048]{1,0:T(8,128)(2,1)} %get-tuple-element.300.refs_3_.refs_11_, ...), custom_call_target="tpu_custom_call" | custom-call | bytes 1024 | tf_op jit(solution)/shard_map/weight_gradient/pallas_call | solution.py:1039
  (461 shorter events, 225.1 us)
Async XLA Ops:
  271.5 50.7 %collective-permute-start.27 = (bf16[208,2048]{1,0:T(8,128)(2,1)}, bf16[208,2048]{1,0:T(8,128)(2,1)S(1)}, u32[]{:S(2)}, u32[]{:S(2)}) collective-permute-start(bf16[208,2048]{1,0:T(8,128)(2,1)} %get-tuple-element.229.refs_5_.refs_2_), channel_id=1, source_target_pairs={{1,2},{2,1},{5,6},{6,5},{9,10},{10,9},{13,14},{14,13},{17,18},{18,... | collective-permute-start | bytes 2555912 | tf_op jit(solution)/shard_map/ppermute | solution.py:1439
  272.2 50.0 %collective-permute-start.28 = (bf16[208,2048]{1,0:T(8,128)(2,1)}, bf16[208,2048]{1,0:T(8,128)(2,1)S(1)}, u32[]{:S(2)}, u32[]{:S(2)}) collective-permute-start(bf16[208,2048]{1,0:T(8,128)(2,1)} %get-tuple-element.230.refs_6_.refs_3_), channel_id=1, source_target_pairs={{1,0},{2,3},{5,4},{6,7},{9,8},{10,11},{13,12},{14,15},{17,16},{18,... | collective-permute-start | bytes 2555912 | tf_op jit(solution)/shard_map/ppermute | solution.py:1440
  273.5 47.9 %collective-permute-start.23 = (bf16[128,2048]{1,0:T(8,128)(2,1)}, bf16[128,2048]{1,0:T(8,128)(2,1)S(1)}, u32[]{:S(2)}, u32[]{:S(2)}) collective-permute-start(bf16[128,2048]{1,0:T(8,128)(2,1)} %bitcast.129), channel_id=1, source_target_pairs={{0,1},{1,0},{2,3},{3,2},{4,5},{5,4},{6,7},{7,6},{8,9},{9,8},{10,11... | collective-permute-start | bytes 1572872 | tf_op jit(solution)/shard_map/ppermute | solution.py:64
  319.0 46.6 %collective-permute-start.30 = (bf16[128,2048]{1,0:T(8,128)(2,1)}, bf16[128,2048]{1,0:T(8,128)(2,1)S(1)}, u32[]{:S(2)}, u32[]{:S(2)}) collective-permute-start(bf16[128,2048]{1,0:T(8,128)(2,1)} %bitcast.138), channel_id=1, source_target_pairs={{0,1},{1,0},{2,3},{3,2},{4,5},{5,4},{6,7},{7,6},{8,9},{9,8},{10,11... | collective-permute-start | bytes 1572872 | tf_op jit(solution)/shard_map/ppermute | solution.py:64
  321.5 48.7 %collective-permute-start.31 = (bf16[128,2048]{1,0:T(8,128)(2,1)}, bf16[128,2048]{1,0:T(8,128)(2,1)S(1)}, u32[]{:S(2)}, u32[]{:S(2)}) collective-permute-start(bf16[128,2048]{1,0:T(8,128)(2,1)} %bitcast.139), channel_id=1, source_target_pairs={{1,2},{2,1},{5,6},{6,5},{9,10},{10,9},{13,14},{14,13},{17,18},{18,... | collective-permute-start | bytes 1572872 | tf_op jit(solution)/shard_map/ppermute | solution.py:1437
  324.2 46.7 %collective-permute-start.32 = (bf16[128,2048]{1,0:T(8,128)(2,1)}, bf16[128,2048]{1,0:T(8,128)(2,1)S(1)}, u32[]{:S(2)}, u32[]{:S(2)}) collective-permute-start(bf16[128,2048]{1,0:T(8,128)(2,1)} %get-tuple-element.237.refs_5_.refs_2_), channel_id=1, source_target_pairs={{1,2},{2,1},{5,6},{6,5},{9,10},{10,9},{13,14},{14,13},{17,18},{18,... | collective-permute-start | bytes 1572872 | tf_op jit(solution)/shard_map/ppermute | solution.py:1439
  324.9 46.0 %collective-permute-start.33 = (bf16[128,2048]{1,0:T(8,128)(2,1)}, bf16[128,2048]{1,0:T(8,128)(2,1)S(1)}, u32[]{:S(2)}, u32[]{:S(2)}) collective-permute-start(bf16[128,2048]{1,0:T(8,128)(2,1)} %get-tuple-element.238.refs_6_.refs_3_), channel_id=1, source_target_pairs={{1,0},{2,3},{5,4},{6,7},{9,8},{10,11},{13,12},{14,15},{17,16},{18,... | collective-permute-start | bytes 1572872 | tf_op jit(solution)/shard_map/ppermute | solution.py:1440
  326.2 48.4 %collective-permute-start.29 = (bf16[208,2048]{1,0:T(8,128)(2,1)}, bf16[208,2048]{1,0:T(8,128)(2,1)S(1)}, u32[]{:S(2)}, u32[]{:S(2)}) collective-permute-start(bf16[208,2048]{1,0:T(8,128)(2,1)} %get-tuple-element.235.refs_7_.refs_11_.refs_3_), channel_id=1, source_target_pairs={{1,0},{2,3},{5,4},{6,7},{9,8},{10,11},{13,12},{14,15},{17,16},{18,... | collective-permute-start | bytes 2555912 | tf_op jit(solution)/shard_map/ppermute | solution.py:1442
  374.6 62.7 %collective-permute-start.34 = (bf16[128,2048]{1,0:T(8,128)(2,1)}, bf16[128,2048]{1,0:T(8,128)(2,1)S(1)}, u32[]{:S(2)}, u32[]{:S(2)}) collective-permute-start(bf16[128,2048]{1,0:T(8,128)(2,1)} %get-tuple-element.243.refs_8_.refs_9_), channel_id=1, source_target_pairs={{1,0},{2,3},{5,4},{6,7},{9,8},{10,11},{13,12},{14,15},{17,16},{18,... | collective-permute-start | bytes 1572872 | tf_op jit(solution)/shard_map/ppermute | solution.py:1442
  395.2 47.6 %collective-permute-start.40 = (bf16[128,2048]{1,0:T(8,128)(2,1)}, bf16[128,2048]{1,0:T(8,128)(2,1)S(1)}, u32[]{:S(2)}, u32[]{:S(2)}) collective-permute-start(bf16[128,2048]{1,0:T(8,128)(2,1)} %get-tuple-element.255.refs_0_), channel_id=1, source_target_pairs={{1,2},{2,1},{5,6},{6,5},{9,10},{10,9},{13,14},{14,13},{17,18},{18,... | collective-permute-start | bytes 1572872 | tf_op jit(solution)/shard_map/ppermute | solution.py:1439
  396.0 47.5 %collective-permute-start.41 = (bf16[128,2048]{1,0:T(8,128)(2,1)}, bf16[128,2048]{1,0:T(8,128)(2,1)S(1)}, u32[]{:S(2)}, u32[]{:S(2)}) collective-permute-start(bf16[128,2048]{1,0:T(8,128)(2,1)} %get-tuple-element.256.refs_1_), channel_id=1, source_target_pairs={{1,0},{2,3},{5,4},{6,7},{9,8},{10,11},{13,12},{14,15},{17,16},{18,... | collective-permute-start | bytes 1572872 | tf_op jit(solution)/shard_map/ppermute | solution.py:1440
  397.3 48.8 %collective-permute-start.46 = (bf16[4,288,256]{2,1,0:T(8,128)(2,1)S(1)}, bf16[4,288,256]{2,1,0:T(8,128)(2,1)S(1)}, u32[]{:S(2)}, u32[]{:S(2)}) collective-permute-start(bf16[4,288,256]{2,1,0:T(8,128)(2,1)S(1)} %copy-done.104), channel_id=1, source_target_pairs={{0,4},{4,0},{8,12},{12,8},{16,20},{20,16},{24,28},{28,24},{1,5},{5... | collective-permute-start | bytes 1769480 | tf_op jit(solution)/shard_map/ppermute | solution.py:54
  397.4 50.2 %collective-permute-start.39 = (bf16[128,2048]{1,0:T(8,128)(2,1)}, bf16[128,2048]{1,0:T(8,128)(2,1)S(1)}, u32[]{:S(2)}, u32[]{:S(2)}) collective-permute-start(bf16[128,2048]{1,0:T(8,128)(2,1)} %get-tuple-element.254.refs_3_.refs_8_.refs_9_.refs_15_), channel_id=1, source_target_pairs={{1,0},{2,3},{5,4},{6,7},{9,8},{10,11},{13,12},{14,15},{17,16},{18,... | collective-permute-start | bytes 1572872 | tf_op jit(solution)/shard_map/ppermute | solution.py:1442
  437.3 53.5 %collective-permute-start.43 = (bf16[8,16,2048]{2,1,0:T(8,128)(2,1)}, bf16[8,16,2048]{2,1,0:T(8,128)(2,1)S(1)}, u32[]{:S(2)}, u32[]{:S(2)}) collective-permute-start(bf16[8,16,2048]{2,1,0:T(8,128)(2,1)} %get-tuple-element.269), channel_id=1, source_target_pairs={{0,1},{1,0},{2,3},{3,2},{4,5},{5,4},{6,7},{7,6},{8,9},{9,8},{10,11... | collective-permute-start | bytes 1572872 | tf_op jit(solution)/shard_map/ppermute | solution.py:64
  442.8 50.9 %collective-permute-start.44 = (bf16[8,16,2048]{2,1,0:T(8,128)(2,1)}, bf16[8,16,2048]{2,1,0:T(8,128)(2,1)S(1)}, u32[]{:S(2)}, u32[]{:S(2)}) collective-permute-start(bf16[8,16,2048]{2,1,0:T(8,128)(2,1)} %get-tuple-element.270), channel_id=1, source_target_pairs={{0,2},{1,3},{2,0},{3,1},{4,6},{5,7},{6,4},{7,5},{8,10},{9,11},{10,... | collective-permute-start | bytes 1572872 | tf_op jit(solution)/shard_map/ppermute | solution.py:64
  443.5 50.8 %collective-permute-start.45 = (bf16[8,16,2048]{2,1,0:T(8,128)(2,1)}, bf16[8,16,2048]{2,1,0:T(8,128)(2,1)S(1)}, u32[]{:S(2)}, u32[]{:S(2)}) collective-permute-start(bf16[8,16,2048]{2,1,0:T(8,128)(2,1)} %get-tuple-element.271), channel_id=1, source_target_pairs={{0,3},{1,2},{2,1},{3,0},{4,7},{5,6},{6,5},{7,4},{8,11},{9,10},{10,... | collective-permute-start | bytes 1572872 | tf_op jit(solution)/shard_map/ppermute | solution.py:64
  446.2 50.0 %collective-permute-start.42 = (bf16[128,2048]{1,0:T(8,128)(2,1)}, bf16[128,2048]{1,0:T(8,128)(2,1)S(1)}, u32[]{:S(2)}, u32[]{:S(2)}) collective-permute-start(bf16[128,2048]{1,0:T(8,128)(2,1)} %get-tuple-element.264.refs_7_.refs_12_.refs_3_.refs_21_), channel_id=1, source_target_pairs={{1,0},{2,3},{5,4},{6,7},{9,8},{10,11},{13,12},{14,15},{17,16},{18,... | collective-permute-start | bytes 1572872 | tf_op jit(solution)/shard_map/ppermute | solution.py:1442
  490.9 49.2 %collective-permute-start.51 = (bf16[8,16,2048]{2,1,0:T(8,128)(2,1)}, bf16[8,16,2048]{2,1,0:T(8,128)(2,1)S(1)}, u32[]{:S(2)}, u32[]{:S(2)}) collective-permute-start(bf16[8,16,2048]{2,1,0:T(8,128)(2,1)} %get-tuple-element.287), channel_id=1, source_target_pairs={{0,1},{1,0},{2,3},{3,2},{4,5},{5,4},{6,7},{7,6},{8,9},{9,8},{10,11... | collective-permute-start | bytes 1572872 | tf_op jit(solution)/shard_map/ppermute | solution.py:64
  493.7 48.0 %collective-permute-start.52 = (bf16[8,16,2048]{2,1,0:T(8,128)(2,1)}, bf16[8,16,2048]{2,1,0:T(8,128)(2,1)S(1)}, u32[]{:S(2)}, u32[]{:S(2)}) collective-permute-start(bf16[8,16,2048]{2,1,0:T(8,128)(2,1)} %get-tuple-element.288), channel_id=1, source_target_pairs={{0,2},{1,3},{2,0},{3,1},{4,6},{5,7},{6,4},{7,5},{8,10},{9,11},{10,... | collective-permute-start | bytes 1572872 | tf_op jit(solution)/shard_map/ppermute | solution.py:64
  494.4 49.1 %collective-permute-start.53 = (bf16[8,16,2048]{2,1,0:T(8,128)(2,1)}, bf16[8,16,2048]{2,1,0:T(8,128)(2,1)S(1)}, u32[]{:S(2)}, u32[]{:S(2)}) collective-permute-start(bf16[8,16,2048]{2,1,0:T(8,128)(2,1)} %get-tuple-element.289), channel_id=1, source_target_pairs={{0,3},{1,2},{2,1},{3,0},{4,7},{5,6},{6,5},{7,4},{8,11},{9,10},{10,... | collective-permute-start | bytes 1572872 | tf_op jit(solution)/shard_map/ppermute | solution.py:64
  540.1 59.0 %collective-permute-start.49 = (bf16[8,16,2048]{2,1,0:T(8,128)(2,1)}, bf16[8,16,2048]{2,1,0:T(8,128)(2,1)S(1)}, u32[]{:S(2)}, u32[]{:S(2)}) collective-permute-start(bf16[8,16,2048]{2,1,0:T(8,128)(2,1)} %get-tuple-element.283), channel_id=1, source_target_pairs={{0,2},{1,3},{2,0},{3,1},{4,6},{5,7},{6,4},{7,5},{8,10},{9,11},{10,... | collective-permute-start | bytes 1572872 | tf_op jit(solution)/shard_map/ppermute | solution.py:64
  541.7 57.4 %collective-permute-start.50 = (bf16[8,16,2048]{2,1,0:T(8,128)(2,1)}, bf16[8,16,2048]{2,1,0:T(8,128)(2,1)S(1)}, u32[]{:S(2)}, u32[]{:S(2)}) collective-permute-start(bf16[8,16,2048]{2,1,0:T(8,128)(2,1)} %get-tuple-element.284), channel_id=1, source_target_pairs={{0,3},{1,2},{2,1},{3,0},{4,7},{5,6},{6,5},{7,4},{8,11},{9,10},{10,... | collective-permute-start | bytes 1572872 | tf_op jit(solution)/shard_map/ppermute | solution.py:64
  574.3 45.7 %collective-permute-start.55 = (bf16[6,16,2048]{2,1,0:T(8,128)(2,1)}, bf16[6,16,2048]{2,1,0:T(8,128)(2,1)S(1)}, u32[]{:S(2)}, u32[]{:S(2)}) collective-permute-start(bf16[6,16,2048]{2,1,0:T(8,128)(2,1)} %get-tuple-element.312), channel_id=1, source_target_pairs={{0,1},{1,0},{2,3},{3,2},{4,5},{5,4},{6,7},{7,6},{8,9},{9,8},{10,11... | collective-permute-start | bytes 1179656 | tf_op jit(solution)/shard_map/ppermute | solution.py:64
  575.4 47.3 %collective-permute-start.56 = (bf16[6,16,2048]{2,1,0:T(8,128)(2,1)}, bf16[6,16,2048]{2,1,0:T(8,128)(2,1)S(1)}, u32[]{:S(2)}, u32[]{:S(2)}) collective-permute-start(bf16[6,16,2048]{2,1,0:T(8,128)(2,1)} %get-tuple-element.313), channel_id=1, source_target_pairs={{0,2},{1,3},{2,0},{3,1},{4,6},{5,7},{6,4},{7,5},{8,10},{9,11},{10,... | collective-permute-start | bytes 1179656 | tf_op jit(solution)/shard_map/ppermute | solution.py:64
  (169 other events, 2044.5 us)

commit v5 on v4

--- a/solution.py
+++ b/solution.py
@@ -1422,7 +1422,7 @@
         onward = [n for n in numbers if n in range(len(befores)) and len(befores[n]) in (3, 5)]
         old = [v for n in onward for v in befores[n][1:3] + befores[n][3:4]]
         if old:
-            new = hold(old, [latest])
+            new = hold(old, [keep_far(latest)])
             for values in list(started.values()) + [befores[n] for n in onward]:
                 values[:] = [
                     next((w for u, w in zip(old, new) if u is v), v) for v in values
@@ -1453,7 +1453,7 @@
         if number == 0:
             before = join_rows([before, decoder_packed])
         befores.append([before])
-        started["forward", number] = pass_on(hidden, (number, number - 1, number - 2))
+        started["forward", number] = pass_on(cells, (number, number - 1, number - 2))
         chunks.append((start, steps, preact, cells))
         lows.append(low.reshape(steps * seqs, hidden_width))
         start += steps
@@ -1510,9 +1510,9 @@
         launched = dpres[-1][1:]
         names = [("backward", number - 1)] if number else [("forward", count - 1), "decoder"]
         if number == 0:
-            launched = launched + pass_on(grads[0], (count - 1,))
+            launched = launched + pass_on(out[0], (count - 1,))
         if square and number < 2:
-            ties = [grads[0]] + due(*names)
+            ties = [out[0]] + due(*names)
             decoder_sent, decoder_kept = add_parts(decoder_kept, moved, True, ties)
             if number == 1:
                 decoder_sent, decoder_kept = decoder_sent[0], decoder_kept[0]

time: 741 us -> 737 us (level)
    unnamed x219 -> x211, local copies, waits for them, and re-layouts: 24.3 us -> 20.3 us
where the time goes in v5:
time: 737 us; the launch traced here: 729 us
  Pallas kernels  435 us (59%)
  waiting for transfers between devices  138 us (19%)
  starting transfers between devices  114 us (15%)
  local copies, waits for them, and re-layouts  33.4 us (5%)
    pallas_call x5, Pallas kernels, run_backward(): pl.pallas_call(functools.partial(backward_kernel, first_step, steps, len(...  157 us
    pallas_call x4, Pallas kernels, run_forward(): pl.pallas_call(functools.partial(forward_kernel, start, len(ties)), grid=...  152 us
    ppermute x29, waiting for transfers between devices, swap_units(): return lax.ppermute(value, 'units', [(z, z ^ bits) for z in range(count)])  67.2 us
    ppermute x29, starting transfers between devices, swap_units(): return lax.ppermute(value, 'units', [(z, z ^ bits) for z in range(count)])  62.5 us
    pallas_call x3, Pallas kernels, run_grow(): pl.pallas_call(functools.partial(grow_kernel, tuple(spec), mode, sizes, b...  42.5 us
    ppermute x37, waiting for transfers between devices, send_rows(): return lax.ppermute(value, 'rows', row_shift(sizes, axis, step))  37.6 us
    ppermute x37, starting transfers between devices, send_rows(): return lax.ppermute(value, 'rows', row_shift(sizes, axis, step))  27.8 us
    ppermute x1, waiting for transfers between devices, gather_weight(): down = lax.ppermute(z3[0], 'units', [(2, 1), (1, 0)])  26.1 us
  transfers between devices with their start and end apart: 86, of which 30 were waited for; matrix products, arithmetic and copies ran while one was open for 2% of the time, Pallas kernels for 51%

profile of v5, /device:TPU:0, one launch (start us, length us, event | category | flops | bytes accessed | tf_op | source)
XLA Modules:
  0.0 729.4 jit_solution(5474450780815213276)
XLA Ops:
  38.2 29.9 %collective-permute-done.1.refs_6_.refs_2_ = bf16[80,2048]{1,0:T(8,128)(2,1)S(1)} collective-permute-done((bf16[80,2048]{1,0:T(8,128)(2,1)}, bf16[80,2048]{1,0:T(8,128)(2,1)S(1)}, u32[]{:S(2)}, u32[]{:S(2)}) %collective-permute-start.1) | collective-permute-done | bytes 327712 | tf_op jit(solution)/shard_map/ppermute | solution.py:64
  77.6 26.1 %collective-permute-done.9.refs_3_ = bf16[2,128,2048]{2,1,0:T(8,128)(2,1)S(1)} collective-permute-done((bf16[2,128,2048]{2,1,0:T(8,128)(2,1)S(1)}, bf16[2,128,2048]{2,1,0:T(8,128)(2,1)S(1)}, u32[]{:S(2)}, u32[]{:S(2)}) %collective-permute-start.9) | collective-permute-done | bytes 1048608 | tf_op jit(solution)/shard_map/ppermute | solution.py:268
  117.4 9.2 %collective-permute-done.14.refs_4_.refs_6_ = bf16[80,2048]{1,0:T(8,128)(2,1)S(1)} collective-permute-done((bf16[80,2048]{1,0:T(8,128)(2,1)}, bf16[80,2048]{1,0:T(8,128)(2,1)S(1)}, u32[]{:S(2)}, u32[]{:S(2)}) %collective-permute-start.14) | collective-permute-done | bytes 327712 | tf_op jit(solution)/shard_map/ppermute | solution.py:64
  126.6 17.9 %collective-permute-done.13.refs_3_.refs_5_ = bf16[80,2048]{1,0:T(8,128)(2,1)S(1)} collective-permute-done((bf16[80,2048]{1,0:T(8,128)(2,1)}, bf16[80,2048]{1,0:T(8,128)(2,1)S(1)}, u32[]{:S(2)}, u32[]{:S(2)}) %collective-permute-start.13) | collective-permute-done | bytes 327712 | tf_op jit(solution)/shard_map/ppermute | solution.py:64
  144.8 7.5 %collective-permute-done.16.refs_2_ = bf16[3,128,2048]{2,1,0:T(8,128)(2,1)S(1)} collective-permute-done((bf16[3,128,2048]{2,1,0:T(8,128)(2,1)S(1)}, bf16[3,128,2048]{2,1,0:T(8,128)(2,1)S(1)}, u32[]{:S(2)}, u32[]{:S(2)}) %collective-permute-start.16) | collective-permute-done | bytes 1572896 | tf_op jit(solution)/shard_map/ppermute | solution.py:54
  158.2 8.6 %join_packs.1 = (f32[32,4,16,2048]{3,2,1,0:T(8,128)}, f32[16,2048]{1,0:T(8,128)S(1)}, f32[16,2048]{1,0:T(8,128)S(1)}) custom-call(s32[2]{0:T(128)S(1)} %copy-done.36, bf16[80,2048]{1,0:T(8,128)(2,1)S(1)} %maximum_maximum_fusion.refs_13_.refs_1_, bf16[80,2048]{1,0:T(8,128)(2,1)S(1)} %collective-permute-done.1.refs_6_.refs_2_, ...), custom_call_target="tpu_custom_call" | custom-call | bytes 1024 | tf_op jit(solution)/shard_map/join_packs/pallas_call | solution.py:410
  168.1 9.4 %load_pieces.3 = (bf16[4,2048,2048]{2,1,0:T(8,128)(2,1)S(1)}, f32[8,128]{1,0:T(8,128)}) custom-call(s32[2]{0:T(128)} %copy-done.35, bf16[2,128,2048]{2,1,0:T(8,128)(2,1)} %copy-done.6, bf16[2,128,2048]{2,1,0:T(8,128)(2,1)} %copy-done.7, bf16[1,128,2048]{2,1,0:T(8,128)(2,1)} %collective-permute-done.3.refs_4_.refs_3_, ...), custom_call_target="tpu_custom_call" | custom-call | bytes 1024 | tf_op jit(solution)/shard_map/load_pieces/pallas_call | solution.py:198
  191.4 38.0 %forward_steps.4 = (f32[8,4,16,2048]{3,2,1,0:T(8,128)}, f32[8,16,2048]{2,1,0:T(8,128)}, bf16[8,16,2048]{2,1,0:T(8,128)(2,1)}, bf16[8,16,2048]{2,1,0:T(8,128)(2,1...) custom-call(s32[16,1]{1,0:T(8,128)} %copy-done.30, f32[32,4,16,2048]{3,2,1,0:T(8,128)} %get-tuple-element.211.refs_1_, ...), custom_call_target="tpu_custom_call" | custom-call | bytes 134217728 | tf_op jit(solution)/shard_map/forward_steps/pallas_call | solution.py:483
  231.3 38.0 %forward_steps.5 = (f32[8,4,16,2048]{3,2,1,0:T(8,128)}, f32[8,16,2048]{2,1,0:T(8,128)}, bf16[8,16,2048]{2,1,0:T(8,128)(2,1)}, bf16[8,16,2048]{2,1,0:T(8,128)(2,1...) custom-call(s32[16,1]{1,0:T(8,128)} %copy-done.30, f32[32,4,16,2048]{3,2,1,0:T(8,128)} %get-tuple-element.211.refs_1_, ...), custom_call_target="tpu_custom_call" | custom-call | bytes 134217728 | tf_op jit(solution)/shard_map/forward_steps/pallas_call | solution.py:483
  272.6 6.5 collective-permute-start.23
  280.0 38.0 %forward_steps.6 = (f32[8,4,16,2048]{3,2,1,0:T(8,128)}, f32[8,16,2048]{2,1,0:T(8,128)}, bf16[8,16,2048]{2,1,0:T(8,128)(2,1)}, bf16[8,16,2048]{2,1,0:T(8,128)(2,1...) custom-call(s32[16,1]{1,0:T(8,128)} %copy-done.30, f32[32,4,16,2048]{3,2,1,0:T(8,128)} %get-tuple-element.211.refs_1_, ...), custom_call_target="tpu_custom_call" | custom-call | bytes 134217728 | tf_op jit(solution)/shard_map/forward_steps/pallas_call | solution.py:483
  326.0 38.0 %forward_steps.7 = (f32[8,4,16,2048]{3,2,1,0:T(8,128)}, f32[8,16,2048]{2,1,0:T(8,128)}, bf16[8,16,2048]{2,1,0:T(8,128)(2,1)}, bf16[8,16,2048]{2,1,0:T(8,128)(2,1...) custom-call(s32[16,1]{1,0:T(8,128)} %copy-done.30, f32[32,4,16,2048]{3,2,1,0:T(8,128)} %get-tuple-element.211.refs_1_, ...), custom_call_target="tpu_custom_call" | custom-call | bytes 134217728 | tf_op jit(solution)/shard_map/forward_steps/pallas_call | solution.py:483
  373.9 15.7 %decoder.1 = (bf16[4,2048,2048]{2,1,0:T(8,128)(2,1)S(1)}, bf16[512,2048]{1,0:T(8,128)(2,1)}, f32[8,128]{1,0:T(8,128)}, bf16[4,288,256]{2,1,0:T(8,128)(2,1)}, f32[4,288,256]{2,1,0:T(8,128)}) custom-call(s32[2]{0:T(128)} %copy-done.35, f32[1,384]{1,0:T(1,128)} %copy-done.40, s32[512,1]{1,0:T(8,128)} %reshape.328.refs_8_.refs_2_, ...), custom_call_target="tpu_custom_call", output_to_operand_aliasing={{0}: (14, {})} | custom-call | tf_op jit(solution)/shard_map/decoder/pallas_call | solution.py:734
  396.3 38.6 %backward_steps.5 = (bf16[8,16,2048]{2,1,0:T(8,128)(2,1)}, bf16[8,16,2048]{2,1,0:T(8,128)(2,1)}, bf16[8,16,2048]{2,1,0:T(8,128)(2,1)}, bf16[8,16,2048]{2,1,0:T(8...) custom-call(s32[2]{0:T(128)} %copy-done.35, s32[16,1]{1,0:T(8,128)} %copy-done.30, ...), custom_call_target="tpu_custom_call" | custom-call | bytes 134217728 | tf_op jit(solution)/shard_map/backward_steps/pallas_call | solution.py:571
  448.1 38.7 %backward_steps.6 = (bf16[8,16,2048]{2,1,0:T(8,128)(2,1)}, bf16[8,16,2048]{2,1,0:T(8,128)(2,1)}, bf16[8,16,2048]{2,1,0:T(8,128)(2,1)}, bf16[8,16,2048]{2,1,0:T(8...) custom-call(s32[2]{0:T(128)} %copy-done.35, s32[16,1]{1,0:T(8,128)} %copy-done.30, ...), custom_call_target="tpu_custom_call" | custom-call | bytes 134217728 | tf_op jit(solution)/shard_map/backward_steps/pallas_call | solution.py:571
  494.9 38.7 %backward_steps.7 = (bf16[8,16,2048]{2,1,0:T(8,128)(2,1)}, bf16[8,16,2048]{2,1,0:T(8,128)(2,1)}, bf16[8,16,2048]{2,1,0:T(8,128)(2,1)}, bf16[8,16,2048]{2,1,0:T(8...) custom-call(s32[2]{0:T(128)} %copy-done.35, s32[16,1]{1,0:T(8,128)} %copy-done.30, ...), custom_call_target="tpu_custom_call" | custom-call | bytes 134217728 | tf_op jit(solution)/shard_map/backward_steps/pallas_call | solution.py:571
  540.6 29.7 %backward_steps.8 = (bf16[6,16,2048]{2,1,0:T(8,128)(2,1)}, bf16[6,16,2048]{2,1,0:T(8,128)(2,1)}, bf16[6,16,2048]{2,1,0:T(8,128)(2,1)}, bf16[6,16,2048]{2,1,0:T(8...) custom-call(s32[2]{0:T(128)} %copy-done.35, s32[16,1]{1,0:T(8,128)} %copy-done.30, ...), custom_call_target="tpu_custom_call" | custom-call | bytes 100663296 | tf_op jit(solution)/shard_map/backward_steps/pallas_call | solution.py:571
  574.7 20.3 %weight_gradient.3 = (f32[128,2048]{1,0:T(8,128)}, f32[288,128]{1,0:T(8,128)}, f32[2048,2048]{1,0:T(8,128)}) custom-call(s32[2]{0:T(128)} %copy-done.35, bf16[128,2048]{1,0:T(8,128)(2,1)} %bitcast.144, bf16[128,2048]{1,0:T(8,128)(2,1)} %get-tuple-element.263.refs_1_.refs_6_.refs_2_.refs_19_, ...), custom_call_target="tpu_custom_call" | custom-call | bytes 1024 | tf_op jit(solution)/shard_map/weight_gradient/pallas_call | solution.py:1039
  596.0 11.4 %backward_steps.9 = (bf16[2,16,2048]{2,1,0:T(8,128)(2,1)}, bf16[2,16,2048]{2,1,0:T(8,128)(2,1)}, bf16[2,16,2048]{2,1,0:T(8,128)(2,1)}, bf16[2,16,2048]{2,1,0:T(8...) custom-call(s32[2]{0:T(128)} %copy-done.35, s32[16,1]{1,0:T(8,128)} %copy-done.30, ...), custom_call_target="tpu_custom_call" | custom-call | bytes 33554432 | tf_op jit(solution)/shard_map/backward_steps/pallas_call | solution.py:571
  607.4 7.9 %collective-permute-start.58 = (bf16[2,16,2048]{2,1,0:T(8,128)(2,1)}, bf16[2,16,2048]{2,1,0:T(8,128)(2,1)S(1)}, u32[]{:S(2)}, u32[]{:S(2)}) collective-permute-start(bf16[2,16,2048]{2,1,0:T(8,128)(2,1)} %get-tuple-element.315), channel_id=1, source_target_pairs={{0,1},{1,0},{2,3},{3,2},{4,5},{5,4},{6,7},{7,6},{8,9},{9,8},{10,11... | collective-permute-start | bytes 393224 | tf_op jit(solution)/shard_map/ppermute | solution.py:64
  619.6 8.5 %little_gradients.1 = (f32[128,2048]{1,0:T(8,128)}, f32[288,128]{1,0:T(8,128)}) custom-call(bf16[128,2048]{1,0:T(8,128)(2,1)} %bitcast.132, bf16[128,2048]{1,0:T(8,128)(2,1)} %bitcast.120, bf16[128,2048]{1,0:T(8,128)(2,1)} %bitcast.123, bf16[128,2048]{1,0:T(8,128)(2,1)} %bitcast.126, bf16[96,2048]{1,0:T(8,128)(2,1)} %bitcast.147, ...), custom_call_target="tpu_custom_call" | custom-call | bytes 1024 | tf_op jit(solution)/shard_map/little_gradients/pallas_call | solution.py:872
  631.8 11.2 %weight_gradient.4 = (f32[128,2048]{1,0:T(8,128)}, f32[288,128]{1,0:T(8,128)}, bf16[4,272,2048]{2,1,0:T(8,128)(2,1)S(1)}) custom-call(s32[2]{0:T(128)S(1)} %copy-done.38, bf16[128,2048]{1,0:T(8,128)(2,1)} %get-tuple-element.297.refs_1_.refs_8_, bf16[128,2048]{1,0:T(8,128)(2,1)} %get-tuple-element.298.refs_2_.refs_9_, ...), custom_call_target="tpu_custom_call" | custom-call | bytes 1024 | tf_op jit(solution)/shard_map/weight_gradient/pallas_call | solution.py:1039
  643.1 6.5 collective-permute-start.62
  652.1 11.0 %weight_gradient.5.refs_5_.refs_0_ = f32[4,272,2048]{2,1,0:T(8,128)S(1)} custom-call(s32[2]{0:T(128)S(1)} %copy-done.38, bf16[128,2048]{1,0:T(8,128)(2,1)} %get-tuple-element.297.refs_1_.refs_8_, bf16[128,2048]{1,0:T(8,128)(2,1)} %get-tuple-element.298.refs_2_.refs_9_, bf16[128,2048]{1,0:T(8,128)(2,1)} %get-tuple-element.299.refs_3_.refs_11_, ...), custom_call_target="tpu_custom_call" | custom-call | bytes 1024 | tf_op jit(solution)/shard_map/weight_gradient/pallas_call | solution.py:1039
  (453 shorter events, 221.0 us)
Async XLA Ops:
  270.6 50.7 %collective-permute-start.27 = (bf16[208,2048]{1,0:T(8,128)(2,1)}, bf16[208,2048]{1,0:T(8,128)(2,1)S(1)}, u32[]{:S(2)}, u32[]{:S(2)}) collective-permute-start(bf16[208,2048]{1,0:T(8,128)(2,1)} %get-tuple-element.229.refs_5_.refs_2_), channel_id=1, source_target_pairs={{1,2},{2,1},{5,6},{6,5},{9,10},{10,9},{13,14},{14,13},{17,18},{18,... | collective-permute-start | bytes 2555912 | tf_op jit(solution)/shard_map/ppermute | solution.py:1439
  271.3 50.0 %collective-permute-start.28 = (bf16[208,2048]{1,0:T(8,128)(2,1)}, bf16[208,2048]{1,0:T(8,128)(2,1)S(1)}, u32[]{:S(2)}, u32[]{:S(2)}) collective-permute-start(bf16[208,2048]{1,0:T(8,128)(2,1)} %get-tuple-element.230.refs_6_.refs_3_), channel_id=1, source_target_pairs={{1,0},{2,3},{5,4},{6,7},{9,8},{10,11},{13,12},{14,15},{17,16},{18,... | collective-permute-start | bytes 2555912 | tf_op jit(solution)/shard_map/ppermute | solution.py:1440
  272.6 47.9 %collective-permute-start.23 = (bf16[128,2048]{1,0:T(8,128)(2,1)S(1)}, bf16[128,2048]{1,0:T(8,128)(2,1)S(1)}, u32[]{:S(2)}, u32[]{:S(2)}) collective-permute-start(bf16[128,2048]{1,0:T(8,128)(2,1)S(1)} %bitcast.130), channel_id=1, source_target_pairs={{0,1},{1,0},{2,3},{3,2},{4,5},{5,4},{6,7},{7,6},{8,9},{9,8},{10,11... | collective-permute-start | bytes 1572872 | tf_op jit(solution)/shard_map/ppermute | solution.py:64
  318.0 45.9 %collective-permute-start.30 = (bf16[128,2048]{1,0:T(8,128)(2,1)}, bf16[128,2048]{1,0:T(8,128)(2,1)S(1)}, u32[]{:S(2)}, u32[]{:S(2)}) collective-permute-start(bf16[128,2048]{1,0:T(8,128)(2,1)} %bitcast.138), channel_id=1, source_target_pairs={{0,1},{1,0},{2,3},{3,2},{4,5},{5,4},{6,7},{7,6},{8,9},{9,8},{10,11... | collective-permute-start | bytes 1572872 | tf_op jit(solution)/shard_map/ppermute | solution.py:64
  320.5 48.1 %collective-permute-start.31 = (bf16[128,2048]{1,0:T(8,128)(2,1)}, bf16[128,2048]{1,0:T(8,128)(2,1)S(1)}, u32[]{:S(2)}, u32[]{:S(2)}) collective-permute-start(bf16[128,2048]{1,0:T(8,128)(2,1)} %bitcast.139), channel_id=1, source_target_pairs={{1,2},{2,1},{5,6},{6,5},{9,10},{10,9},{13,14},{14,13},{17,18},{18,... | collective-permute-start | bytes 1572872 | tf_op jit(solution)/shard_map/ppermute | solution.py:1437
  322.7 46.7 %collective-permute-start.32 = (bf16[128,2048]{1,0:T(8,128)(2,1)}, bf16[128,2048]{1,0:T(8,128)(2,1)S(1)}, u32[]{:S(2)}, u32[]{:S(2)}) collective-permute-start(bf16[128,2048]{1,0:T(8,128)(2,1)} %get-tuple-element.238.refs_5_.refs_2_), channel_id=1, source_target_pairs={{1,2},{2,1},{5,6},{6,5},{9,10},{10,9},{13,14},{14,13},{17,18},{18,... | collective-permute-start | bytes 1572872 | tf_op jit(solution)/shard_map/ppermute | solution.py:1439
  323.4 46.0 %collective-permute-start.33 = (bf16[128,2048]{1,0:T(8,128)(2,1)}, bf16[128,2048]{1,0:T(8,128)(2,1)S(1)}, u32[]{:S(2)}, u32[]{:S(2)}) collective-permute-start(bf16[128,2048]{1,0:T(8,128)(2,1)} %get-tuple-element.239.refs_6_.refs_3_), channel_id=1, source_target_pairs={{1,0},{2,3},{5,4},{6,7},{9,8},{10,11},{13,12},{14,15},{17,16},{18,... | collective-permute-start | bytes 1572872 | tf_op jit(solution)/shard_map/ppermute | solution.py:1440
  324.7 47.5 %collective-permute-start.29 = (bf16[208,2048]{1,0:T(8,128)(2,1)}, bf16[208,2048]{1,0:T(8,128)(2,1)S(1)}, u32[]{:S(2)}, u32[]{:S(2)}) collective-permute-start(bf16[208,2048]{1,0:T(8,128)(2,1)} %get-tuple-element.236.refs_7_.refs_11_.refs_3_), channel_id=1, source_target_pairs={{1,0},{2,3},{5,4},{6,7},{9,8},{10,11},{13,12},{14,15},{17,16},{18,... | collective-permute-start | bytes 2555912 | tf_op jit(solution)/shard_map/ppermute | solution.py:1442
  372.2 62.8 %collective-permute-start.34 = (bf16[128,2048]{1,0:T(8,128)(2,1)}, bf16[128,2048]{1,0:T(8,128)(2,1)S(1)}, u32[]{:S(2)}, u32[]{:S(2)}) collective-permute-start(bf16[128,2048]{1,0:T(8,128)(2,1)} %get-tuple-element.245.refs_8_.refs_9_), channel_id=1, source_target_pairs={{1,0},{2,3},{5,4},{6,7},{9,8},{10,11},{13,12},{14,15},{17,16},{18,... | collective-permute-start | bytes 1572872 | tf_op jit(solution)/shard_map/ppermute | solution.py:1442
  392.9 46.7 %collective-permute-start.40 = (bf16[128,2048]{1,0:T(8,128)(2,1)}, bf16[128,2048]{1,0:T(8,128)(2,1)S(1)}, u32[]{:S(2)}, u32[]{:S(2)}) collective-permute-start(bf16[128,2048]{1,0:T(8,128)(2,1)} %get-tuple-element.257.refs_0_), channel_id=1, source_target_pairs={{1,2},{2,1},{5,6},{6,5},{9,10},{10,9},{13,14},{14,13},{17,18},{18,... | collective-permute-start | bytes 1572872 | tf_op jit(solution)/shard_map/ppermute | solution.py:1439
  393.6 46.7 %collective-permute-start.41 = (bf16[128,2048]{1,0:T(8,128)(2,1)}, bf16[128,2048]{1,0:T(8,128)(2,1)S(1)}, u32[]{:S(2)}, u32[]{:S(2)}) collective-permute-start(bf16[128,2048]{1,0:T(8,128)(2,1)} %get-tuple-element.258.refs_1_), channel_id=1, source_target_pairs={{1,0},{2,3},{5,4},{6,7},{9,8},{10,11},{13,12},{14,15},{17,16},{18,... | collective-permute-start | bytes 1572872 | tf_op jit(solution)/shard_map/ppermute | solution.py:1440
  395.0 47.1 %collective-permute-start.46 = (bf16[4,288,256]{2,1,0:T(8,128)(2,1)S(1)}, bf16[4,288,256]{2,1,0:T(8,128)(2,1)S(1)}, u32[]{:S(2)}, u32[]{:S(2)}) collective-permute-start(bf16[4,288,256]{2,1,0:T(8,128)(2,1)S(1)} %copy-done.100), channel_id=1, source_target_pairs={{0,4},{4,0},{8,12},{12,8},{16,20},{20,16},{24,28},{28,24},{1,5},{5... | collective-permute-start | bytes 1769480 | tf_op jit(solution)/shard_map/ppermute | solution.py:54
  395.0 48.5 %collective-permute-start.39 = (bf16[128,2048]{1,0:T(8,128)(2,1)}, bf16[128,2048]{1,0:T(8,128)(2,1)S(1)}, u32[]{:S(2)}, u32[]{:S(2)}) collective-permute-start(bf16[128,2048]{1,0:T(8,128)(2,1)} %get-tuple-element.256.refs_3_.refs_8_.refs_9_.refs_15_), channel_id=1, source_target_pairs={{1,0},{2,3},{5,4},{6,7},{9,8},{10,11},{13,12},{14,15},{17,16},{18,... | collective-permute-start | bytes 1572872 | tf_op jit(solution)/shard_map/ppermute | solution.py:1442
  435.0 51.8 %collective-permute-start.43 = (bf16[8,16,2048]{2,1,0:T(8,128)(2,1)}, bf16[8,16,2048]{2,1,0:T(8,128)(2,1)S(1)}, u32[]{:S(2)}, u32[]{:S(2)}) collective-permute-start(bf16[8,16,2048]{2,1,0:T(8,128)(2,1)} %get-tuple-element.269), channel_id=1, source_target_pairs={{0,1},{1,0},{2,3},{3,2},{4,5},{5,4},{6,7},{7,6},{8,9},{9,8},{10,11... | collective-permute-start | bytes 1572872 | tf_op jit(solution)/shard_map/ppermute | solution.py:64
  439.6 49.9 %collective-permute-start.44 = (bf16[8,16,2048]{2,1,0:T(8,128)(2,1)}, bf16[8,16,2048]{2,1,0:T(8,128)(2,1)S(1)}, u32[]{:S(2)}, u32[]{:S(2)}) collective-permute-start(bf16[8,16,2048]{2,1,0:T(8,128)(2,1)} %get-tuple-element.270), channel_id=1, source_target_pairs={{0,2},{1,3},{2,0},{3,1},{4,6},{5,7},{6,4},{7,5},{8,10},{9,11},{10,... | collective-permute-start | bytes 1572872 | tf_op jit(solution)/shard_map/ppermute | solution.py:64
  440.4 49.9 %collective-permute-start.45 = (bf16[8,16,2048]{2,1,0:T(8,128)(2,1)}, bf16[8,16,2048]{2,1,0:T(8,128)(2,1)S(1)}, u32[]{:S(2)}, u32[]{:S(2)}) collective-permute-start(bf16[8,16,2048]{2,1,0:T(8,128)(2,1)} %get-tuple-element.271), channel_id=1, source_target_pairs={{0,3},{1,2},{2,1},{3,0},{4,7},{5,6},{6,5},{7,4},{8,11},{9,10},{10,... | collective-permute-start | bytes 1572872 | tf_op jit(solution)/shard_map/ppermute | solution.py:64
  442.1 49.9 %collective-permute-start.42 = (bf16[128,2048]{1,0:T(8,128)(2,1)}, bf16[128,2048]{1,0:T(8,128)(2,1)S(1)}, u32[]{:S(2)}, u32[]{:S(2)}) collective-permute-start(bf16[128,2048]{1,0:T(8,128)(2,1)} %get-tuple-element.265.refs_7_.refs_12_.refs_3_.refs_21_), channel_id=1, source_target_pairs={{1,0},{2,3},{5,4},{6,7},{9,8},{10,11},{13,12},{14,15},{17,16},{18,... | collective-permute-start | bytes 1572872 | tf_op jit(solution)/shard_map/ppermute | solution.py:1442
  486.8 49.2 %collective-permute-start.51 = (bf16[8,16,2048]{2,1,0:T(8,128)(2,1)}, bf16[8,16,2048]{2,1,0:T(8,128)(2,1)S(1)}, u32[]{:S(2)}, u32[]{:S(2)}) collective-permute-start(bf16[8,16,2048]{2,1,0:T(8,128)(2,1)} %get-tuple-element.286), channel_id=1, source_target_pairs={{0,1},{1,0},{2,3},{3,2},{4,5},{5,4},{6,7},{7,6},{8,9},{9,8},{10,11... | collective-permute-start | bytes 1572872 | tf_op jit(solution)/shard_map/ppermute | solution.py:64
  489.6 48.0 %collective-permute-start.52 = (bf16[8,16,2048]{2,1,0:T(8,128)(2,1)}, bf16[8,16,2048]{2,1,0:T(8,128)(2,1)S(1)}, u32[]{:S(2)}, u32[]{:S(2)}) collective-permute-start(bf16[8,16,2048]{2,1,0:T(8,128)(2,1)} %get-tuple-element.287), channel_id=1, source_target_pairs={{0,2},{1,3},{2,0},{3,1},{4,6},{5,7},{6,4},{7,5},{8,10},{9,11},{10,... | collective-permute-start | bytes 1572872 | tf_op jit(solution)/shard_map/ppermute | solution.py:64
  490.3 49.1 %collective-permute-start.53 = (bf16[8,16,2048]{2,1,0:T(8,128)(2,1)}, bf16[8,16,2048]{2,1,0:T(8,128)(2,1)S(1)}, u32[]{:S(2)}, u32[]{:S(2)}) collective-permute-start(bf16[8,16,2048]{2,1,0:T(8,128)(2,1)} %get-tuple-element.288), channel_id=1, source_target_pairs={{0,3},{1,2},{2,1},{3,0},{4,7},{5,6},{6,5},{7,4},{8,11},{9,10},{10,... | collective-permute-start | bytes 1572872 | tf_op jit(solution)/shard_map/ppermute | solution.py:64
  536.0 59.0 %collective-permute-start.49 = (bf16[8,16,2048]{2,1,0:T(8,128)(2,1)}, bf16[8,16,2048]{2,1,0:T(8,128)(2,1)S(1)}, u32[]{:S(2)}, u32[]{:S(2)}) collective-permute-start(bf16[8,16,2048]{2,1,0:T(8,128)(2,1)} %get-tuple-element.284), channel_id=1, source_target_pairs={{0,2},{1,3},{2,0},{3,1},{4,6},{5,7},{6,4},{7,5},{8,10},{9,11},{10,... | collective-permute-start | bytes 1572872 | tf_op jit(solution)/shard_map/ppermute | solution.py:64
  537.6 57.4 %collective-permute-start.50 = (bf16[8,16,2048]{2,1,0:T(8,128)(2,1)}, bf16[8,16,2048]{2,1,0:T(8,128)(2,1)S(1)}, u32[]{:S(2)}, u32[]{:S(2)}) collective-permute-start(bf16[8,16,2048]{2,1,0:T(8,128)(2,1)} %get-tuple-element.285), channel_id=1, source_target_pairs={{0,3},{1,2},{2,1},{3,0},{4,7},{5,6},{6,5},{7,4},{8,11},{9,10},{10,... | collective-permute-start | bytes 1572872 | tf_op jit(solution)/shard_map/ppermute | solution.py:64
  570.3 45.7 %collective-permute-start.55 = (bf16[6,16,2048]{2,1,0:T(8,128)(2,1)}, bf16[6,16,2048]{2,1,0:T(8,128)(2,1)S(1)}, u32[]{:S(2)}, u32[]{:S(2)}) collective-permute-start(bf16[6,16,2048]{2,1,0:T(8,128)(2,1)} %get-tuple-element.311), channel_id=1, source_target_pairs={{0,1},{1,0},{2,3},{3,2},{4,5},{5,4},{6,7},{7,6},{8,9},{9,8},{10,11... | collective-permute-start | bytes 1179656 | tf_op jit(solution)/shard_map/ppermute | solution.py:64
  571.3 47.3 %collective-permute-start.56 = (bf16[6,16,2048]{2,1,0:T(8,128)(2,1)}, bf16[6,16,2048]{2,1,0:T(8,128)(2,1)S(1)}, u32[]{:S(2)}, u32[]{:S(2)}) collective-permute-start(bf16[6,16,2048]{2,1,0:T(8,128)(2,1)} %get-tuple-element.312), channel_id=1, source_target_pairs={{0,2},{1,3},{2,0},{3,1},{4,6},{5,7},{6,4},{7,5},{8,10},{9,11},{10,... | collective-permute-start | bytes 1179656 | tf_op jit(solution)/shard_map/ppermute | solution.py:64
  (165 other events, 2040.0 us)
